TPU v7x, 32 devices: a whole 2x2x4 slice. The times are simulated.
32 devices in a mesh: group: 4 (over y, core), blk: 8 (over z, x).
Axes of the slice: x: 2, y: 2, z: 4, core: 2. Of those that a mesh axis runs over, the one named last changes fastest.
Arguments:
- points: bfloat16 [262144, 768], P(('group', 'blk')), may hold values from -128 to 128
- block_lists: int32 [2048, 4], P(('group', 'blk')), may hold values from 0 to 127, as said below
- centroids: bfloat16 [8192, 768], P('blk'), may hold values from -6 to 6
- dual_weights: bfloat16 [8192], P('blk'), may hold values from -1 to 1
Outputs:
- new_centroids: bfloat16 [8192, 768], P('blk')
- new_weights: bfloat16 [8192], P('blk')
Inputs may be any that keep to these rules, and one draw needn't show every extreme that they name: `block_lists`: cycle position q (index q along blk) owns blocks q * 16 to (q + 1) * 16 - 1. For a tile held by a device at cycle position p, slot 0 names a block of position p - 1, slot 2 a block of position p + 1, and slots 1 and 3 two different blocks of position p, positions taken modulo the number of devices along blk.
All inputs are finite; a program needn't handle non-finite values.
Results may differ from a plain program's by a relative error of at most 0.0052.
Values may be sent and summed in bfloat16 or wider, within the bound.
No kernel may reach another device: no remote copies, remote signals or barrier semaphores. Data moves between devices by JAX's collectives and lax.ppermute only.
A program may use at most 128 MiB of HBM per device.

v0:
```python
import math

import jax
import jax.numpy as jnp
from jax import lax
from jax.sharding import PartitionSpec as P

D = 768
BLOCK = 64
TILE = 128
SLOTS = 4
ITERS = 2


prior_mass = 1.0
dual_step = 0.5


def passed_along(block, axis, distance):
    devices = range(lax.axis_size(axis))
    route = [((i - distance) % len(devices), i) for i in devices]
    return lax.ppermute(block, axis, route)


def with_halo(cells, sides, width):
    for axis, dim in sides:
        count = lax.axis_size(axis)
        head = lax.slice_in_dim(cells, 0, width, axis=dim)
        tail = lax.slice_in_dim(cells, cells.shape[dim] - width, cells.shape[dim], axis=dim)
        cells = jnp.concatenate(
            [
                lax.ppermute(tail, axis, [(i, (i + 1) % count) for i in range(count)]),
                cells,
                lax.ppermute(head, axis, [((i + 1) % count, i) for i in range(count)]),
            ],
            axis=dim,
        )
    return cells


def renew_blocks(numerator, masses, centroids, weights, target):
    base = centroids.astype(jnp.float32)
    fresh = ((numerator + prior_mass * base) / (masses + prior_mass)[:, None]).astype(jnp.bfloat16)
    renewed = (weights.astype(jnp.float32) + dual_step * (1.0 - masses / target)).astype(
        jnp.bfloat16
    )
    return (fresh, renewed)


def return_cycle(near_num, near_mass):
    upper_num, upper_mass = passed_along((near_num[0], near_mass[0]), "blk", -1)
    lower_num, lower_mass = passed_along((near_num[2], near_mass[2]), "blk", 1)
    return (near_num[1] + upper_num + lower_num, near_mass[1] + upper_mass + lower_mass)


def assign_tiles(points, near_ids, near_centroids, offsets):
    tile_count = near_ids.shape[0]
    group_size = math.gcd(tile_count, 8)
    block_total = near_centroids.shape[0] // BLOCK
    width = points.shape[1]
    cand_flat = near_centroids.reshape(block_total, BLOCK * width)
    offset_blocks = offsets.reshape(block_total, BLOCK)
    tiled_points = points.reshape(tile_count // group_size, group_size, TILE, width)
    tiled_ids = near_ids.reshape(tile_count // group_size, group_size, SLOTS)
    block_iota = jnp.arange(block_total, dtype=jnp.int32)

    def tile_step(running, packet):
        sum_num, sum_mass = running
        tile_points, block_ids = packet
        picker = block_ids.reshape(-1)[:, None] == block_iota[None, :]
        candidates = jnp.dot(
            picker.astype(jnp.bfloat16), cand_flat, preferred_element_type=jnp.float32
        ).astype(jnp.bfloat16)
        candidates = candidates.reshape(group_size, SLOTS * BLOCK, width)
        picker_f = picker.astype(jnp.float32)
        cand_offsets = jnp.dot(
            picker_f,
            offset_blocks,
            precision=lax.Precision.HIGHEST,
            preferred_element_type=jnp.float32,
        )
        scores = jnp.einsum(
            "tpd,tkd->tpk", tile_points, candidates, preferred_element_type=jnp.float32
        ) * (32.0 / width)
        scores = scores + cand_offsets.reshape(group_size, 1, SLOTS * BLOCK)
        membership = jax.nn.softmax(scores, axis=-1).astype(jnp.bfloat16)
        masses = jnp.sum(membership.astype(jnp.float32), axis=1).reshape(group_size * SLOTS, BLOCK)
        numerator = jnp.einsum(
            "tpk,tpd->tkd", membership, tile_points, preferred_element_type=jnp.float32
        )
        numerator = numerator.reshape(group_size * SLOTS, BLOCK * width)
        add_num = jnp.dot(
            picker_f.T,
            numerator,
            precision=lax.Precision.HIGHEST,
            preferred_element_type=jnp.float32,
        )
        add_mass = jnp.dot(
            picker_f.T, masses, precision=lax.Precision.HIGHEST, preferred_element_type=jnp.float32
        )
        return ((sum_num + add_num, sum_mass + add_mass), None)

    start = (
        jnp.zeros((block_total, BLOCK * width), jnp.float32),
        jnp.zeros((block_total, BLOCK), jnp.float32),
    )
    (sum_num, sum_mass), _ = lax.scan(tile_step, start, (tiled_points, tiled_ids))
    return (sum_num.reshape(3, -1, width), sum_mass.reshape(3, -1))


def per_device(points, block_lists, centroids, dual_weights):
    own_rows = centroids.shape[0]
    own_blocks = own_rows // BLOCK
    cycle_size = lax.axis_size("blk")
    position = lax.axis_index("blk")
    groups = lax.axis_size("group")
    target = points.shape[0] * groups / own_rows
    owner = block_lists // own_blocks
    near_ids = (owner - position + 1) % cycle_size * own_blocks + block_lists % own_blocks
    weights = dual_weights
    for sweep in range(ITERS):
        near_centroids, near_weights = (
            with_halo(centroids, (("blk", 0),), own_rows),
            with_halo(weights, (("blk", 0),), own_rows),
        )
        squares = jnp.sum(jnp.square(near_centroids.astype(jnp.float32)), axis=1)
        offsets = near_weights.astype(jnp.float32) - squares * (16.0 / D)
        near_num, near_mass = assign_tiles(points, near_ids, near_centroids, offsets)
        own_num, own_mass = return_cycle(near_num, near_mass)
        total_num, total_mass = lax.psum((own_num, own_mass), "group")
        centroids, weights = renew_blocks(total_num, total_mass, centroids, weights, target)
    return (centroids, weights)


def solution(mesh):
    return jax.shard_map(
        per_device,
        mesh=mesh,
        in_specs=(P(("group", "blk"), None), P(("group", "blk"), None), P("blk", None), P("blk")),
        out_specs=(P("blk", None), P("blk")),
        check_vma=False,
    )
```

profile of v0, /device:TPU:0, one launch (start us, length us, event | category | flops | bytes accessed | tf_op | source)
XLA Modules:
  0.0 1156.2 jit_solution(4328213704491727257)
XLA Ops:
  19.6 58.4 %collective-permute-done.2 = bf16[1024]{0:T(1024)(128)(2,1)S(1)} collective-permute-done((bf16[1024]{0:T(1024)(128)(2,1)}, bf16[1024]{0:T(1024)(128)(2,1)S(1)}, u32[]{:S(2)}, u32[]{:S(2)}) %collective-permute-start.2) | collective-permute-done | bytes 2080 | tf_op jit(solution)/shard_map/ppermute | solution.py:32
  85.4 6.9 reshape.98
  95.7 258.4 %while.26 = (s32[]{:T(128)}, f32[48,49152]{1,0:T(8,128)}, f32[48,64]{1,0:T(8,128)S(1)}, s32[8,8,4]{2,1,0:T(8,128)S(1)}, bf16[8,8,128,768]{3,2,1,0:T(8,128)(2,1)}...) while((s32[]{:T(128)}, f32[48,49152]{1,0:T(8,128)}, ...), condition=%wide.region_5.6_spmd.clone, body=%wide.region_1.5_spmd.clone.sunk | while | flops 1873029376 | bytes 67745896 | solution.py:107
  111.3 6.2 reshape.113
  117.5 8.9 convolution_add_fusion.8
  142.3 6.2 reshape.113
  148.5 10.3 convolution_add_fusion.8
  174.8 6.2 reshape.113
  181.0 10.3 convolution_add_fusion.8
  207.3 6.2 reshape.113
  213.5 10.3 convolution_add_fusion.8
  239.8 6.2 reshape.113
  246.0 10.3 convolution_add_fusion.8
  272.3 6.2 reshape.113
  278.5 10.3 convolution_add_fusion.8
  304.7 6.2 reshape.113
  310.9 10.3 convolution_add_fusion.8
  337.2 6.2 reshape.113
  343.4 10.3 convolution_add_fusion.8
  354.1 6.9 fusion.57
  373.0 127.7 %collective-permute-done.4 = f32[1024,768]{1,0:T(8,128)} collective-permute-done((f32[1024,768]{1,0:T(8,128)}, f32[1024,768]{1,0:T(8,128)}, u32[]{:S(2)}, u32[]{:S(2)}) %collective-permute-start.4) | collective-permute-done | bytes 3145760 | tf_op jit(solution)/shard_map/ppermute | solution.py:22
  506.9 6.5 collective-permute-start.6
  519.8 6.2 psum.29
  525.9 52.8 %all-reduce.3.cloned.1.call-done = f32[1024,768]{1,0:T(8,128)} async-done(((f32[1024,768]{1,0:T(8,128)}), f32[1024,768]{1,0:T(8,128)}) %all-reduce.3.cloned.1.call-update) | async-done | bytes 3145744 | tf_op jit(solution)/shard_map/psum | solution.py:130
  590.6 59.3 %collective-permute-done.10 = bf16[1024]{0:T(1024)(128)(2,1)S(1)} collective-permute-done((bf16[1024]{0:T(1024)(128)(2,1)S(1)}, bf16[1024]{0:T(1024)(128)(2,1)S(1)}, u32[]{:S(2)}, u32[]{:S(2)}) %collective-permute-start.10) | collective-permute-done | bytes 2080 | tf_op jit(solution)/shard_map/ppermute | solution.py:32
  656.9 6.9 reshape.99
  663.8 258.4 %while.27 = (s32[]{:T(128)}, f32[48,49152]{1,0:T(8,128)}, f32[48,64]{1,0:T(8,128)S(1)}, s32[8,8,4]{2,1,0:T(8,128)S(1)}, bf16[8,8,128,768]{3,2,1,0:T(8,128)(2,1)}...) while((s32[]{:T(128)}, f32[48,49152]{1,0:T(8,128)}, ...), condition=%wide.region_13.14_spmd.clone, body=%wide.region_9.13_spmd.clone.sunk | while | flops 1873029376 | bytes 67745896 | solution.py:107
  679.4 6.2 reshape.116
  685.6 8.9 convolution_add_fusion.10
  710.5 6.2 reshape.116
  716.7 10.3 convolution_add_fusion.10
  743.0 6.2 reshape.116
  749.2 10.3 convolution_add_fusion.10
  775.5 6.2 reshape.116
  781.7 10.3 convolution_add_fusion.10
  808.0 6.2 reshape.116
  814.2 10.3 convolution_add_fusion.10
  840.4 6.2 reshape.116
  846.6 10.3 convolution_add_fusion.10
  872.9 6.2 reshape.116
  879.1 10.3 convolution_add_fusion.10
  905.4 6.2 reshape.116
  911.6 10.3 convolution_add_fusion.10
  922.2 6.9 fusion.56
  940.7 128.1 %collective-permute-done.12 = f32[1024,768]{1,0:T(8,128)} collective-permute-done((f32[1024,768]{1,0:T(8,128)}, f32[1024,768]{1,0:T(8,128)}, u32[]{:S(2)}, u32[]{:S(2)}) %collective-permute-start.12) | collective-permute-done | bytes 3145760 | tf_op jit(solution)/shard_map/ppermute | solution.py:22
  1074.9 6.1 collective-permute-start.14
  1087.4 6.2 psum.31
  1094.1 51.8 %all-reduce.5.cloned.1.call-done = f32[1024,768]{1,0:T(8,128)} async-done(((f32[1024,768]{1,0:T(8,128)}), f32[1024,768]{1,0:T(8,128)}) %all-reduce.5.cloned.1.call-update) | async-done | bytes 3145744 | tf_op jit(solution)/shard_map/psum | solution.py:130
  (261 shorter events, 349.8 us)
Async XLA Ops:
  7.2 75.7 %copy-start.2 = (bf16[1024,768]{1,0:T(8,128)(2,1)S(1)}, bf16[1024,768]{1,0:T(8,128)(2,1)}, u32[]{:S(2)}) copy-start(bf16[1024,768]{1,0:T(8,128)(2,1)} %param.10) | copy-start | bytes 4718596
  7.2 571.5 %all-reduce.3.cloned.1.call-start = ((), (), s32[]{:S(2)}) async-start(), calls=%async_computation | async-start | bytes 6291456 | tf_op jit(solution)/shard_map/psum | solution.py:130
  7.2 72.9 %collective-permute-start = (bf16[1024,768]{1,0:T(8,128)(2,1)}, bf16[1024,768]{1,0:T(8,128)(2,1)}, u32[]{:S(2)}, u32[]{:S(2)}) collective-permute-start(bf16[1024,768]{1,0:T(8,128)(2,1)} %param.10), channel_id=1, source_target_pairs={{0,1},{1,2},{2,3},{3,4},{4,5},{5,6},{6,7},{7,0},{8,9},{9,10},{10,1... | collective-permute-start | bytes 4718600 | tf_op jit(solution)/shard_map/ppermute | solution.py:32
  10.2 73.9 %collective-permute-start.1 = (bf16[1024,768]{1,0:T(8,128)(2,1)}, bf16[1024,768]{1,0:T(8,128)(2,1)S(1)}, u32[]{:S(2)}, u32[]{:S(2)}) collective-permute-start(bf16[1024,768]{1,0:T(8,128)(2,1)} %param.10), channel_id=1, source_target_pairs={{1,0},{2,1},{3,2},{4,3},{5,4},{6,5},{7,6},{0,7},{9,8},{10,9},{11,1... | collective-permute-start | bytes 4718600 | tf_op jit(solution)/shard_map/ppermute | solution.py:34
  13.3 64.6 %collective-permute-start.2 = (bf16[1024]{0:T(1024)(128)(2,1)}, bf16[1024]{0:T(1024)(128)(2,1)S(1)}, u32[]{:S(2)}, u32[]{:S(2)}) collective-permute-start(bf16[1024]{0:T(1024)(128)(2,1)} %param.11), channel_id=1, source_target_pairs={{0,1},{1,2},{2,3},{3,4},{4,5},{5,6},{6,7},{7,0},{8,9},{9,10},{10,1... | collective-permute-start | bytes 6152 | tf_op jit(solution)/shard_map/ppermute | solution.py:32
  13.3 66.7 %collective-permute-start.3 = (bf16[1024]{0:T(1024)(128)(2,1)}, bf16[1024]{0:T(1024)(128)(2,1)S(1)}, u32[]{:S(2)}, u32[]{:S(2)}) collective-permute-start(bf16[1024]{0:T(1024)(128)(2,1)} %param.11), channel_id=1, source_target_pairs={{1,0},{2,1},{3,2},{4,3},{5,4},{6,5},{7,6},{0,7},{9,8},{10,9},{11,1... | collective-permute-start | bytes 6152 | tf_op jit(solution)/shard_map/ppermute | solution.py:34
  364.3 136.4 %collective-permute-start.4 = (f32[1024,768]{1,0:T(8,128)}, f32[1024,768]{1,0:T(8,128)}, u32[]{:S(2)}, u32[]{:S(2)}) collective-permute-start(f32[1024,768]{1,0:T(8,128)} %squeeze.47), channel_id=1, source_target_pairs={{1,0},{2,1},{3,2},{4,3},{5,4},{6,5},{7,6},{0,7},{9,8},{10,9},{11,1... | collective-permute-start | bytes 9437192 | tf_op jit(solution)/shard_map/ppermute | solution.py:22
  371.1 129.6 %collective-permute-start.5 = (f32[1024,768]{1,0:T(8,128)}, f32[1024,768]{1,0:T(8,128)}, u32[]{:S(2)}, u32[]{:S(2)}) collective-permute-start(f32[1024,768]{1,0:T(8,128)} %squeeze.48), channel_id=1, source_target_pairs={{7,0},{0,1},{1,2},{2,3},{3,4},{4,5},{5,6},{6,7},{15,8},{8,9},{9,10... | collective-permute-start | bytes 9437192 | tf_op jit(solution)/shard_map/ppermute | solution.py:22
  506.7 19.2 %copy-start.4 = (bf16[1024]{0:T(1024)(128)(2,1)S(1)}, bf16[1024]{0:T(1024)(128)(2,1)}, u32[]{:S(2)}) copy-start(bf16[1024]{0:T(1024)(128)(2,1)} %param.11) | copy-start | bytes 6148
  506.7 72.0 %copy-start.3 = (bf16[1024,768]{1,0:T(8,128)(2,1)S(1)}, bf16[1024,768]{1,0:T(8,128)(2,1)}, u32[]{:S(2)}) copy-start(bf16[1024,768]{1,0:T(8,128)(2,1)} %param.10) | copy-start | bytes 4718596
  506.7 639.2 %all-reduce.5.cloned.1.call-start = ((), (), s32[]{:S(2)}) async-start(), calls=%async_computation.1 | async-start | bytes 6291456 | tf_op jit(solution)/shard_map/psum | solution.py:130
  506.9 7.8 collective-permute-start.6
  513.4 6.3 collective-permute-start.7
  581.0 75.8 %copy-start = (bf16[1024,768]{1,0:T(8,128)(2,1)}, bf16[1024,768]{1,0:T(8,128)(2,1)S(1)}, u32[]{:S(2)}) copy-start(bf16[1024,768]{1,0:T(8,128)(2,1)S(1)} %divide_convert_fusion.3) | copy-start | bytes 4718596
  581.0 71.2 %collective-permute-start.8 = (bf16[1024,768]{1,0:T(8,128)(2,1)S(1)}, bf16[1024,768]{1,0:T(8,128)(2,1)S(1)}, u32[]{:S(2)}, u32[]{:S(2)}) collective-permute-start(bf16[1024,768]{1,0:T(8,128)(2,1)S(1)} %divide_convert_fusion.3), channel_id=1, source_target_pairs={{0,1},{1,2},{2,3},{3,4},{4,5},{5,6},{6,7},{7,0},{8,9},{9,10},{10,1... | collective-permute-start | bytes 4718600 | tf_op jit(solution)/shard_map/ppermute | solution.py:32
  582.5 69.7 %collective-permute-start.9 = (bf16[1024,768]{1,0:T(8,128)(2,1)S(1)}, bf16[1024,768]{1,0:T(8,128)(2,1)}, u32[]{:S(2)}, u32[]{:S(2)}) collective-permute-start(bf16[1024,768]{1,0:T(8,128)(2,1)S(1)} %divide_convert_fusion.3), channel_id=1, source_target_pairs={{1,0},{2,1},{3,2},{4,3},{5,4},{6,5},{7,6},{0,7},{9,8},{10,9},{11,1... | collective-permute-start | bytes 4718600 | tf_op jit(solution)/shard_map/ppermute | solution.py:34
  585.8 64.1 %collective-permute-start.10 = (bf16[1024]{0:T(1024)(128)(2,1)S(1)}, bf16[1024]{0:T(1024)(128)(2,1)S(1)}, u32[]{:S(2)}, u32[]{:S(2)}) collective-permute-start(bf16[1024]{0:T(1024)(128)(2,1)S(1)} %get-tuple-element.196), channel_id=1, source_target_pairs={{0,1},{1,2},{2,3},{3,4},{4,5},{5,6},{6,7},{7,0},{8,9},{9,10},{10,1... | collective-permute-start | bytes 6152 | tf_op jit(solution)/shard_map/ppermute | solution.py:32
  585.8 66.4 %collective-permute-start.11 = (bf16[1024]{0:T(1024)(128)(2,1)S(1)}, bf16[1024]{0:T(1024)(128)(2,1)S(1)}, u32[]{:S(2)}, u32[]{:S(2)}) collective-permute-start(bf16[1024]{0:T(1024)(128)(2,1)S(1)} %get-tuple-element.196), channel_id=1, source_target_pairs={{1,0},{2,1},{3,2},{4,3},{5,4},{6,5},{7,6},{0,7},{9,8},{10,9},{11,1... | collective-permute-start | bytes 6152 | tf_op jit(solution)/shard_map/ppermute | solution.py:34
  932.5 136.3 %collective-permute-start.12 = (f32[1024,768]{1,0:T(8,128)}, f32[1024,768]{1,0:T(8,128)}, u32[]{:S(2)}, u32[]{:S(2)}) collective-permute-start(f32[1024,768]{1,0:T(8,128)} %squeeze.53), channel_id=1, source_target_pairs={{1,0},{2,1},{3,2},{4,3},{5,4},{6,5},{7,6},{0,7},{9,8},{10,9},{11,1... | collective-permute-start | bytes 9437192 | tf_op jit(solution)/shard_map/ppermute | solution.py:22
  938.8 130.0 %collective-permute-start.13 = (f32[1024,768]{1,0:T(8,128)}, f32[1024,768]{1,0:T(8,128)}, u32[]{:S(2)}, u32[]{:S(2)}) collective-permute-start(f32[1024,768]{1,0:T(8,128)} %squeeze.54), channel_id=1, source_target_pairs={{7,0},{0,1},{1,2},{2,3},{3,4},{4,5},{5,6},{6,7},{15,8},{8,9},{9,10... | collective-permute-start | bytes 9437192 | tf_op jit(solution)/shard_map/ppermute | solution.py:22
  1074.8 71.1 %copy-start.1 = (bf16[1024,768]{1,0:T(8,128)(2,1)S(1)}, bf16[1024,768]{1,0:T(8,128)(2,1)}, u32[]{:S(2)}) copy-start(bf16[1024,768]{1,0:T(8,128)(2,1)} %copy-done) | copy-start | bytes 4718596
  1074.9 7.4 collective-permute-start.14
  1081.0 6.3 collective-permute-start.15
Sparse Core Ops, SparseCore 0:
  506.9 71.8 all-reduce.2
  1074.9 70.9 all-reduce.4
where the time goes:
time: 1160 us
  waiting for transfers between devices  495 us (43%)
  matrix products  363 us (31%)
  local copies, waits for them, and re-layouts  201 us (17%)
  starting transfers between devices  39.5 us (3%)
  other arithmetic  30.6 us (3%)
  between operations  14.1 us (1%)
  blocking collectives  12.3 us (1%)
    ppermute x8, waiting for transfers between devices, passed_along(): return lax.ppermute(block, axis, route)  268 us
    dot_general x16, matrix products, tile_step(): jnp.dot(picker_f.T, numerator, precision=lax.Precision.HIGHEST, preferred...  162 us
    ppermute x4, waiting for transfers between devices, with_halo(): lax.ppermute(tail, axis, [(i, (i + 1) % count) for i in range(count)])  118 us
    psum x2, waiting for transfers between devices, per_device(): total_num, total_mass = lax.psum((own_num, own_mass), 'group')  105 us
    reshape x16, local copies, waits for them, and re-layouts, tile_step(): numerator = numerator.reshape(group_size * SLOTS, BLOCK * width)  99.3 us
    dot_general x16, matrix products, tile_step(): jnp.einsum('tpk,tpd->tkd', membership, tile_points, preferred_element_typ...  80.8 us
    sub x16, matrix products, tile_step(): membership = jax.nn.softmax(scores, axis=-1).astype(jnp.bfloat16)  59.2 us
    dot_general x16, matrix products, tile_step(): jnp.dot(picker.astype(jnp.bfloat16), cand_flat, preferred_element_type=jn...  53.8 us
  transfers between devices with their start and end apart: 18, of which 12 were waited for; matrix products, arithmetic and copies ran while one was open for 1% of the time, Pallas kernels for 0%

commit v1 on v0

v1 whole, which is shorter than its diff:
```python
import functools

import jax
import jax.numpy as jnp
from jax import lax
from jax.experimental import pallas as pl
from jax.experimental.pallas import tpu as pltpu
from jax.sharding import PartitionSpec as P

BLOCK = 64
TILE = 128
SLOTS = 4
ITERS = 2
TAIL = 16
STEP_TILES = 4
prior_mass = 1.0
dual_step = 0.5
F32 = jnp.float32
BF16 = jnp.bfloat16
VMEM_LIMIT = 56 * 1024 * 1024


def swap(x, bit):
    groups = lax.axis_size("group")
    return lax.ppermute(x, "group", [(i, i ^ bit) for i in range(groups)])


def core_swap(x):
    return swap(x, 1)


def plane_swap(x):
    return swap(x, 2)


def along(x, distance):
    count = lax.axis_size("blk")
    return lax.ppermute(x, "blk", [((i - distance) % count, i) for i in range(count)])


def eye():
    shape = (TILE, TILE)
    return lax.broadcasted_iota(jnp.int32, shape, 0) == lax.broadcasted_iota(jnp.int32, shape, 1)


def to_column(row):
    return jnp.sum(jnp.where(eye(), row, 0.0), axis=1, keepdims=True)


def to_row(column):
    return jnp.sum(jnp.where(eye(), column, 0.0), axis=0, keepdims=True)


def split_masses(row):
    high = row.astype(BF16)
    rest = row - high.astype(F32)
    mid = rest.astype(BF16)
    low = (rest - mid.astype(F32)).astype(BF16)
    return jnp.concatenate([high, mid, low], axis=1)


def tail_of(row):
    wide = jnp.broadcast_to(row.astype(F32), (TAIL, row.shape[1]))
    first = lax.broadcasted_iota(jnp.int32, wide.shape, 0) == 0
    return jnp.where(first, wide, 0.0)


def mass_of(tail, quarter):
    row = tail[0:1, :].astype(F32)
    return row[:, :quarter] + row[:, quarter : 2 * quarter] + row[:, 2 * quarter : 3 * quarter]


def tiles_kernel(rows, ids_ref, me_ref, points_ref, *refs):
    quarter = rows // 4
    packet = quarter + TAIL
    half = rows // 2
    packets = refs[:12]
    sends = refs[12:15]
    keeps = refs[15:18]
    near, tails, offs, acc, macc, stage, ktail, in_sem, out_sem = refs[18:]
    step = pl.program_id(0)
    core = me_ref[0]
    plane = me_ref[1]

    def place(side, j):
        c = core if j < 2 else 1 - core
        y = plane if j % 2 == 0 else 1 - plane
        return side * 4 + c * 2 + y

    def arrivals():
        out = []
        for side in range(3):
            for j in range(4):
                n = side * 4 + j
                at = place(side, j)
                out.append(
                    pltpu.make_async_copy(
                        packets[n].at[pl.ds(0, quarter)],
                        near.at[pl.ds(pl.multiple_of(at * quarter, quarter), quarter)],
                        in_sem.at[2 * n],
                    )
                )
                out.append(
                    pltpu.make_async_copy(
                        packets[n].at[pl.ds(quarter, TAIL)],
                        tails.at[pl.ds(pl.multiple_of(at * TAIL, TAIL), TAIL)],
                        in_sem.at[2 * n + 1],
                    )
                )
        return out

    @pl.when(step == 0)
    def _():
        copies = arrivals()
        for copy in copies:
            copy.start()

        @pl.loop(0, 3 * rows // BLOCK)
        def _(b):
            at = pl.ds(pl.multiple_of(b * BLOCK, BLOCK), BLOCK)
            acc[at, :] = jnp.zeros((BLOCK, acc.shape[1]), F32)
            macc[at, :] = jnp.zeros((BLOCK, TILE), F32)

        for copy in copies:
            copy.wait()

        width = near.shape[1]

        @pl.loop(0, 12)
        def _(n):
            tail = tails[pl.ds(pl.multiple_of(n * TAIL, TAIL), TAIL), :].astype(F32)
            for k in range(quarter // TILE):
                at = pl.ds(pl.multiple_of(n * quarter + k * TILE, TILE), TILE)
                base = near[at, :].astype(F32)
                squares = jnp.sum(base * base, axis=1, keepdims=True)
                weights = to_column(tail[0:1, k * TILE : (k + 1) * TILE])
                offs[at, :] = jnp.broadcast_to(weights - squares * (16.0 / width), (TILE, TILE))

    width = near.shape[1]
    for t in range(STEP_TILES):
        points = points_ref[pl.ds(t * TILE, TILE), :]
        tile = step * STEP_TILES + t
        at = [
            pl.ds(pl.multiple_of(ids_ref[tile * SLOTS + k] * BLOCK, BLOCK), BLOCK)
            for k in range(SLOTS)
        ]
        cand = jnp.concatenate([near[a, :] for a in at], axis=0)
        off = jnp.concatenate([offs[a, :] for a in at], axis=0)
        scores = lax.dot_general(
            cand, points, (((1,), (1,)), ((), ())), preferred_element_type=F32
        )
        scores = scores * (32.0 / width) + off
        top = jnp.max(scores, axis=0, keepdims=True)
        raw = jnp.exp(scores - top)
        total = jnp.sum(raw, axis=0, keepdims=True)
        member = (raw * (1.0 / total)).astype(BF16)
        numerator = jnp.dot(member, points, preferred_element_type=F32)
        masses = member.astype(F32)
        for k in range(SLOTS):
            acc[at[k], :] += numerator[k * BLOCK : (k + 1) * BLOCK]
            macc[at[k], :] += masses[k * BLOCK : (k + 1) * BLOCK]

    @pl.when(step == pl.num_programs(0) - 1)
    def _():
        copies = []
        for side in (0, 2, 1):
            for y in range(2):
                n = side * 2 + y
                mine = pl.multiple_of(side * rows + core * half + y * quarter, quarter)
                other = pl.multiple_of(side * rows + (1 - core) * half + y * quarter, quarter)

                def masses_at(start):
                    return jnp.concatenate(
                        [
                            to_row(
                                jnp.sum(
                                    macc[pl.ds(start + k * TILE, TILE), :], axis=1, keepdims=True
                                )
                            )
                            for k in range(quarter // TILE)
                        ],
                        axis=1,
                    )

                stage[side, pl.ds(y * packet, quarter), :] = acc[pl.ds(other, quarter), :].astype(
                    BF16
                )
                stage[side, pl.ds(y * packet + quarter, TAIL), :] = tail_of(
                    split_masses(masses_at(other))
                ).astype(BF16)
                row = masses_at(mine)
                ktail[n] = tail_of(jnp.concatenate([row, row * 0.0, row * 0.0], axis=1))
                copies.append(
                    pltpu.make_async_copy(
                        acc.at[pl.ds(mine, quarter)],
                        keeps[side].at[pl.ds(y * packet, quarter)],
                        out_sem.at[n],
                    )
                )
                copies[-1].start()
                copies.append(
                    pltpu.make_async_copy(
                        ktail.at[n],
                        keeps[side].at[pl.ds(y * packet + quarter, TAIL)],
                        out_sem.at[6 + n],
                    )
                )
                copies[-1].start()
            copies.append(
                pltpu.make_async_copy(stage.at[side], sends[side], out_sem.at[12 + side])
            )
            copies[-1].start()
        for copy in copies:
            copy.wait()


def assign_tiles(points, ids, me, packets, rows):
    count, width = points.shape
    quarter = rows // 4
    packet = quarter + TAIL
    tiles = count // TILE
    any_spec = pl.BlockSpec(memory_space=pl.ANY)
    step_rows = STEP_TILES * TILE
    outs = pl.pallas_call(
        functools.partial(tiles_kernel, rows),
        grid_spec=pltpu.PrefetchScalarGridSpec(
            num_scalar_prefetch=2,
            grid=(tiles // STEP_TILES,),
            in_specs=[pl.BlockSpec((step_rows, width), lambda i, ids, me: (i, 0))]
            + [any_spec] * 12,
            out_specs=[any_spec] * 6,
            scratch_shapes=[
                pltpu.VMEM((3 * rows, width), BF16),
                pltpu.VMEM((12 * TAIL, width), BF16),
                pltpu.VMEM((3 * rows, TILE), F32),
                pltpu.VMEM((3 * rows, width), F32),
                pltpu.VMEM((3 * rows, TILE), F32),
                pltpu.VMEM((3, 2 * packet, width), BF16),
                pltpu.VMEM((6, TAIL, width), F32),
                pltpu.SemaphoreType.DMA((24,)),
                pltpu.SemaphoreType.DMA((15,)),
            ],
        ),
        out_shape=[jax.ShapeDtypeStruct((2 * packet, width), BF16)] * 3
        + [jax.ShapeDtypeStruct((2 * packet, width), F32)] * 3,
        compiler_params=pltpu.CompilerParams(vmem_limit_bytes=VMEM_LIMIT),
        cost_estimate=pl.CostEstimate(
            flops=4 * count * SLOTS * BLOCK * width,
            bytes_accessed=2 * count * width,
            transcendentals=count * SLOTS * BLOCK,
        ),
        name="tiles",
    )(ids, me, points, *packets)
    return outs[:3], outs[3:]


def sum_kernel(quarter, me_ref, *refs):
    out = refs[-1]
    terms = refs[:-1]
    total = terms[0][pl.ds(0, quarter), :].astype(F32)
    for term in terms[1:]:
        total = total + term[pl.ds(0, quarter), :].astype(F32)
    out[pl.ds(0, quarter), :] = total.astype(BF16)
    mass = mass_of(terms[0][pl.ds(quarter, TAIL), :], quarter)
    for term in terms[1:]:
        mass = mass + mass_of(term[pl.ds(quarter, TAIL), :], quarter)
    out[pl.ds(quarter, TAIL), :] = tail_of(split_masses(mass)).astype(BF16)


def part_spec(packet, width, other):
    if other is None:
        return pl.BlockSpec((packet, width), lambda i, me: (0, 0))
    if other:
        return pl.BlockSpec((packet, width), lambda i, me: (1 - me[1], 0))
    return pl.BlockSpec((packet, width), lambda i, me: (me[1], 0))


def add_packets(me, pairs, singles, other):
    width = pairs[0].shape[1]
    packet = pairs[0].shape[0] // 2
    terms = list(pairs) + list(singles)
    return pl.pallas_call(
        functools.partial(sum_kernel, packet - TAIL),
        grid_spec=pltpu.PrefetchScalarGridSpec(
            num_scalar_prefetch=1,
            grid=(1,),
            in_specs=[part_spec(packet, width, other)] * len(pairs)
            + [part_spec(packet, width, None)] * len(singles),
            out_specs=part_spec(packet, width, None),
        ),
        out_shape=jax.ShapeDtypeStruct((packet, width), BF16),
        compiler_params=pltpu.CompilerParams(vmem_limit_bytes=VMEM_LIMIT),
        cost_estimate=pl.CostEstimate(
            flops=packet * width * len(terms),
            bytes_accessed=sum(t.size * t.dtype.itemsize for t in terms),
            transcendentals=0,
        ),
        name="add_packets",
    )(me, *terms)


def renew_kernel(quarter, target, me_ref, base_ref, *refs):
    out = refs[-1]
    terms = refs[:-1]
    mass = mass_of(terms[0][pl.ds(quarter, TAIL), :], quarter)
    for term in terms[1:]:
        mass = mass + mass_of(term[pl.ds(quarter, TAIL), :], quarter)
    weights = base_ref[pl.ds(quarter, TAIL), :].astype(F32)[0:1, :quarter]
    renewed = weights + dual_step * (1.0 - mass / target)
    zero = renewed * 0.0
    out[pl.ds(quarter, TAIL), :] = tail_of(
        jnp.concatenate([renewed, zero, zero], axis=1)
    ).astype(BF16)
    for k in range(quarter // TILE):
        at = pl.ds(k * TILE, TILE)
        total = terms[0][at, :].astype(F32)
        for term in terms[1:]:
            total = total + term[at, :].astype(F32)
        base = base_ref[at, :].astype(F32)
        column = to_column(mass[:, k * TILE : (k + 1) * TILE]) + prior_mass
        out[at, :] = ((total + prior_mass * base) / column).astype(BF16)


def renew(me, base, pairs, singles, target):
    width = pairs[0].shape[1]
    packet = pairs[0].shape[0] // 2
    terms = list(pairs) + list(singles)
    return pl.pallas_call(
        functools.partial(renew_kernel, packet - TAIL, target),
        grid_spec=pltpu.PrefetchScalarGridSpec(
            num_scalar_prefetch=1,
            grid=(1,),
            in_specs=[part_spec(packet, width, None)]
            + [part_spec(packet, width, False)] * len(pairs)
            + [part_spec(packet, width, None)] * len(singles),
            out_specs=part_spec(packet, width, None),
        ),
        out_shape=jax.ShapeDtypeStruct((packet, width), BF16),
        compiler_params=pltpu.CompilerParams(vmem_limit_bytes=VMEM_LIMIT),
        name="renew",
    )(me, base, *terms)


def per_device(points, block_lists, centroids, dual_weights):
    rows, width = centroids.shape
    quarter = rows // 4
    own_blocks = rows // BLOCK
    cycle_size = lax.axis_size("blk")
    position = lax.axis_index("blk")
    groups = lax.axis_size("group")
    member = lax.axis_index("group")
    core, plane = member % 2, member // 2
    me = jnp.stack([core, plane]).astype(jnp.int32)
    target = points.shape[0] * groups / rows
    owner = block_lists // own_blocks
    near_ids = (owner - position + 1) % cycle_size * own_blocks + block_lists % own_blocks
    near_ids = near_ids.reshape(-1).astype(jnp.int32)

    def start_packet(c, y):
        first = (c * 2 + y) * quarter
        block = lax.dynamic_slice_in_dim(centroids, first, quarter, 0)
        row = lax.dynamic_slice_in_dim(dual_weights, first, quarter, 0)
        tail = jnp.pad(row[None, :], ((0, TAIL - 1), (0, width - quarter)))
        return jnp.concatenate([block, tail], axis=0)

    def spread(packet):
        beside = plane_swap(packet)
        return [packet, beside, core_swap(packet), core_swap(beside)]

    mine = start_packet(core, plane)
    own = None
    for sweep in range(ITERS):
        lower, upper = along(mine, 1), along(mine, -1)
        if sweep == 0:
            own = [
                mine,
                start_packet(core, 1 - plane),
                start_packet(1 - core, plane),
                start_packet(1 - core, 1 - plane),
            ]
        else:
            own = spread(mine)
        packets = spread(lower) + own + spread(upper)
        sends, keeps = assign_tiles(points, near_ids, me, packets, rows)
        halves = [None] * 3
        for side in (0, 2, 1):
            halves[side] = (keeps[side], core_swap(sends[side]))
        planes = [None] * 3
        for side in (0, 2, 1):
            planes[side] = plane_swap(add_packets(me, halves[side], [], True))
        down = along(add_packets(me, halves[0], [planes[0]], False), -1)
        up = along(add_packets(me, halves[2], [planes[2]], False), 1)
        mine = renew(me, mine, halves[1], [planes[1], down, up], target)
    own = spread(mine)
    order = jnp.stack(
        [core * 2 + plane, core * 2 + 1 - plane, 2 - core * 2 + plane, 3 - core * 2 - plane]
    )
    stacked = jnp.stack(own)[jnp.argsort(order)]
    new_centroids = stacked[:, :quarter, :].reshape(rows, width)
    new_weights = stacked[:, quarter, :quarter].reshape(rows)
    return (new_centroids, new_weights)


def solution(mesh):
    return jax.shard_map(
        per_device,
        mesh=mesh,
        in_specs=(P(("group", "blk"), None), P(("group", "blk"), None), P("blk", None), P("blk")),
        out_specs=(P("blk", None), P("blk")),
        check_vma=False,
    )
```

time: 1160 us -> 282 us (0.24)
  waiting for transfers between devices: 495 us -> 105 us
  matrix products: 363 us -> 0 us
  local copies, waits for them, and re-layouts: 201 us -> 15.9 us
  Pallas kernels: 0 us -> 113 us
  other arithmetic: 30.6 us -> 4.53 us
  between operations: 14.1 us -> 1.03 us
  blocking collectives: 12.3 us -> 0 us
    dot_general x80 -> x0, matrix products: 304 us -> none  [the longest x16 162 us: tile_step(): jnp.dot(picker_f.T, numerator, precision=lax.Precision.HIGHEST, preferred...]
    ppermute x16 -> x38, waiting for transfers between devices: 390 us -> 105 us  [the longest x30 59.4 us: swap(): return lax.ppermute(x, 'group', [(i, i ^ bit) for i in range(groups)])]
    reshape x50 -> x1, local copies, waits for them, and re-layouts: 161 us -> 0.67 us  [per_device(): near_ids = near_ids.reshape(-1).astype(jnp.int32)]
    pallas_call x0 -> x14, Pallas kernels: none -> 113 us  [the longest x2 77.1 us: assign_tiles(): pl.pallas_call(functools.partial(tiles_kernel, rows), grid_spec=pltpu.Pre...]
    psum x2 -> x0, waiting for transfers between devices: 105 us -> none  [per_device(): total_num, total_mass = lax.psum((own_num, own_mass), 'group')]
    sub x16 -> x0, matrix products: 59.2 us -> none  [tile_step(): membership = jax.nn.softmax(scores, axis=-1).astype(jnp.bfloat16)]
    squeeze x12 -> x0, local copies, waits for them, and re-layouts: 17.4 us -> none  [the longest x4 6.82 us: return_cycle(): upper_num, upper_mass = passed_along((near_num[0], near_mass[0]), 'blk', -1)]
    slice x4 -> x2, local copies, waits for them, and re-layouts: 13.9 us -> 1.27 us  [the longest x1 1.25 us: per_device(): new_centroids = stacked[:, :quarter, :].reshape(rows, width)]
  transfers between devices with their start and end apart: 18 -> 38, of which waited for: 12 -> 21; matrix products, arithmetic and copies ran while one was open for 1% -> 1% of each run, Pallas kernels for 0% -> 10%
where the time goes in v1:
time: 282 us
  Pallas kernels  113 us (40%)
  waiting for transfers between devices  105 us (37%)
  starting transfers between devices  42.3 us (15%)
  local copies, waits for them, and re-layouts  15.9 us (6%)
  other arithmetic  4.53 us (2%)
    pallas_call x2, Pallas kernels, assign_tiles(): pl.pallas_call(functools.partial(tiles_kernel, rows), grid_spec=pltpu.Pre...  77.1 us
    ppermute x30, waiting for transfers between devices, swap(): return lax.ppermute(x, 'group', [(i, i ^ bit) for i in range(groups)])  59.4 us
    ppermute x8, waiting for transfers between devices, along(): lax.ppermute(x, 'blk', [((i - distance) % count, i) for i in range(count)])  46 us
    pallas_call x10, Pallas kernels, add_packets(): pl.pallas_call(functools.partial(sum_kernel, packet - TAIL), grid_spec=pl...  28.5 us
    ppermute x8, starting transfers between devices, along(): lax.ppermute(x, 'blk', [((i - distance) % count, i) for i in range(count)])  23.1 us
    ppermute x30, starting transfers between devices, swap(): return lax.ppermute(x, 'group', [(i, i ^ bit) for i in range(groups)])  19.1 us
    unnamed x69, local copies, waits for them, and re-layouts  11.6 us
    pallas_call x2, Pallas kernels, renew(): pl.pallas_call(functools.partial(renew_kernel, packet - TAIL, target), gr...  7 us
  transfers between devices with their start and end apart: 38, of which 21 were waited for; matrix products, arithmetic and copies ran while one was open for 1% of the time, Pallas kernels for 10%

profile of v1, /device:TPU:0, one launch (start us, length us, event | category | flops | bytes accessed | tf_op | source)
XLA Modules:
  0.0 281.6 jit_solution(2157009630072866728)
XLA Ops:
  2.3 3.0 %collective-permute-start = (bf16[272,768]{1,0:T(8,128)(2,1)S(1)}, bf16[272,768]{1,0:T(8,128)(2,1)S(1)}, u32[]{:S(2)}, u32[]{:S(2)}) collective-permute-start(bf16[272,768]{1,0:T(8,128)(2,1)S(1)} %fusion.4.refs_4_.base_ref), channel_id=1, source_target_pairs={{7,0},{0,1},{1,2},{2,3},{3,4},{4,5},{5,6},{6,7},{15,8},{8,9},{9,10... | collective-permute-start | bytes 1253384 | tf_op jit(solution)/shard_map/ppermute | solution.py:38
  5.3 3.1 %collective-permute-start.4 = (bf16[272,768]{1,0:T(8,128)(2,1)S(1)}, bf16[272,768]{1,0:T(8,128)(2,1)S(1)}, u32[]{:S(2)}, u32[]{:S(2)}) collective-permute-start(bf16[272,768]{1,0:T(8,128)(2,1)S(1)} %fusion.4.refs_4_.base_ref), channel_id=1, source_target_pairs={{1,0},{2,1},{3,2},{4,3},{5,4},{6,5},{7,6},{0,7},{9,8},{10,9},{11,1... | collective-permute-start | bytes 1253384 | tf_op jit(solution)/shard_map/ppermute | solution.py:38
  8.4 14.7 %collective-permute-done.refs_0_ = bf16[272,768]{1,0:T(8,128)(2,1)S(1)} collective-permute-done((bf16[272,768]{1,0:T(8,128)(2,1)S(1)}, bf16[272,768]{1,0:T(8,128)(2,1)S(1)}, u32[]{:S(2)}, u32[]{:S(2)}) %collective-permute-start) | collective-permute-done | bytes 417824 | tf_op jit(solution)/shard_map/ppermute | solution.py:38
  23.2 1.5 collective-permute-start.1
  25.4 1.5 collective-permute-start.5
  27.4 8.3 %collective-permute-done.1.refs_1_ = bf16[272,768]{1,0:T(8,128)(2,1)S(1)} collective-permute-done((bf16[272,768]{1,0:T(8,128)(2,1)S(1)}, bf16[272,768]{1,0:T(8,128)(2,1)S(1)}, u32[]{:S(2)}, u32[]{:S(2)}) %collective-permute-start.1) | collective-permute-done | bytes 417824 | tf_op jit(solution)/shard_map/ppermute | solution.py:25
  35.7 6.9 %collective-permute-done.5.refs_9_ = bf16[272,768]{1,0:T(8,128)(2,1)S(1)} collective-permute-done((bf16[272,768]{1,0:T(8,128)(2,1)S(1)}, bf16[272,768]{1,0:T(8,128)(2,1)S(1)}, u32[]{:S(2)}, u32[]{:S(2)}) %collective-permute-start.5) | collective-permute-done | bytes 417824 | tf_op jit(solution)/shard_map/ppermute | solution.py:25
  46.0 38.5 %tiles.2 = (bf16[544,768]{1,0:T(8,128)(2,1)}, bf16[544,768]{1,0:T(8,128)(2,1)}, bf16[544,768]{1,0:T(8,128)(2,1)}, f32[544,768]{1,0:T(8,128)}, f32[544,768]{1,0:T(8,128)}, /*index=5*/f32[544,768]{1,0:T(8,128)}) custom-call(s32[256]{0:T(256)} %reshape.10.ids_ref, s32[2]{0:T(128)} %pad_add_fusion.me_ref, bf16[8192,768]{1,0:T(8,128)(2,1)} %points_ref.3, ...), custom_call_target="tpu_custom_call" | custom-call | flops 6442450944 | bytes 12582912 | tf_op jit(solution)/shard_map/tiles/pallas_call | solution.py:224
  85.6 1.7 collective-permute-done.13.refs_1_
  88.3 2.8 add_packets.13
  91.0 1.5 collective-permute-start.14
  93.5 2.8 add_packets.11
  97.7 2.8 add_packets.10
  100.4 1.5 collective-permute-start.9
  102.0 1.7 collective-permute-done.14.refs_2_
  104.5 2.9 %add_packets.14 = bf16[272,768]{1,0:T(8,128)(2,1)} custom-call(s32[2]{0:T(128)} %pad_add_fusion.me_ref, f32[544,768]{1,0:T(8,128)} %get-tuple-element.19.refs_0_, bf16[544,768]{1,0:T(8,128)(2,1)} %copy-done.4, bf16[272,768]{1,0:T(8,128)(2,1)} %copy-done.15), custom_call_target="tpu_custom_call" | custom-call | flops 626688 | bytes 2924544 | tf_op jit(solution)/shard_map/add_packets/pallas_call | solution.py:282
  107.4 2.5 collective-permute-start.15
  109.9 2.8 collective-permute-done.11.refs_2_
  113.4 2.9 %add_packets.12 = bf16[272,768]{1,0:T(8,128)(2,1)} custom-call(s32[2]{0:T(128)} %pad_add_fusion.me_ref, f32[544,768]{1,0:T(8,128)} %get-tuple-element.17.refs_0_, bf16[544,768]{1,0:T(8,128)(2,1)} %copy-done.2, bf16[272,768]{1,0:T(8,128)(2,1)} %copy-done.13), custom_call_target="tpu_custom_call" | custom-call | flops 626688 | bytes 2924544 | tf_op jit(solution)/shard_map/add_packets/pallas_call | solution.py:282
  116.4 5.5 %collective-permute-start.12 = (bf16[272,768]{1,0:T(8,128)(2,1)}, bf16[272,768]{1,0:T(8,128)(2,1)S(1)}, u32[]{:S(2)}, u32[]{:S(2)}) collective-permute-start(bf16[272,768]{1,0:T(8,128)(2,1)} %add_packets.12), channel_id=1, source_target_pairs={{1,0},{2,1},{3,2},{4,3},{5,4},{6,5},{7,6},{0,7},{9,8},{10,9},{11,1... | collective-permute-start | bytes 1253384 | tf_op jit(solution)/shard_map/ppermute | solution.py:38
  122.0 8.8 %collective-permute-done.12.refs_3_ = bf16[272,768]{1,0:T(8,128)(2,1)S(1)} collective-permute-done((bf16[272,768]{1,0:T(8,128)(2,1)}, bf16[272,768]{1,0:T(8,128)(2,1)S(1)}, u32[]{:S(2)}, u32[]{:S(2)}) %collective-permute-start.12) | collective-permute-done | bytes 417824 | tf_op jit(solution)/shard_map/ppermute | solution.py:38
  131.7 3.5 %renew.2.refs_4_.base_ref = bf16[272,768]{1,0:T(8,128)(2,1)} custom-call(s32[2]{0:T(128)} %pad_add_fusion.me_ref, bf16[272,768]{1,0:T(8,128)(2,1)} %copy-done.6, f32[544,768]{1,0:T(8,128)} %get-tuple-element.15.refs_0_, bf16[544,768]{1,0:T(8,128)(2,1)} %copy-done.1, bf16[272,768]{1,0:T(8,128)(2,1)} %copy-done.8, bf16[272,768]{1,0:T(8,128)(2,1)} %copy-done.12, ...), custom_call_target="tpu_custom_call" | custom-call | tf_op jit(solution)/shard_map/renew/pallas_call | solution.py:328
  135.2 4.7 %collective-permute-start.23 = (bf16[272,768]{1,0:T(8,128)(2,1)}, bf16[272,768]{1,0:T(8,128)(2,1)S(1)}, u32[]{:S(2)}, u32[]{:S(2)}) collective-permute-start(bf16[272,768]{1,0:T(8,128)(2,1)} %renew.2.refs_4_.base_ref), channel_id=1, source_target_pairs={{1,0},{2,1},{3,2},{4,3},{5,4},{6,5},{7,6},{0,7},{9,8},{10,9},{11,1... | collective-permute-start | bytes 1253384 | tf_op jit(solution)/shard_map/ppermute | solution.py:38
  139.9 1.5 collective-permute-start.20
  141.4 12.4 %collective-permute-done.16.refs_0_ = bf16[272,768]{1,0:T(8,128)(2,1)S(1)} collective-permute-done((bf16[272,768]{1,0:T(8,128)(2,1)}, bf16[272,768]{1,0:T(8,128)(2,1)S(1)}, u32[]{:S(2)}, u32[]{:S(2)}) %collective-permute-start.16) | collective-permute-done | bytes 417824 | tf_op jit(solution)/shard_map/ppermute | solution.py:38
  153.8 1.5 collective-permute-start.17
  155.9 1.5 collective-permute-start.24
  158.0 8.3 %collective-permute-done.17.refs_1_ = bf16[272,768]{1,0:T(8,128)(2,1)S(1)} collective-permute-done((bf16[272,768]{1,0:T(8,128)(2,1)S(1)}, bf16[272,768]{1,0:T(8,128)(2,1)S(1)}, u32[]{:S(2)}, u32[]{:S(2)}) %collective-permute-start.17) | collective-permute-done | bytes 417824 | tf_op jit(solution)/shard_map/ppermute | solution.py:25
  166.3 7.8 %collective-permute-done.24.refs_9_ = bf16[272,768]{1,0:T(8,128)(2,1)S(1)} collective-permute-done((bf16[272,768]{1,0:T(8,128)(2,1)S(1)}, bf16[272,768]{1,0:T(8,128)(2,1)S(1)}, u32[]{:S(2)}, u32[]{:S(2)}) %collective-permute-start.24) | collective-permute-done | bytes 417824 | tf_op jit(solution)/shard_map/ppermute | solution.py:25
  174.2 1.7 collective-permute-done.26.refs_11_
  176.7 38.6 %tiles.3 = (bf16[544,768]{1,0:T(8,128)(2,1)}, bf16[544,768]{1,0:T(8,128)(2,1)}, bf16[544,768]{1,0:T(8,128)(2,1)}, f32[544,768]{1,0:T(8,128)}, f32[544,768]{1,0:T(8,128)}, /*index=5*/f32[544,768]{1,0:T(8,128)}) custom-call(s32[256]{0:T(256)} %reshape.10.ids_ref, s32[2]{0:T(128)} %pad_add_fusion.me_ref, bf16[8192,768]{1,0:T(8,128)(2,1)} %points_ref.3, ...), custom_call_target="tpu_custom_call" | custom-call | flops 6442450944 | bytes 12582912 | tf_op jit(solution)/shard_map/tiles/pallas_call | solution.py:224
  216.0 1.9 collective-permute-done.32.refs_1_
  218.9 2.8 %add_packets.18 = bf16[272,768]{1,0:T(8,128)(2,1)} custom-call(s32[2]{0:T(128)} %pad_add_fusion.me_ref, f32[544,768]{1,0:T(8,128)} %get-tuple-element.25.refs_0_, bf16[544,768]{1,0:T(8,128)(2,1)} %copy-done.5), custom_call_target="tpu_custom_call" | custom-call | flops 417792 | bytes 2506752 | tf_op jit(solution)/shard_map/add_packets/pallas_call | solution.py:282
  221.7 1.5 collective-permute-start.33
  224.1 2.8 add_packets.16
  228.3 2.8 add_packets.15
  231.1 1.5 collective-permute-start.28
  232.6 1.8 collective-permute-done.33.refs_2_
  235.2 3.0 %add_packets.19 = bf16[272,768]{1,0:T(8,128)(2,1)} custom-call(s32[2]{0:T(128)} %pad_add_fusion.me_ref, f32[544,768]{1,0:T(8,128)} %get-tuple-element.25.refs_0_, bf16[544,768]{1,0:T(8,128)(2,1)} %copy-done.5, bf16[272,768]{1,0:T(8,128)(2,1)} %copy-done.16), custom_call_target="tpu_custom_call" | custom-call | flops 626688 | bytes 2924544 | tf_op jit(solution)/shard_map/add_packets/pallas_call | solution.py:282
  238.2 2.4 collective-permute-start.34
  240.5 2.8 %collective-permute-done.30.refs_2_ = bf16[272,768]{1,0:T(8,128)(2,1)S(1)} collective-permute-done((bf16[272,768]{1,0:T(8,128)(2,1)}, bf16[272,768]{1,0:T(8,128)(2,1)S(1)}, u32[]{:S(2)}, u32[]{:S(2)}) %collective-permute-start.30) | collective-permute-done | bytes 417824 | tf_op jit(solution)/shard_map/ppermute | solution.py:25
  244.1 2.9 %add_packets.17 = bf16[272,768]{1,0:T(8,128)(2,1)} custom-call(s32[2]{0:T(128)} %pad_add_fusion.me_ref, f32[544,768]{1,0:T(8,128)} %get-tuple-element.23.refs_0_, bf16[544,768]{1,0:T(8,128)(2,1)} %copy-done.3, bf16[272,768]{1,0:T(8,128)(2,1)} %copy-done.14), custom_call_target="tpu_custom_call" | custom-call | flops 626688 | bytes 2924544 | tf_op jit(solution)/shard_map/add_packets/pallas_call | solution.py:282
  247.1 2.0 collective-permute-start.31
  249.0 2.5 collective-permute-done.28.refs_2_
  251.5 8.6 %collective-permute-done.31.refs_3_ = bf16[272,768]{1,0:T(8,128)(2,1)S(1)} collective-permute-done((bf16[272,768]{1,0:T(8,128)(2,1)}, bf16[272,768]{1,0:T(8,128)(2,1)S(1)}, u32[]{:S(2)}, u32[]{:S(2)}) %collective-permute-start.31) | collective-permute-done | bytes 417824 | tf_op jit(solution)/shard_map/ppermute | solution.py:38
  260.8 3.5 %renew.3 = bf16[272,768]{1,0:T(8,128)(2,1)} custom-call(s32[2]{0:T(128)} %pad_add_fusion.me_ref, bf16[272,768]{1,0:T(8,128)(2,1)} %renew.2.refs_4_.base_ref, f32[544,768]{1,0:T(8,128)} %get-tuple-element.21.refs_0_, bf16[544,768]{1,0:T(8,128)(2,1)} %copy-done, bf16[272,768]{1,0:T(8,128)(2,1)} %copy-done.7, bf16[272,768]{1,0:T(8,128)(2,1)} %copy-done.11, ...), custom_call_target="tpu_custom_call" | custom-call | tf_op jit(solution)/shard_map/renew/pallas_call | solution.py:328
  264.3 1.5 collective-permute-start.35
  265.9 10.3 %collective-permute-done.35 = bf16[272,768]{1,0:T(8,128)(2,1)S(1)} collective-permute-done((bf16[272,768]{1,0:T(8,128)(2,1)}, bf16[272,768]{1,0:T(8,128)(2,1)S(1)}, u32[]{:S(2)}, u32[]{:S(2)}) %collective-permute-start.35) | collective-permute-done | bytes 417824 | tf_op jit(solution)/shard_map/ppermute | solution.py:25
  (133 shorter events, 26.7 us)
Async XLA Ops:
  0.7 41.9 %copy-start.18 = (s32[64,4]{0,1:T(4,128)S(1)}, s32[64,4]{0,1:T(4,128)}, u32[]{:S(2)}) copy-start(s32[64,4]{0,1:T(4,128)} %param.5) | copy-start | bytes 3076
  2.3 43.6 %copy-start.6 = (bf16[272,768]{1,0:T(8,128)(2,1)}, bf16[272,768]{1,0:T(8,128)(2,1)S(1)}, u32[]{:S(2)}) copy-start(bf16[272,768]{1,0:T(8,128)(2,1)S(1)} %fusion.4.refs_4_.base_ref) | copy-start | bytes 1253380
  2.3 20.8 %collective-permute-start = (bf16[272,768]{1,0:T(8,128)(2,1)S(1)}, bf16[272,768]{1,0:T(8,128)(2,1)S(1)}, u32[]{:S(2)}, u32[]{:S(2)}) collective-permute-start(bf16[272,768]{1,0:T(8,128)(2,1)S(1)} %fusion.4.refs_4_.base_ref), channel_id=1, source_target_pairs={{7,0},{0,1},{1,2},{2,3},{3,4},{4,5},{5,6},{6,7},{15,8},{8,9},{9,10... | collective-permute-start | bytes 1253384 | tf_op jit(solution)/shard_map/ppermute | solution.py:38
  5.3 20.1 %collective-permute-start.4 = (bf16[272,768]{1,0:T(8,128)(2,1)S(1)}, bf16[272,768]{1,0:T(8,128)(2,1)S(1)}, u32[]{:S(2)}, u32[]{:S(2)}) collective-permute-start(bf16[272,768]{1,0:T(8,128)(2,1)S(1)} %fusion.4.refs_4_.base_ref), channel_id=1, source_target_pairs={{1,0},{2,1},{3,2},{4,3},{5,4},{6,5},{7,6},{0,7},{9,8},{10,9},{11,1... | collective-permute-start | bytes 1253384 | tf_op jit(solution)/shard_map/ppermute | solution.py:38
  23.2 22.8 %copy-start.19 = (bf16[272,768]{1,0:T(8,128)(2,1)}, bf16[272,768]{1,0:T(8,128)(2,1)S(1)}, u32[]{:S(2)}) copy-start(bf16[272,768]{1,0:T(8,128)(2,1)S(1)} %collective-permute-done.refs_0_) | copy-start | bytes 1253380
  23.2 12.6 %collective-permute-start.1 = (bf16[272,768]{1,0:T(8,128)(2,1)S(1)}, bf16[272,768]{1,0:T(8,128)(2,1)S(1)}, u32[]{:S(2)}, u32[]{:S(2)}) collective-permute-start(bf16[272,768]{1,0:T(8,128)(2,1)S(1)} %collective-permute-done.refs_0_), channel_id=1, source_target_pairs={{0,16},{8,24},{16,0},{24,8},{1,17},{9,25},{17,1},{25,9},{2,18},{10... | collective-permute-start | bytes 1253384 | tf_op jit(solution)/shard_map/ppermute | solution.py:25
  25.4 20.6 %copy-start.20 = (bf16[272,768]{1,0:T(8,128)(2,1)}, bf16[272,768]{1,0:T(8,128)(2,1)S(1)}, u32[]{:S(2)}) copy-start(bf16[272,768]{1,0:T(8,128)(2,1)S(1)} %collective-permute-done.4.refs_8_) | copy-start | bytes 1253380
  25.4 17.3 %collective-permute-start.5 = (bf16[272,768]{1,0:T(8,128)(2,1)S(1)}, bf16[272,768]{1,0:T(8,128)(2,1)S(1)}, u32[]{:S(2)}, u32[]{:S(2)}) collective-permute-start(bf16[272,768]{1,0:T(8,128)(2,1)S(1)} %collective-permute-done.4.refs_8_), channel_id=1, source_target_pairs={{0,16},{8,24},{16,0},{24,8},{1,17},{9,25},{17,1},{25,9},{2,18},{10... | collective-permute-start | bytes 1253384 | tf_op jit(solution)/shard_map/ppermute | solution.py:25
  26.9 19.0 %collective-permute-start.2 = (bf16[272,768]{1,0:T(8,128)(2,1)S(1)}, bf16[272,768]{1,0:T(8,128)(2,1)}, u32[]{:S(2)}, u32[]{:S(2)}) collective-permute-start(bf16[272,768]{1,0:T(8,128)(2,1)S(1)} %collective-permute-done.refs_0_), channel_id=1, source_target_pairs={{0,8},{8,0},{16,24},{24,16},{1,9},{9,1},{17,25},{25,17},{2,10},{10... | collective-permute-start | bytes 1253384 | tf_op jit(solution)/shard_map/ppermute | solution.py:25
  26.9 19.0 %collective-permute-start.6 = (bf16[272,768]{1,0:T(8,128)(2,1)S(1)}, bf16[272,768]{1,0:T(8,128)(2,1)}, u32[]{:S(2)}, u32[]{:S(2)}) collective-permute-start(bf16[272,768]{1,0:T(8,128)(2,1)S(1)} %collective-permute-done.4.refs_8_), channel_id=1, source_target_pairs={{0,8},{8,0},{16,24},{24,16},{1,9},{9,1},{17,25},{25,17},{2,10},{10... | collective-permute-start | bytes 1253384 | tf_op jit(solution)/shard_map/ppermute | solution.py:25
  35.7 10.2 %copy-start.21 = (bf16[272,768]{1,0:T(8,128)(2,1)}, bf16[272,768]{1,0:T(8,128)(2,1)S(1)}, u32[]{:S(2)}) copy-start(bf16[272,768]{1,0:T(8,128)(2,1)S(1)} %collective-permute-done.1.refs_1_) | copy-start | bytes 1253380
  35.7 10.2 %collective-permute-start.3 = (bf16[272,768]{1,0:T(8,128)(2,1)S(1)}, bf16[272,768]{1,0:T(8,128)(2,1)}, u32[]{:S(2)}, u32[]{:S(2)}) collective-permute-start(bf16[272,768]{1,0:T(8,128)(2,1)S(1)} %collective-permute-done.1.refs_1_), channel_id=1, source_target_pairs={{0,8},{8,0},{16,24},{24,16},{1,9},{9,1},{17,25},{25,17},{2,10},{10... | collective-permute-start | bytes 1253384 | tf_op jit(solution)/shard_map/ppermute | solution.py:25
  42.6 3.3 %collective-permute-start.7 = (bf16[272,768]{1,0:T(8,128)(2,1)S(1)}, bf16[272,768]{1,0:T(8,128)(2,1)}, u32[]{:S(2)}, u32[]{:S(2)}) collective-permute-start(bf16[272,768]{1,0:T(8,128)(2,1)S(1)} %collective-permute-done.5.refs_9_), channel_id=1, source_target_pairs={{0,8},{8,0},{16,24},{24,16},{1,9},{9,1},{17,25},{25,17},{2,10},{10... | collective-permute-start | bytes 1253384 | tf_op jit(solution)/shard_map/ppermute | solution.py:25
  84.5 2.8 collective-permute-start.13
  85.1 7.5 %collective-permute-start.10 = (bf16[544,768]{1,0:T(8,128)(2,1)}, bf16[544,768]{1,0:T(8,128)(2,1)S(1)}, u32[]{:S(2)}, u32[]{:S(2)}) collective-permute-start(bf16[544,768]{1,0:T(8,128)(2,1)} %get-tuple-element.18), channel_id=1, source_target_pairs={{0,8},{8,0},{16,24},{24,16},{1,9},{9,1},{17,25},{25,17},{2,10},{10... | collective-permute-start | bytes 2506760 | tf_op jit(solution)/shard_map/ppermute | solution.py:25
  85.2 11.6 %collective-permute-start.8 = (bf16[544,768]{1,0:T(8,128)(2,1)}, bf16[544,768]{1,0:T(8,128)(2,1)S(1)}, u32[]{:S(2)}, u32[]{:S(2)}) collective-permute-start(bf16[544,768]{1,0:T(8,128)(2,1)} %get-tuple-element.16), channel_id=1, source_target_pairs={{0,8},{8,0},{16,24},{24,16},{1,9},{9,1},{17,25},{25,17},{2,10},{10... | collective-permute-start | bytes 2506760 | tf_op jit(solution)/shard_map/ppermute | solution.py:25
  91.0 12.7 %collective-permute-start.14 = (bf16[272,768]{1,0:T(8,128)(2,1)}, bf16[272,768]{1,0:T(8,128)(2,1)S(1)}, u32[]{:S(2)}, u32[]{:S(2)}) collective-permute-start(bf16[272,768]{1,0:T(8,128)(2,1)} %add_packets.13), channel_id=1, source_target_pairs={{0,16},{8,24},{16,0},{24,8},{1,17},{9,25},{17,1},{25,9},{2,18},{10... | collective-permute-start | bytes 1253384 | tf_op jit(solution)/shard_map/ppermute | solution.py:25
  96.3 16.4 %collective-permute-start.11 = (bf16[272,768]{1,0:T(8,128)(2,1)}, bf16[272,768]{1,0:T(8,128)(2,1)S(1)}, u32[]{:S(2)}, u32[]{:S(2)}) collective-permute-start(bf16[272,768]{1,0:T(8,128)(2,1)} %add_packets.11), channel_id=1, source_target_pairs={{0,16},{8,24},{16,0},{24,8},{1,17},{9,25},{17,1},{25,9},{2,18},{10... | collective-permute-start | bytes 1253384 | tf_op jit(solution)/shard_map/ppermute | solution.py:25
  100.4 21.4 %collective-permute-start.9 = (bf16[272,768]{1,0:T(8,128)(2,1)}, bf16[272,768]{1,0:T(8,128)(2,1)S(1)}, u32[]{:S(2)}, u32[]{:S(2)}) collective-permute-start(bf16[272,768]{1,0:T(8,128)(2,1)} %add_packets.10), channel_id=1, source_target_pairs={{0,16},{8,24},{16,0},{24,8},{1,17},{9,25},{17,1},{25,9},{2,18},{10... | collective-permute-start | bytes 1253384 | tf_op jit(solution)/shard_map/ppermute | solution.py:25
  107.4 14.6 %collective-permute-start.15 = (bf16[272,768]{1,0:T(8,128)(2,1)}, bf16[272,768]{1,0:T(8,128)(2,1)S(1)}, u32[]{:S(2)}, u32[]{:S(2)}) collective-permute-start(bf16[272,768]{1,0:T(8,128)(2,1)} %add_packets.14), channel_id=1, source_target_pairs={{7,0},{0,1},{1,2},{2,3},{3,4},{4,5},{5,6},{6,7},{15,8},{8,9},{9,10... | collective-permute-start | bytes 1253384 | tf_op jit(solution)/shard_map/ppermute | solution.py:38
  116.4 14.5 %collective-permute-start.12 = (bf16[272,768]{1,0:T(8,128)(2,1)}, bf16[272,768]{1,0:T(8,128)(2,1)S(1)}, u32[]{:S(2)}, u32[]{:S(2)}) collective-permute-start(bf16[272,768]{1,0:T(8,128)(2,1)} %add_packets.12), channel_id=1, source_target_pairs={{1,0},{2,1},{3,2},{4,3},{5,4},{6,5},{7,6},{0,7},{9,8},{10,9},{11,1... | collective-permute-start | bytes 1253384 | tf_op jit(solution)/shard_map/ppermute | solution.py:38
  135.2 18.6 %collective-permute-start.16 = (bf16[272,768]{1,0:T(8,128)(2,1)}, bf16[272,768]{1,0:T(8,128)(2,1)S(1)}, u32[]{:S(2)}, u32[]{:S(2)}) collective-permute-start(bf16[272,768]{1,0:T(8,128)(2,1)} %renew.2.refs_4_.base_ref), channel_id=1, source_target_pairs={{7,0},{0,1},{1,2},{2,3},{3,4},{4,5},{5,6},{6,7},{15,8},{8,9},{9,10... | collective-permute-start | bytes 1253384 | tf_op jit(solution)/shard_map/ppermute | solution.py:38
  135.2 20.7 %collective-permute-start.23 = (bf16[272,768]{1,0:T(8,128)(2,1)}, bf16[272,768]{1,0:T(8,128)(2,1)S(1)}, u32[]{:S(2)}, u32[]{:S(2)}) collective-permute-start(bf16[272,768]{1,0:T(8,128)(2,1)} %renew.2.refs_4_.base_ref), channel_id=1, source_target_pairs={{1,0},{2,1},{3,2},{4,3},{5,4},{6,5},{7,6},{0,7},{9,8},{10,9},{11,1... | collective-permute-start | bytes 1253384 | tf_op jit(solution)/shard_map/ppermute | solution.py:38
  139.9 17.5 %collective-permute-start.20 = (bf16[272,768]{1,0:T(8,128)(2,1)}, bf16[272,768]{1,0:T(8,128)(2,1)S(1)}, u32[]{:S(2)}, u32[]{:S(2)}) collective-permute-start(bf16[272,768]{1,0:T(8,128)(2,1)} %renew.2.refs_4_.base_ref), channel_id=1, source_target_pairs={{0,16},{8,24},{16,0},{24,8},{1,17},{9,25},{17,1},{25,9},{2,18},{10... | collective-permute-start | bytes 1253384 | tf_op jit(solution)/shard_map/ppermute | solution.py:25
  141.4 16.5 %collective-permute-start.21 = (bf16[272,768]{1,0:T(8,128)(2,1)}, bf16[272,768]{1,0:T(8,128)(2,1)S(1)}, u32[]{:S(2)}, u32[]{:S(2)}) collective-permute-start(bf16[272,768]{1,0:T(8,128)(2,1)} %renew.2.refs_4_.base_ref), channel_id=1, source_target_pairs={{0,8},{8,0},{16,24},{24,16},{1,9},{9,1},{17,25},{25,17},{2,10},{10... | collective-permute-start | bytes 1253384 | tf_op jit(solution)/shard_map/ppermute | solution.py:25
  153.8 22.1 %copy-start.22 = (bf16[272,768]{1,0:T(8,128)(2,1)}, bf16[272,768]{1,0:T(8,128)(2,1)S(1)}, u32[]{:S(2)}) copy-start(bf16[272,768]{1,0:T(8,128)(2,1)S(1)} %collective-permute-done.16.refs_0_) | copy-start | bytes 1253380
  153.8 12.5 %collective-permute-start.17 = (bf16[272,768]{1,0:T(8,128)(2,1)S(1)}, bf16[272,768]{1,0:T(8,128)(2,1)S(1)}, u32[]{:S(2)}, u32[]{:S(2)}) collective-permute-start(bf16[272,768]{1,0:T(8,128)(2,1)S(1)} %collective-permute-done.16.refs_0_), channel_id=1, source_target_pairs={{0,16},{8,24},{16,0},{24,8},{1,17},{9,25},{17,1},{25,9},{2,18},{10... | collective-permute-start | bytes 1253384 | tf_op jit(solution)/shard_map/ppermute | solution.py:25
  155.9 20.0 %copy-start.23 = (bf16[272,768]{1,0:T(8,128)(2,1)}, bf16[272,768]{1,0:T(8,128)(2,1)S(1)}, u32[]{:S(2)}) copy-start(bf16[272,768]{1,0:T(8,128)(2,1)S(1)} %collective-permute-done.23.refs_8_) | copy-start | bytes 1253380
  155.9 18.2 %collective-permute-start.24 = (bf16[272,768]{1,0:T(8,128)(2,1)S(1)}, bf16[272,768]{1,0:T(8,128)(2,1)S(1)}, u32[]{:S(2)}, u32[]{:S(2)}) collective-permute-start(bf16[272,768]{1,0:T(8,128)(2,1)S(1)} %collective-permute-done.23.refs_8_), channel_id=1, source_target_pairs={{0,16},{8,24},{16,0},{24,8},{1,17},{9,25},{17,1},{25,9},{2,18},{10... | collective-permute-start | bytes 1253384 | tf_op jit(solution)/shard_map/ppermute | solution.py:25
  157.4 16.7 %collective-permute-start.18 = (bf16[272,768]{1,0:T(8,128)(2,1)S(1)}, bf16[272,768]{1,0:T(8,128)(2,1)S(1)}, u32[]{:S(2)}, u32[]{:S(2)}) collective-permute-start(bf16[272,768]{1,0:T(8,128)(2,1)S(1)} %collective-permute-done.16.refs_0_), channel_id=1, source_target_pairs={{0,8},{8,0},{16,24},{24,16},{1,9},{9,1},{17,25},{25,17},{2,10},{10... | collective-permute-start | bytes 1253384 | tf_op jit(solution)/shard_map/ppermute | solution.py:25
  157.4 18.4 %copy-start.25 = (bf16[272,768]{1,0:T(8,128)(2,1)}, bf16[272,768]{1,0:T(8,128)(2,1)S(1)}, u32[]{:S(2)}) copy-start(bf16[272,768]{1,0:T(8,128)(2,1)S(1)} %collective-permute-done.20.refs_5_) | copy-start | bytes 1253380
  157.4 16.7 %collective-permute-start.25 = (bf16[272,768]{1,0:T(8,128)(2,1)S(1)}, bf16[272,768]{1,0:T(8,128)(2,1)S(1)}, u32[]{:S(2)}, u32[]{:S(2)}) collective-permute-start(bf16[272,768]{1,0:T(8,128)(2,1)S(1)} %collective-permute-done.23.refs_8_), channel_id=1, source_target_pairs={{0,8},{8,0},{16,24},{24,16},{1,9},{9,1},{17,25},{25,17},{2,10},{10... | collective-permute-start | bytes 1253384 | tf_op jit(solution)/shard_map/ppermute | solution.py:25
  157.9 17.9 %copy-start.26 = (bf16[272,768]{1,0:T(8,128)(2,1)}, bf16[272,768]{1,0:T(8,128)(2,1)S(1)}, u32[]{:S(2)}) copy-start(bf16[272,768]{1,0:T(8,128)(2,1)S(1)} %collective-permute-done.21.refs_6_) | copy-start | bytes 1253380
  157.9 16.2 %collective-permute-start.22 = (bf16[272,768]{1,0:T(8,128)(2,1)S(1)}, bf16[272,768]{1,0:T(8,128)(2,1)S(1)}, u32[]{:S(2)}, u32[]{:S(2)}) collective-permute-start(bf16[272,768]{1,0:T(8,128)(2,1)S(1)} %collective-permute-done.20.refs_5_), channel_id=1, source_target_pairs={{0,8},{8,0},{16,24},{24,16},{1,9},{9,1},{17,25},{25,17},{2,10},{10... | collective-permute-start | bytes 1253384 | tf_op jit(solution)/shard_map/ppermute | solution.py:25
  166.3 9.5 %copy-start.27 = (bf16[272,768]{1,0:T(8,128)(2,1)}, bf16[272,768]{1,0:T(8,128)(2,1)S(1)}, u32[]{:S(2)}) copy-start(bf16[272,768]{1,0:T(8,128)(2,1)S(1)} %collective-permute-done.17.refs_1_) | copy-start | bytes 1253380
  166.3 7.8 %collective-permute-start.19 = (bf16[272,768]{1,0:T(8,128)(2,1)S(1)}, bf16[272,768]{1,0:T(8,128)(2,1)S(1)}, u32[]{:S(2)}, u32[]{:S(2)}) collective-permute-start(bf16[272,768]{1,0:T(8,128)(2,1)S(1)} %collective-permute-done.17.refs_1_), channel_id=1, source_target_pairs={{0,8},{8,0},{16,24},{24,16},{1,9},{9,1},{17,25},{25,17},{2,10},{10... | collective-permute-start | bytes 1253384 | tf_op jit(solution)/shard_map/ppermute | solution.py:25
  174.1 1.8 collective-permute-start.26
  215.3 2.6 collective-permute-start.32
  215.5 7.8 %collective-permute-start.29 = (bf16[544,768]{1,0:T(8,128)(2,1)}, bf16[544,768]{1,0:T(8,128)(2,1)S(1)}, u32[]{:S(2)}, u32[]{:S(2)}) collective-permute-start(bf16[544,768]{1,0:T(8,128)(2,1)} %get-tuple-element.24), channel_id=1, source_target_pairs={{0,8},{8,0},{16,24},{24,16},{1,9},{9,1},{17,25},{25,17},{2,10},{10... | collective-permute-start | bytes 2506760 | tf_op jit(solution)/shard_map/ppermute | solution.py:25
  215.9 11.5 %collective-permute-start.27 = (bf16[544,768]{1,0:T(8,128)(2,1)}, bf16[544,768]{1,0:T(8,128)(2,1)S(1)}, u32[]{:S(2)}, u32[]{:S(2)}) collective-permute-start(bf16[544,768]{1,0:T(8,128)(2,1)} %get-tuple-element.22), channel_id=1, source_target_pairs={{0,8},{8,0},{16,24},{24,16},{1,9},{9,1},{17,25},{25,17},{2,10},{10... | collective-permute-start | bytes 2506760 | tf_op jit(solution)/shard_map/ppermute | solution.py:25
  221.7 12.7 %collective-permute-start.33 = (bf16[272,768]{1,0:T(8,128)(2,1)}, bf16[272,768]{1,0:T(8,128)(2,1)S(1)}, u32[]{:S(2)}, u32[]{:S(2)}) collective-permute-start(bf16[272,768]{1,0:T(8,128)(2,1)} %add_packets.18), channel_id=1, source_target_pairs={{0,16},{8,24},{16,0},{24,8},{1,17},{9,25},{17,1},{25,9},{2,18},{10... | collective-permute-start | bytes 1253384 | tf_op jit(solution)/shard_map/ppermute | solution.py:25
  226.9 16.5 %collective-permute-start.30 = (bf16[272,768]{1,0:T(8,128)(2,1)}, bf16[272,768]{1,0:T(8,128)(2,1)S(1)}, u32[]{:S(2)}, u32[]{:S(2)}) collective-permute-start(bf16[272,768]{1,0:T(8,128)(2,1)} %add_packets.16), channel_id=1, source_target_pairs={{0,16},{8,24},{16,0},{24,8},{1,17},{9,25},{17,1},{25,9},{2,18},{10... | collective-permute-start | bytes 1253384 | tf_op jit(solution)/shard_map/ppermute | solution.py:25
  231.1 20.4 %collective-permute-start.28 = (bf16[272,768]{1,0:T(8,128)(2,1)}, bf16[272,768]{1,0:T(8,128)(2,1)S(1)}, u32[]{:S(2)}, u32[]{:S(2)}) collective-permute-start(bf16[272,768]{1,0:T(8,128)(2,1)} %add_packets.15), channel_id=1, source_target_pairs={{0,16},{8,24},{16,0},{24,8},{1,17},{9,25},{17,1},{25,9},{2,18},{10... | collective-permute-start | bytes 1253384 | tf_op jit(solution)/shard_map/ppermute | solution.py:25
  238.2 13.4 %collective-permute-start.34 = (bf16[272,768]{1,0:T(8,128)(2,1)}, bf16[272,768]{1,0:T(8,128)(2,1)S(1)}, u32[]{:S(2)}, u32[]{:S(2)}) collective-permute-start(bf16[272,768]{1,0:T(8,128)(2,1)} %add_packets.19), channel_id=1, source_target_pairs={{7,0},{0,1},{1,2},{2,3},{3,4},{4,5},{5,6},{6,7},{15,8},{8,9},{9,10... | collective-permute-start | bytes 1253384 | tf_op jit(solution)/shard_map/ppermute | solution.py:38
  247.1 13.0 %collective-permute-start.31 = (bf16[272,768]{1,0:T(8,128)(2,1)}, bf16[272,768]{1,0:T(8,128)(2,1)S(1)}, u32[]{:S(2)}, u32[]{:S(2)}) collective-permute-start(bf16[272,768]{1,0:T(8,128)(2,1)} %add_packets.17), channel_id=1, source_target_pairs={{1,0},{2,1},{3,2},{4,3},{5,4},{6,5},{7,6},{0,7},{9,8},{10,9},{11,1... | collective-permute-start | bytes 1253384 | tf_op jit(solution)/shard_map/ppermute | solution.py:38
  264.3 11.8 %collective-permute-start.35 = (bf16[272,768]{1,0:T(8,128)(2,1)}, bf16[272,768]{1,0:T(8,128)(2,1)S(1)}, u32[]{:S(2)}, u32[]{:S(2)}) collective-permute-start(bf16[272,768]{1,0:T(8,128)(2,1)} %renew.3), channel_id=1, source_target_pairs={{0,16},{8,24},{16,0},{24,8},{1,17},{9,25},{17,1},{25,9},{2,18},{10... | collective-permute-start | bytes 1253384 | tf_op jit(solution)/shard_map/ppermute | solution.py:25
  265.8 11.1 %collective-permute-start.36 = (bf16[272,768]{1,0:T(8,128)(2,1)}, bf16[272,768]{1,0:T(8,128)(2,1)S(1)}, u32[]{:S(2)}, u32[]{:S(2)}) collective-permute-start(bf16[272,768]{1,0:T(8,128)(2,1)} %renew.3), channel_id=1, source_target_pairs={{0,8},{8,0},{16,24},{24,16},{1,9},{9,1},{17,25},{25,17},{2,10},{10... | collective-permute-start | bytes 1253384 | tf_op jit(solution)/shard_map/ppermute | solution.py:25
  276.1 1.8 collective-permute-start.37
  (24 other events, 59.7 us)

commit v2 on v1

v2 whole, which is shorter than its diff:
```python
import functools

import jax
import jax.numpy as jnp
from jax import lax
from jax.experimental import pallas as pl
from jax.experimental.pallas import tpu as pltpu
from jax.sharding import PartitionSpec as P

BLOCK = 64
TILE = 128
SLOTS = 4
ITERS = 2
TAIL = 16
STEP_TILES = 8
CHUNKS = 2
prior_mass = 1.0
dual_step = 0.5
F32 = jnp.float32
BF16 = jnp.bfloat16
VMEM_LIMIT = 36 * 1024 * 1024
SMALL_LIMIT = 16 * 1024 * 1024


def swap(x, bit):
    groups = lax.axis_size("group")
    return lax.ppermute(x, "group", [(i, i ^ bit) for i in range(groups)])


def core_swap(x):
    return swap(x, 1)


def plane_swap(x):
    return swap(x, 2)


def pair_swap(x):
    count = lax.axis_size("blk")
    return lax.ppermute(x, "blk", [(i, i ^ 1) for i in range(count)])


def outward(x):
    count = lax.axis_size("blk")
    return lax.ppermute(x, "blk", [(i, (i + 2 - i % 2 * 4) % count) for i in range(count)])


def inward(x):
    count = lax.axis_size("blk")
    return lax.ppermute(x, "blk", [((i + 2 - i % 2 * 4) % count, i) for i in range(count)])


def ranges(quarter):
    size = quarter // CHUNKS
    return [(k * size, (k + 1) * size) for k in range(CHUNKS)]


def part_rows(part, quarter):
    return part[1] - part[0] + (TAIL if part[1] == quarter else 0)


def eye():
    shape = (TILE, TILE)
    return lax.broadcasted_iota(jnp.int32, shape, 0) == lax.broadcasted_iota(jnp.int32, shape, 1)


def to_column(row):
    return jnp.sum(jnp.where(eye(), row, 0.0), axis=1, keepdims=True)


def to_row(column):
    return jnp.sum(jnp.where(eye(), column, 0.0), axis=0, keepdims=True)


def split_masses(row):
    high = row.astype(BF16)
    rest = row - high.astype(F32)
    mid = rest.astype(BF16)
    low = (rest - mid.astype(F32)).astype(BF16)
    return jnp.concatenate([high, mid, low], axis=1)


def tail_of(row):
    wide = jnp.broadcast_to(row.astype(F32), (TAIL, row.shape[1]))
    first = lax.broadcasted_iota(jnp.int32, wide.shape, 0) == 0
    return jnp.where(first, wide, 0.0)


def mass_of(tail, quarter):
    row = tail[0:1, :].astype(F32)
    return row[:, :quarter] + row[:, quarter : 2 * quarter] + row[:, 2 * quarter : 3 * quarter]


def tiles_kernel(rows, sizes, ids_ref, me_ref, points_ref, *refs):
    quarter = rows // 4
    packet = quarter + TAIL
    half = rows // 2
    count = sum(len(parts) for side in sizes for parts in side)
    parts_refs = list(refs[:count])
    sends = refs[count : count + 3]
    keeps = refs[count + 3 : count + 6]
    near, tails, offs, acc, macc, in_sem = refs[count + 6 :]
    step = pl.program_id(0)
    core = me_ref[0]
    plane = me_ref[1]

    def arrivals():
        out = []
        left = list(parts_refs)
        for side in range(3):
            for j in range(4):
                c = core if j < 2 else 1 - core
                y = plane if j % 2 == 0 else 1 - plane
                at = side * 4 + c * 2 + y
                first = 0
                for size in sizes[side][j]:
                    ref = left.pop(0)
                    last = min(first + size, quarter)
                    out.append(
                        pltpu.make_async_copy(
                            ref.at[pl.ds(0, last - first)],
                            near.at[
                                pl.ds(pl.multiple_of(at * quarter + first, TILE), last - first)
                            ],
                            in_sem.at[len(out)],
                        )
                    )
                    if first + size > quarter:
                        out.append(
                            pltpu.make_async_copy(
                                ref.at[pl.ds(last - first, TAIL)],
                                tails.at[pl.ds(pl.multiple_of(at * TAIL, TAIL), TAIL)],
                                in_sem.at[len(out)],
                            )
                        )
                    first = last
        return out

    width = near.shape[1]

    @pl.when(step == 0)
    def _():
        copies = arrivals()
        for copy in copies:
            copy.start()

        @pl.loop(0, 3 * rows // BLOCK)
        def _(b):
            at = pl.ds(pl.multiple_of(b * BLOCK, BLOCK), BLOCK)
            acc[at, :] = jnp.zeros((BLOCK, width), F32)
            macc[at, :] = jnp.zeros((BLOCK, TILE), F32)

        for copy in copies:
            copy.wait()

        @pl.loop(0, 12)
        def _(n):
            tail = tails[pl.ds(pl.multiple_of(n * TAIL, TAIL), TAIL), :].astype(F32)
            for k in range(quarter // TILE):
                at = pl.ds(pl.multiple_of(n * quarter + k * TILE, TILE), TILE)
                base = near[at, :].astype(F32)
                squares = jnp.sum(base * base, axis=1, keepdims=True)
                weights = to_column(tail[0:1, k * TILE : (k + 1) * TILE])
                offs[at, :] = jnp.broadcast_to(weights - squares * (16.0 / width), (TILE, TILE))

    def blocks_of(t):
        tile = step * STEP_TILES + t
        return [
            pl.ds(pl.multiple_of(ids_ref[tile * SLOTS + k] * BLOCK, BLOCK), BLOCK)
            for k in range(SLOTS)
        ]

    members = []
    for t in range(STEP_TILES):
        points = points_ref[pl.ds(t * TILE, TILE), :]
        at = blocks_of(t)
        cand = jnp.concatenate([near[a, :] for a in at], axis=0)
        off = jnp.concatenate([offs[a, :] for a in at], axis=0)
        scores = lax.dot_general(
            cand, points, (((1,), (1,)), ((), ())), preferred_element_type=F32
        )
        scores = scores * (32.0 / width) + off
        top = jnp.max(scores, axis=0, keepdims=True)
        raw = jnp.exp(scores - top)
        total = jnp.sum(raw, axis=0, keepdims=True)
        members.append((raw * (1.0 / total)).astype(BF16))
    for t in range(STEP_TILES):
        points = points_ref[pl.ds(t * TILE, TILE), :]
        at = blocks_of(t)
        numerator = jnp.dot(members[t], points, preferred_element_type=F32)
        masses = members[t].astype(F32)
        for k in range(SLOTS):
            acc[at[k], :] += numerator[k * BLOCK : (k + 1) * BLOCK]
            macc[at[k], :] += masses[k * BLOCK : (k + 1) * BLOCK]

    @pl.when(step == pl.num_programs(0) - 1)
    def _():
        def masses_at(start):
            return jnp.concatenate(
                [
                    to_row(jnp.sum(macc[pl.ds(start + k * TILE, TILE), :], axis=1, keepdims=True))
                    for k in range(quarter // TILE)
                ],
                axis=1,
            )

        for side in range(3):
            for y in range(2):
                mine = pl.multiple_of(side * rows + core * half + y * quarter, quarter)
                other = pl.multiple_of(side * rows + (1 - core) * half + y * quarter, quarter)
                body = pl.ds(y * packet, quarter)
                tail = pl.ds(y * packet + quarter, TAIL)
                sends[side][body, :] = acc[pl.ds(other, quarter), :].astype(BF16)
                sends[side][tail, :] = tail_of(split_masses(masses_at(other))).astype(BF16)
                row = masses_at(mine)
                keeps[side][body, :] = acc[pl.ds(mine, quarter), :]
                keeps[side][tail, :] = tail_of(
                    jnp.concatenate([row, row * 0.0, row * 0.0], axis=1)
                )


def assign_tiles(points, ids, me, packets, rows):
    count, width = points.shape
    quarter = rows // 4
    packet = quarter + TAIL
    tiles = count // TILE
    any_spec = pl.BlockSpec(memory_space=pl.ANY)
    vmem_spec = pl.BlockSpec(memory_space=pltpu.VMEM)
    step_rows = STEP_TILES * TILE
    sizes = [[[part.shape[0] for part in parts] for parts in side] for side in packets]
    arrays = [part for side in packets for parts in side for part in parts]
    outs = pl.pallas_call(
        functools.partial(tiles_kernel, rows, sizes),
        grid_spec=pltpu.PrefetchScalarGridSpec(
            num_scalar_prefetch=2,
            grid=(tiles // STEP_TILES,),
            in_specs=[pl.BlockSpec((step_rows, width), lambda i, ids, me: (i, 0))]
            + [any_spec] * len(arrays),
            out_specs=[vmem_spec] * 6,
            scratch_shapes=[
                pltpu.VMEM((3 * rows, width), BF16),
                pltpu.VMEM((12 * TAIL, width), BF16),
                pltpu.VMEM((3 * rows, TILE), F32),
                pltpu.VMEM((3 * rows, width), F32),
                pltpu.VMEM((3 * rows, TILE), F32),
                pltpu.SemaphoreType.DMA((len(arrays) + 12,)),
            ],
        ),
        out_shape=[jax.ShapeDtypeStruct((2 * packet, width), BF16)] * 3
        + [jax.ShapeDtypeStruct((2 * packet, width), F32)] * 3,
        compiler_params=pltpu.CompilerParams(vmem_limit_bytes=VMEM_LIMIT),
        cost_estimate=pl.CostEstimate(
            flops=4 * count * SLOTS * BLOCK * width,
            bytes_accessed=2 * count * width,
            transcendentals=count * SLOTS * BLOCK,
        ),
        name="tiles",
    )(ids, me, points, *arrays)
    return outs[:3], outs[3:]


def small_call(kernel, me, arrays, outs, name):
    vmem_spec = pl.BlockSpec(memory_space=pltpu.VMEM)
    return pl.pallas_call(
        kernel,
        in_specs=[pl.BlockSpec(memory_space=pltpu.SMEM)] + [vmem_spec] * len(arrays),
        out_specs=[vmem_spec] * len(outs),
        out_shape=outs,
        compiler_params=pltpu.CompilerParams(vmem_limit_bytes=SMALL_LIMIT),
        cost_estimate=pl.CostEstimate(
            flops=sum(a.size for a in arrays),
            bytes_accessed=sum(a.size * a.dtype.itemsize for a in arrays),
            transcendentals=0,
        ),
        name=name,
    )(me, *arrays)


def sum_kernel(quarter, pairs, other, parts, me_ref, *refs):
    terms = refs[: len(refs) - len(parts)]
    outs = refs[len(refs) - len(parts) :]
    plane = 1 - me_ref[1] if other else me_ref[1]
    start = plane * (quarter + TAIL)

    def rows_of(first, size):
        at = [pl.ds(pl.multiple_of(start + first, TAIL), size)] * pairs
        at += [pl.ds(first - parts[0][0], size)] * (len(terms) - pairs)
        return [term[a, :] for term, a in zip(terms, at)]

    for (first, last), out in zip(parts, outs):
        size = last - first
        out[pl.ds(0, size), :] = sum(r.astype(F32) for r in rows_of(first, size)).astype(BF16)
        if last == quarter:
            mass = sum(mass_of(r, quarter) for r in rows_of(quarter, TAIL))
            out[pl.ds(size, TAIL), :] = tail_of(split_masses(mass)).astype(BF16)


def add_packets(me, pairs, singles, other, parts):
    packet, width = pairs[0].shape[0] // 2, pairs[0].shape[1]
    quarter = packet - TAIL
    return small_call(
        functools.partial(sum_kernel, quarter, len(pairs), other, parts),
        me,
        [*pairs, *singles],
        [jax.ShapeDtypeStruct((part_rows(p, quarter), width), BF16) for p in parts],
        "add_packets",
    )


def renew_kernel(quarter, target, whole, parts, me_ref, base, keep, beside, plane_sum, *refs):
    arrived = refs[: len(parts)]
    outs = refs[len(parts) :]
    start = me_ref[1] * (quarter + TAIL)
    mass = mass_of(arrived[-1][pl.ds(parts[-1][1] - parts[-1][0], TAIL), :], quarter)
    mass = mass + mass_of(plane_sum[pl.ds(quarter, TAIL), :], quarter)
    for term in (keep, beside):
        tail = term[pl.ds(pl.multiple_of(start + quarter, TAIL), TAIL), :]
        mass = mass + mass_of(tail, quarter)
    weights = base[pl.ds(quarter, TAIL), :].astype(F32)[0:1, :quarter]
    renewed = weights + dual_step * (1.0 - mass / target)
    zero = renewed * 0.0
    tail = tail_of(jnp.concatenate([renewed, zero, zero], axis=1)).astype(BF16)
    for k, (first, last) in enumerate(parts):
        for row in range(first, last, TILE):
            here = pl.ds(pl.multiple_of(start + row, TAIL), TILE)
            total = keep[here, :] + beside[here, :].astype(F32)
            total = total + plane_sum[pl.ds(row, TILE), :].astype(F32)
            total = total + arrived[k][pl.ds(row - first, TILE), :].astype(F32)
            column = to_column(mass[:, row : row + TILE]) + prior_mass
            total = total + prior_mass * base[pl.ds(row, TILE), :].astype(F32)
            fresh = (total / column).astype(BF16)
            outs[k][pl.ds(row - first, TILE), :] = fresh
            if whole:
                outs[-1][pl.ds(row, TILE), :] = fresh
    outs[len(parts) - 1][pl.ds(parts[-1][1] - parts[-1][0], TAIL), :] = tail
    if whole:
        outs[-1][pl.ds(quarter, TAIL), :] = tail


def renew(me, base, keep, beside, plane_sum, arrived, target, whole):
    packet, width = base.shape
    quarter = packet - TAIL
    parts = ranges(quarter)
    outs = [jax.ShapeDtypeStruct((part_rows(p, quarter), width), BF16) for p in parts]
    if whole:
        outs.append(jax.ShapeDtypeStruct((packet, width), BF16))
    return small_call(
        functools.partial(renew_kernel, quarter, target, whole, parts),
        me,
        [base, keep, beside, plane_sum, *arrived],
        outs,
        "renew",
    )


def finish_kernel(rows, parts, me_ref, *refs):
    quarter = rows // 4
    n = 4 * len(parts)
    packets = refs[:n]
    out, weights_out, tails, sem = refs[n:]
    core, plane = me_ref[0], me_ref[1]
    copies = []
    places = []
    for j in range(4):
        c = core if j < 2 else 1 - core
        y = plane if j % 2 == 0 else 1 - plane
        places.append(c * 2 + y)
        for k, (first, last) in enumerate(parts):
            ref = packets[j * len(parts) + k]
            at = pl.multiple_of(places[j] * quarter + first, TILE)
            copies.append(
                pltpu.make_async_copy(
                    ref.at[pl.ds(0, last - first)],
                    out.at[pl.ds(at, last - first)],
                    sem.at[len(copies)],
                )
            )
            if last == quarter:
                copies.append(
                    pltpu.make_async_copy(
                        ref.at[pl.ds(last - first, TAIL)], tails.at[j], sem.at[len(copies)]
                    )
                )
    for copy in copies:
        copy.start()
    for copy in copies:
        copy.wait()
    found = [tails[j][0:1, :quarter].astype(F32) for j in range(4)]
    lines = []
    for q in range(4):
        line = found[0]
        for j in range(1, 4):
            line = jnp.where(places[j] == q, found[j], line)
        lines.append(line)
    weights_out[...] = jnp.concatenate(lines, axis=0).astype(BF16)


def finish(me, own, rows):
    width = own[0][0].shape[1]
    quarter = rows // 4
    parts = ranges(quarter)
    arrays = [part for packet in own for part in packet]
    any_spec = pl.BlockSpec(memory_space=pl.ANY)
    return pl.pallas_call(
        functools.partial(finish_kernel, rows, parts),
        in_specs=[pl.BlockSpec(memory_space=pltpu.SMEM)] + [any_spec] * len(arrays),
        out_specs=[any_spec, pl.BlockSpec(memory_space=pltpu.VMEM)],
        out_shape=[
            jax.ShapeDtypeStruct((rows, width), BF16),
            jax.ShapeDtypeStruct((4, quarter), BF16),
        ],
        scratch_shapes=[
            pltpu.VMEM((4, TAIL, width), BF16),
            pltpu.SemaphoreType.DMA((len(arrays) + 4,)),
        ],
        compiler_params=pltpu.CompilerParams(vmem_limit_bytes=SMALL_LIMIT),
        name="finish",
    )(me, *arrays)


def per_device(points, block_lists, centroids, dual_weights):
    rows, width = centroids.shape
    quarter = rows // 4
    own_blocks = rows // BLOCK
    position = lax.axis_index("blk")
    groups = lax.axis_size("group")
    member = lax.axis_index("group")
    core, plane = member % 2, member // 2
    me = jnp.stack([core, plane]).astype(jnp.int32)
    target = points.shape[0] * groups / rows
    parts = ranges(quarter)
    whole = [(0, quarter)]
    owner = block_lists // own_blocks
    side = jnp.where(owner == position, 1, jnp.where(owner == position ^ 1, 2, 0))
    near_ids = side * own_blocks + block_lists % own_blocks
    near_ids = near_ids.reshape(-1).astype(jnp.int32)

    def start_packet(c, y):
        first = (c * 2 + y) * quarter
        block = lax.dynamic_slice_in_dim(centroids, first, quarter, 0)
        row = lax.dynamic_slice_in_dim(dual_weights, first, quarter, 0)
        tail = jnp.pad(row[None, :], ((0, TAIL - 1), (0, width - quarter)))
        return jnp.concatenate([block, tail], axis=0)

    def each(move, arrays):
        return [move(a) for a in arrays]

    mine = start_packet(core, plane)
    mine_parts = [mine[a : a + part_rows((a, b), quarter)] for a, b in parts]
    for sweep in range(ITERS):
        near = each(pair_swap, mine_parts)
        far = each(outward, near)
        if sweep == 0:
            beside = start_packet(core, 1 - plane)
            own = [mine, beside, start_packet(1 - core, plane), start_packet(1 - core, 1 - plane)]
        else:
            beside = plane_swap(mine)
            own = [mine, beside, core_swap(mine), core_swap(beside)]
        own = [[packet] for packet in own]
        near_beside = [pair_swap(beside)]
        far_beside = each(plane_swap, far)
        packets = [
            [far, far_beside, each(core_swap, far), each(core_swap, far_beside)],
            own,
            [near, near_beside, each(core_swap, near), each(core_swap, near_beside)],
        ]
        sends, keeps = assign_tiles(points, near_ids, me, packets, rows)
        far_pair, near_pair, own_pair = [(keeps[s], core_swap(sends[s])) for s in (0, 2, 1)]
        far_over = each(plane_swap, add_packets(me, far_pair, [], True, parts))
        near_over = pair_swap(add_packets(me, near_pair, [], True, whole)[0])
        arrived = []
        for part, over in zip(parts, far_over):
            passed = inward(add_packets(me, far_pair, [over], False, [part])[0])
            arrived.append(pair_swap(add_packets(me, near_pair, [passed], False, [part])[0]))
        own_over = plane_swap(add_packets(me, own_pair, [near_over], True, whole)[0])
        last = sweep == ITERS - 1
        renewed = renew(me, mine, *own_pair, own_over, arrived, target, not last)
        mine_parts, mine = renewed[: len(parts)], renewed[-1]
    beside = each(plane_swap, mine_parts)
    own = [mine_parts, beside, each(core_swap, mine_parts), each(core_swap, beside)]
    new_centroids, new_weights = finish(me, own, rows)
    return (new_centroids, new_weights.reshape(rows))


def solution(mesh):
    return jax.shard_map(
        per_device,
        mesh=mesh,
        in_specs=(P(("group", "blk"), None), P(("group", "blk"), None), P("blk", None), P("blk")),
        out_specs=(P("blk", None), P("blk")),
        check_vma=False,
    )
```

time: 282 us -> 217 us (0.77)
  Pallas kernels: 113 us -> 67.2 us
  local copies, waits for them, and re-layouts: 15.9 us -> 5.04 us
  waiting for transfers between devices: 105 us -> 95.1 us
  starting transfers between devices: 42.3 us -> 47.4 us
  other arithmetic: 4.53 us -> 1.32 us
    pallas_call x14 -> x19, Pallas kernels: 113 us -> 67.2 us  [the longest x2 54.9 us: assign_tiles(): pl.pallas_call(functools.partial(tiles_kernel, rows, sizes), grid_spec=pl...]
    ppermute x30 -> x39, waiting for transfers between devices: 59.4 us -> 46.2 us  [swap(): return lax.ppermute(x, 'group', [(i, i ^ bit) for i in range(groups)])]
    unnamed x69 -> x3, local copies, waits for them, and re-layouts: 11.6 us -> 0.59 us
    ppermute x8 -> x20, starting transfers between devices: 23.1 us -> 27.9 us  [the longest x12 13.5 us: pair_swap(): return lax.ppermute(x, 'blk', [(i, i ^ 1) for i in range(count)])]
    ppermute x8 -> x20, waiting for transfers between devices: 46 us -> 48.9 us  [the longest x12 24.8 us: pair_swap(): return lax.ppermute(x, 'blk', [(i, i ^ 1) for i in range(count)])]
    ppermute x30 -> x39, starting transfers between devices: 19.1 us -> 19.5 us  [swap(): return lax.ppermute(x, 'group', [(i, i ^ bit) for i in range(groups)])]
  transfers between devices with their start and end apart: 38 -> 59, of which waited for: 21 -> 26; matrix products, arithmetic and copies ran while one was open for 1% -> 1% of each run, Pallas kernels for 10% -> 4%
where the time goes in v2:
time: 217 us
  waiting for transfers between devices  95.1 us (44%)
  Pallas kernels  67.2 us (31%)
  starting transfers between devices  47.4 us (22%)
  local copies, waits for them, and re-layouts  5.04 us (2%)
    pallas_call x2, Pallas kernels, assign_tiles(): pl.pallas_call(functools.partial(tiles_kernel, rows, sizes), grid_spec=pl...  54.9 us
    ppermute x39, waiting for transfers between devices, swap(): return lax.ppermute(x, 'group', [(i, i ^ bit) for i in range(groups)])  46.2 us
    ppermute x12, waiting for transfers between devices, pair_swap(): return lax.ppermute(x, 'blk', [(i, i ^ 1) for i in range(count)])  24.8 us
    ppermute x39, starting transfers between devices, swap(): return lax.ppermute(x, 'group', [(i, i ^ bit) for i in range(groups)])  19.5 us
    ppermute x4, waiting for transfers between devices, outward(): lax.ppermute(x, 'blk', [(i, (i + 2 - i % 2 * 4) % count) for i in range(c...  16.8 us
    ppermute x12, starting transfers between devices, pair_swap(): return lax.ppermute(x, 'blk', [(i, i ^ 1) for i in range(count)])  13.5 us
    pallas_call x16, Pallas kernels, small_call(): pl.pallas_call(kernel, in_specs=[pl.BlockSpec(memory_space=pltpu.SMEM)] +...  10.5 us
    ppermute x4, starting transfers between devices, inward(): lax.ppermute(x, 'blk', [((i + 2 - i % 2 * 4) % count, i) for i in range(c...  9.47 us
  transfers between devices with their start and end apart: 59, of which 26 were waited for; matrix products, arithmetic and copies ran while one was open for 1% of the time, Pallas kernels for 4%

profile of v2, /device:TPU:0, one launch (start us, length us, event | category | flops | bytes accessed | tf_op | source)
XLA Modules:
  0.0 217.0 jit_solution(7168703845685441816)
XLA Ops:
  1.6 2.4 %constant_dynamic-slice_fusion.1 = (bf16[256,768]{1,0:T(8,128)(2,1)}, bf16[256,768]{1,0:T(8,128)(2,1)S(1)}, bf16[256,768]{1,0:T(8,128)(2,1)S(1)}, bf16[256,768]{1,0:T(8,128)(2,1)}) fusion(bf16[1024,768]{1,0:T(8,128)(2,1)} %param.6, s32[]{:T(128)S(6)} %select_n.55, s32[]{:T(128)S(6)} %select_n.53, s32[]{:T(128)S(6)} %select_n.48, s32[]{:T(128)S(6)} %select_n.54), kind=kLoop, calls=%fused_computation.18 | loop fusion | bytes 3145744 | tf_op jit(solution)/shard_map/dynamic_slice | solution.py:440
  4.0 3.0 %collective-permute-start.2 = (bf16[144,768]{1,0:T(8,128)(2,1)S(1)}, bf16[144,768]{1,0:T(8,128)(2,1)S(1)}, u32[]{:S(2)}, u32[]{:S(2)}) collective-permute-start(bf16[144,768]{1,0:T(8,128)(2,1)S(1)} %slice.8), channel_id=1, source_target_pairs={{0,1},{1,0},{2,3},{3,2},{4,5},{5,4},{6,7},{7,6},{8,9},{9,8},{10,11... | collective-permute-start | bytes 663560 | tf_op jit(solution)/shard_map/ppermute | solution.py:40
  8.1 2.1 collective-permute-start
  10.2 3.1 %collective-permute-done.2.refs_13_ = bf16[144,768]{1,0:T(8,128)(2,1)S(1)} collective-permute-done((bf16[144,768]{1,0:T(8,128)(2,1)S(1)}, bf16[144,768]{1,0:T(8,128)(2,1)S(1)}, u32[]{:S(2)}, u32[]{:S(2)}) %collective-permute-start.2) | collective-permute-done | bytes 221216 | tf_op jit(solution)/shard_map/ppermute | solution.py:40
  13.3 2.1 collective-permute-start.3
  15.4 10.2 %collective-permute-done.refs_12_ = bf16[128,768]{1,0:T(8,128)(2,1)S(1)} collective-permute-done((bf16[128,768]{1,0:T(8,128)(2,1)S(1)}, bf16[128,768]{1,0:T(8,128)(2,1)S(1)}, u32[]{:S(2)}, u32[]{:S(2)}) %collective-permute-start) | collective-permute-done | bytes 196640 | tf_op jit(solution)/shard_map/ppermute | solution.py:40
  25.6 1.8 collective-permute-start.1
  28.0 5.5 %collective-permute-done.1.refs_0_ = bf16[128,768]{1,0:T(8,128)(2,1)S(1)} collective-permute-done((bf16[128,768]{1,0:T(8,128)(2,1)S(1)}, bf16[128,768]{1,0:T(8,128)(2,1)S(1)}, u32[]{:S(2)}, u32[]{:S(2)}) %collective-permute-start.1) | collective-permute-done | bytes 196640 | tf_op jit(solution)/shard_map/ppermute | solution.py:45
  33.5 1.5 collective-permute-start.4
  36.4 3.8 %collective-permute-done.4.refs_2_ = bf16[128,768]{1,0:T(8,128)(2,1)S(1)} collective-permute-done((bf16[128,768]{1,0:T(8,128)(2,1)S(1)}, bf16[128,768]{1,0:T(8,128)(2,1)S(1)}, u32[]{:S(2)}, u32[]{:S(2)}) %collective-permute-start.4) | collective-permute-done | bytes 196640 | tf_op jit(solution)/shard_map/ppermute | solution.py:27
  40.2 3.7 %collective-permute-done.5.refs_3_ = bf16[144,768]{1,0:T(8,128)(2,1)S(1)} collective-permute-done((bf16[144,768]{1,0:T(8,128)(2,1)S(1)}, bf16[144,768]{1,0:T(8,128)(2,1)S(1)}, u32[]{:S(2)}, u32[]{:S(2)}) %collective-permute-start.5) | collective-permute-done | bytes 221216 | tf_op jit(solution)/shard_map/ppermute | solution.py:27
  44.0 1.2 fusion.6
  45.4 27.4 %tiles.2 = (bf16[544,768]{1,0:T(8,128)(2,1)S(1)}, bf16[544,768]{1,0:T(8,128)(2,1)S(1)}, bf16[544,768]{1,0:T(8,128)(2,1)S(1)}, f32[544,768]{1,0:T(8,128)S(1)}, f3...) custom-call(s32[256]{0:T(256)S(1)} %reshape.10.ids_ref, s32[2]{0:T(128)S(1)} %pad_add_fusion.me_ref, ...), custom_call_target="tpu_custom_call" | custom-call | flops 6442450944 | bytes 12582912 | tf_op jit(solution)/shard_map/tiles/pallas_call | solution.py:232
  73.8 1.5 collective-permute-done.15.refs_1_
  77.3 1.6 collective-permute-start.22
  79.4 6.3 %collective-permute-done.22.refs_2_ = bf16[144,768]{1,0:T(8,128)(2,1)S(1)} collective-permute-done((bf16[144,768]{1,0:T(8,128)(2,1)S(1)}, bf16[144,768]{1,0:T(8,128)(2,1)S(1)}, u32[]{:S(2)}, u32[]{:S(2)}) %collective-permute-start.22) | collective-permute-done | bytes 221216 | tf_op jit(solution)/shard_map/ppermute | solution.py:27
  86.3 4.3 %collective-permute-start.23 = (bf16[144,768]{1,0:T(8,128)(2,1)S(1)}, bf16[144,768]{1,0:T(8,128)(2,1)S(1)}, u32[]{:S(2)}, u32[]{:S(2)}) collective-permute-start(bf16[144,768]{1,0:T(8,128)(2,1)S(1)} %add_packets.19), channel_id=1, source_target_pairs={{2,0},{7,1},{4,2},{1,3},{6,4},{3,5},{0,6},{5,7},{10,8},{15,9},{12,... | collective-permute-start | bytes 663560 | tf_op jit(solution)/shard_map/ppermute | solution.py:50
  91.3 1.6 collective-permute-start.17
  95.0 1.4 collective-permute-start.24
  96.4 2.9 %collective-permute-done.20.refs_2_ = bf16[128,768]{1,0:T(8,128)(2,1)S(1)} collective-permute-done((bf16[128,768]{1,0:T(8,128)(2,1)S(1)}, bf16[128,768]{1,0:T(8,128)(2,1)S(1)}, u32[]{:S(2)}, u32[]{:S(2)}) %collective-permute-start.20) | collective-permute-done | bytes 196640 | tf_op jit(solution)/shard_map/ppermute | solution.py:50
  99.9 0.9 collective-permute-start.21
  100.9 4.8 %collective-permute-done.21.refs_0_ = bf16[128,768]{1,0:T(8,128)(2,1)S(1)} collective-permute-done((bf16[128,768]{1,0:T(8,128)(2,1)S(1)}, bf16[128,768]{1,0:T(8,128)(2,1)S(1)}, u32[]{:S(2)}, u32[]{:S(2)}) %collective-permute-start.21) | collective-permute-done | bytes 196640 | tf_op jit(solution)/shard_map/ppermute | solution.py:40
  106.5 1.6 collective-permute-start.35
  108.1 1.3 collective-permute-start.25
  110.1 6.7 %collective-permute-done.35.refs_9_ = bf16[272,768]{1,0:T(8,128)(2,1)S(1)} collective-permute-done((bf16[272,768]{1,0:T(8,128)(2,1)S(1)}, bf16[272,768]{1,0:T(8,128)(2,1)S(1)}, u32[]{:S(2)}, u32[]{:S(2)}) %collective-permute-start.35) | collective-permute-done | bytes 417824 | tf_op jit(solution)/shard_map/ppermute | solution.py:27
  116.9 1.1 collective-permute-start.38
  117.9 1.4 collective-permute-done.27.refs_13_
  119.3 1.0 collective-permute-start.26
  120.3 9.2 %collective-permute-done.28.refs_1_ = bf16[144,768]{1,0:T(8,128)(2,1)S(1)} collective-permute-done((bf16[144,768]{1,0:T(8,128)(2,1)S(1)}, bf16[144,768]{1,0:T(8,128)(2,1)S(1)}, u32[]{:S(2)}, u32[]{:S(2)}) %collective-permute-start.28) | collective-permute-done | bytes 221216 | tf_op jit(solution)/shard_map/ppermute | solution.py:45
  129.8 2.0 collective-permute-done.26.refs_0_
  132.4 1.7 collective-permute-start.29
  134.3 1.1 collective-permute-done.30.refs_3_
  135.5 4.2 %collective-permute-done.29.refs_2_ = bf16[128,768]{1,0:T(8,128)(2,1)S(1)} collective-permute-done((bf16[128,768]{1,0:T(8,128)(2,1)S(1)}, bf16[128,768]{1,0:T(8,128)(2,1)S(1)}, u32[]{:S(2)}, u32[]{:S(2)}) %collective-permute-start.29) | collective-permute-done | bytes 196640 | tf_op jit(solution)/shard_map/ppermute | solution.py:27
  139.7 1.4 collective-permute-done.33.refs_6_
  141.1 27.5 %tiles.3 = (bf16[544,768]{1,0:T(8,128)(2,1)S(1)}, bf16[544,768]{1,0:T(8,128)(2,1)S(1)}, bf16[544,768]{1,0:T(8,128)(2,1)S(1)}, f32[544,768]{1,0:T(8,128)S(1)}, f3...) custom-call(s32[256]{0:T(256)S(1)} %reshape.10.ids_ref, s32[2]{0:T(128)S(1)} %pad_add_fusion.me_ref, ...), custom_call_target="tpu_custom_call" | custom-call | flops 6442450944 | bytes 12582912 | tf_op jit(solution)/shard_map/tiles/pallas_call | solution.py:232
  169.3 1.7 collective-permute-done.43.refs_1_
  171.7 1.0 collective-permute-start.44
  173.3 1.8 collective-permute-start.50
  175.4 6.3 %collective-permute-done.50.refs_2_ = bf16[144,768]{1,0:T(8,128)(2,1)S(1)} collective-permute-done((bf16[144,768]{1,0:T(8,128)(2,1)S(1)}, bf16[144,768]{1,0:T(8,128)(2,1)S(1)}, u32[]{:S(2)}, u32[]{:S(2)}) %collective-permute-start.50) | collective-permute-done | bytes 221216 | tf_op jit(solution)/shard_map/ppermute | solution.py:27
  182.3 4.3 %collective-permute-start.51 = (bf16[144,768]{1,0:T(8,128)(2,1)S(1)}, bf16[144,768]{1,0:T(8,128)(2,1)S(1)}, u32[]{:S(2)}, u32[]{:S(2)}) collective-permute-start(bf16[144,768]{1,0:T(8,128)(2,1)S(1)} %add_packets.26), channel_id=1, source_target_pairs={{2,0},{7,1},{4,2},{1,3},{6,4},{3,5},{0,6},{5,7},{10,8},{15,9},{12,... | collective-permute-start | bytes 663560 | tf_op jit(solution)/shard_map/ppermute | solution.py:50
  187.3 1.8 collective-permute-start.45
  191.9 3.6 %collective-permute-done.48.refs_2_ = bf16[128,768]{1,0:T(8,128)(2,1)S(1)} collective-permute-done((bf16[128,768]{1,0:T(8,128)(2,1)S(1)}, bf16[128,768]{1,0:T(8,128)(2,1)S(1)}, u32[]{:S(2)}, u32[]{:S(2)}) %collective-permute-start.48) | collective-permute-done | bytes 196640 | tf_op jit(solution)/shard_map/ppermute | solution.py:50
  196.5 5.3 %collective-permute-done.49.refs_0_ = bf16[128,768]{1,0:T(8,128)(2,1)S(1)} collective-permute-done((bf16[128,768]{1,0:T(8,128)(2,1)S(1)}, bf16[128,768]{1,0:T(8,128)(2,1)S(1)}, u32[]{:S(2)}, u32[]{:S(2)}) %collective-permute-start.49) | collective-permute-done | bytes 196640 | tf_op jit(solution)/shard_map/ppermute | solution.py:40
  202.6 2.2 collective-permute-start.54
  204.9 6.2 %collective-permute-done.54.refs_3_ = bf16[144,768]{1,0:T(8,128)(2,1)S(1)} collective-permute-done((bf16[144,768]{1,0:T(8,128)(2,1)S(1)}, bf16[144,768]{1,0:T(8,128)(2,1)S(1)}, u32[]{:S(2)}, u32[]{:S(2)}) %collective-permute-start.54) | collective-permute-done | bytes 221216 | tf_op jit(solution)/shard_map/ppermute | solution.py:27
  211.6 1.6 collective-permute-done.53.refs_2_
  213.2 1.4 collective-permute-done.57.refs_6_
  214.6 1.8 finish.1
  (107 shorter events, 23.7 us)
Async XLA Ops:
  4.0 9.3 %collective-permute-start.2 = (bf16[144,768]{1,0:T(8,128)(2,1)S(1)}, bf16[144,768]{1,0:T(8,128)(2,1)S(1)}, u32[]{:S(2)}, u32[]{:S(2)}) collective-permute-start(bf16[144,768]{1,0:T(8,128)(2,1)S(1)} %slice.8), channel_id=1, source_target_pairs={{0,1},{1,0},{2,3},{3,2},{4,5},{5,4},{6,7},{7,6},{8,9},{9,8},{10,11... | collective-permute-start | bytes 663560 | tf_op jit(solution)/shard_map/ppermute | solution.py:40
  7.1 28.0 %collective-permute-start.10 = (bf16[272,768]{1,0:T(8,128)(2,1)S(1)}, bf16[272,768]{1,0:T(8,128)(2,1)S(1)}, u32[]{:S(2)}, u32[]{:S(2)}) collective-permute-start(bf16[272,768]{1,0:T(8,128)(2,1)S(1)} %fusion.5.refs_9_), channel_id=1, source_target_pairs={{0,1},{1,0},{2,3},{3,2},{4,5},{5,4},{6,7},{7,6},{8,9},{9,8},{10,11... | collective-permute-start | bytes 1253384 | tf_op jit(solution)/shard_map/ppermute | solution.py:40
  8.1 17.5 %collective-permute-start = (bf16[128,768]{1,0:T(8,128)(2,1)S(1)}, bf16[128,768]{1,0:T(8,128)(2,1)S(1)}, u32[]{:S(2)}, u32[]{:S(2)}) collective-permute-start(bf16[128,768]{1,0:T(8,128)(2,1)S(1)} %constant_dynamic-slice_fusion), channel_id=1, source_target_pairs={{0,1},{1,0},{2,3},{3,2},{4,5},{5,4},{6,7},{7,6},{8,9},{9,8},{10,11... | collective-permute-start | bytes 589832 | tf_op jit(solution)/shard_map/ppermute | solution.py:40
  13.3 21.7 %collective-permute-start.3 = (bf16[144,768]{1,0:T(8,128)(2,1)S(1)}, bf16[144,768]{1,0:T(8,128)(2,1)S(1)}, u32[]{:S(2)}, u32[]{:S(2)}) collective-permute-start(bf16[144,768]{1,0:T(8,128)(2,1)S(1)} %collective-permute-done.2.refs_13_), channel_id=1, source_target_pairs={{0,2},{1,7},{2,4},{3,1},{4,6},{5,3},{6,0},{7,5},{8,10},{9,15},{10,... | collective-permute-start | bytes 663560 | tf_op jit(solution)/shard_map/ppermute | solution.py:45
  25.6 7.9 %collective-permute-start.1 = (bf16[128,768]{1,0:T(8,128)(2,1)S(1)}, bf16[128,768]{1,0:T(8,128)(2,1)S(1)}, u32[]{:S(2)}, u32[]{:S(2)}) collective-permute-start(bf16[128,768]{1,0:T(8,128)(2,1)S(1)} %collective-permute-done.refs_12_), channel_id=1, source_target_pairs={{0,2},{1,7},{2,4},{3,1},{4,6},{5,3},{6,0},{7,5},{8,10},{9,15},{10,... | collective-permute-start | bytes 589832 | tf_op jit(solution)/shard_map/ppermute | solution.py:45
  27.5 8.4 %collective-permute-start.11 = (bf16[128,768]{1,0:T(8,128)(2,1)S(1)}, bf16[128,768]{1,0:T(8,128)(2,1)S(1)}, u32[]{:S(2)}, u32[]{:S(2)}) collective-permute-start(bf16[128,768]{1,0:T(8,128)(2,1)S(1)} %collective-permute-done.refs_12_), channel_id=1, source_target_pairs={{0,8},{8,0},{16,24},{24,16},{1,9},{9,1},{17,25},{25,17},{2,10},{10... | collective-permute-start | bytes 589832 | tf_op jit(solution)/shard_map/ppermute | solution.py:27
  27.5 8.6 %collective-permute-start.12 = (bf16[144,768]{1,0:T(8,128)(2,1)S(1)}, bf16[144,768]{1,0:T(8,128)(2,1)S(1)}, u32[]{:S(2)}, u32[]{:S(2)}) collective-permute-start(bf16[144,768]{1,0:T(8,128)(2,1)S(1)} %collective-permute-done.2.refs_13_), channel_id=1, source_target_pairs={{0,8},{8,0},{16,24},{24,16},{1,9},{9,1},{17,25},{25,17},{2,10},{10... | collective-permute-start | bytes 663560 | tf_op jit(solution)/shard_map/ppermute | solution.py:27
  33.5 6.7 %collective-permute-start.4 = (bf16[128,768]{1,0:T(8,128)(2,1)S(1)}, bf16[128,768]{1,0:T(8,128)(2,1)S(1)}, u32[]{:S(2)}, u32[]{:S(2)}) collective-permute-start(bf16[128,768]{1,0:T(8,128)(2,1)S(1)} %collective-permute-done.1.refs_0_), channel_id=1, source_target_pairs={{0,16},{8,24},{16,0},{24,8},{1,17},{9,25},{17,1},{25,9},{2,18},{10... | collective-permute-start | bytes 589832 | tf_op jit(solution)/shard_map/ppermute | solution.py:27
  35.0 10.2 %collective-permute-start.13 = (bf16[272,768]{1,0:T(8,128)(2,1)S(1)}, bf16[272,768]{1,0:T(8,128)(2,1)S(1)}, u32[]{:S(2)}, u32[]{:S(2)}) collective-permute-start(bf16[272,768]{1,0:T(8,128)(2,1)S(1)} %collective-permute-done.10.refs_14_), channel_id=1, source_target_pairs={{0,8},{8,0},{16,24},{24,16},{1,9},{9,1},{17,25},{25,17},{2,10},{10... | collective-permute-start | bytes 1253384 | tf_op jit(solution)/shard_map/ppermute | solution.py:27
  35.0 8.9 %collective-permute-start.5 = (bf16[144,768]{1,0:T(8,128)(2,1)S(1)}, bf16[144,768]{1,0:T(8,128)(2,1)S(1)}, u32[]{:S(2)}, u32[]{:S(2)}) collective-permute-start(bf16[144,768]{1,0:T(8,128)(2,1)S(1)} %collective-permute-done.3.refs_1_), channel_id=1, source_target_pairs={{0,16},{8,24},{16,0},{24,8},{1,17},{9,25},{17,1},{25,9},{2,18},{10... | collective-permute-start | bytes 663560 | tf_op jit(solution)/shard_map/ppermute | solution.py:27
  35.8 9.3 %collective-permute-start.6 = (bf16[128,768]{1,0:T(8,128)(2,1)S(1)}, bf16[128,768]{1,0:T(8,128)(2,1)S(1)}, u32[]{:S(2)}, u32[]{:S(2)}) collective-permute-start(bf16[128,768]{1,0:T(8,128)(2,1)S(1)} %collective-permute-done.1.refs_0_), channel_id=1, source_target_pairs={{0,8},{8,0},{16,24},{24,16},{1,9},{9,1},{17,25},{25,17},{2,10},{10... | collective-permute-start | bytes 589832 | tf_op jit(solution)/shard_map/ppermute | solution.py:27
  36.1 9.1 %collective-permute-start.7 = (bf16[144,768]{1,0:T(8,128)(2,1)S(1)}, bf16[144,768]{1,0:T(8,128)(2,1)S(1)}, u32[]{:S(2)}, u32[]{:S(2)}) collective-permute-start(bf16[144,768]{1,0:T(8,128)(2,1)S(1)} %collective-permute-done.3.refs_1_), channel_id=1, source_target_pairs={{0,8},{8,0},{16,24},{24,16},{1,9},{9,1},{17,25},{25,17},{2,10},{10... | collective-permute-start | bytes 663560 | tf_op jit(solution)/shard_map/ppermute | solution.py:27
  40.2 4.9 %collective-permute-start.8 = (bf16[128,768]{1,0:T(8,128)(2,1)S(1)}, bf16[128,768]{1,0:T(8,128)(2,1)S(1)}, u32[]{:S(2)}, u32[]{:S(2)}) collective-permute-start(bf16[128,768]{1,0:T(8,128)(2,1)S(1)} %collective-permute-done.4.refs_2_), channel_id=1, source_target_pairs={{0,8},{8,0},{16,24},{24,16},{1,9},{9,1},{17,25},{25,17},{2,10},{10... | collective-permute-start | bytes 589832 | tf_op jit(solution)/shard_map/ppermute | solution.py:27
  73.4 17.3 %collective-permute-start.14 = (bf16[544,768]{1,0:T(8,128)(2,1)S(1)}, bf16[544,768]{1,0:T(8,128)(2,1)S(1)}, u32[]{:S(2)}, u32[]{:S(2)}) collective-permute-start(bf16[544,768]{1,0:T(8,128)(2,1)S(1)} %get-tuple-element.26), channel_id=1, source_target_pairs={{0,8},{8,0},{16,24},{24,16},{1,9},{9,1},{17,25},{25,17},{2,10},{10... | collective-permute-start | bytes 2506760 | tf_op jit(solution)/shard_map/ppermute | solution.py:27
  75.9 14.8 %collective-permute-start.16 = (bf16[272,768]{1,0:T(8,128)(2,1)S(1)}, bf16[272,768]{1,0:T(8,128)(2,1)S(1)}, u32[]{:S(2)}, u32[]{:S(2)}) collective-permute-start(bf16[272,768]{1,0:T(8,128)(2,1)S(1)} %add_packets.14), channel_id=1, source_target_pairs={{0,1},{1,0},{2,3},{3,2},{4,5},{5,4},{6,7},{7,6},{8,9},{9,8},{10,11... | collective-permute-start | bytes 1253384 | tf_op jit(solution)/shard_map/ppermute | solution.py:40
  77.3 8.3 %collective-permute-start.22 = (bf16[144,768]{1,0:T(8,128)(2,1)S(1)}, bf16[144,768]{1,0:T(8,128)(2,1)S(1)}, u32[]{:S(2)}, u32[]{:S(2)}) collective-permute-start(bf16[144,768]{1,0:T(8,128)(2,1)S(1)} %get-tuple-element.32), channel_id=1, source_target_pairs={{0,16},{8,24},{16,0},{24,8},{1,17},{9,25},{17,1},{25,9},{2,18},{10... | collective-permute-start | bytes 663560 | tf_op jit(solution)/shard_map/ppermute | solution.py:27
  79.0 14.0 %collective-permute-start.19 = (bf16[128,768]{1,0:T(8,128)(2,1)S(1)}, bf16[128,768]{1,0:T(8,128)(2,1)S(1)}, u32[]{:S(2)}, u32[]{:S(2)}) collective-permute-start(bf16[128,768]{1,0:T(8,128)(2,1)S(1)} %get-tuple-element.31), channel_id=1, source_target_pairs={{0,16},{8,24},{16,0},{24,8},{1,17},{9,25},{17,1},{25,9},{2,18},{10... | collective-permute-start | bytes 589832 | tf_op jit(solution)/shard_map/ppermute | solution.py:27
  86.3 8.1 %collective-permute-start.23 = (bf16[144,768]{1,0:T(8,128)(2,1)S(1)}, bf16[144,768]{1,0:T(8,128)(2,1)S(1)}, u32[]{:S(2)}, u32[]{:S(2)}) collective-permute-start(bf16[144,768]{1,0:T(8,128)(2,1)S(1)} %add_packets.19), channel_id=1, source_target_pairs={{2,0},{7,1},{4,2},{1,3},{6,4},{3,5},{0,6},{5,7},{10,8},{15,9},{12,... | collective-permute-start | bytes 663560 | tf_op jit(solution)/shard_map/ppermute | solution.py:50
  91.3 14.3 %collective-permute-start.17 = (bf16[272,768]{1,0:T(8,128)(2,1)S(1)}, bf16[272,768]{1,0:T(8,128)(2,1)S(1)}, u32[]{:S(2)}, u32[]{:S(2)}) collective-permute-start(bf16[272,768]{1,0:T(8,128)(2,1)S(1)} %add_packets.15), channel_id=1, source_target_pairs={{0,16},{8,24},{16,0},{24,8},{1,17},{9,25},{17,1},{25,9},{2,18},{10... | collective-permute-start | bytes 1253384 | tf_op jit(solution)/shard_map/ppermute | solution.py:27
  93.6 5.7 %collective-permute-start.20 = (bf16[128,768]{1,0:T(8,128)(2,1)S(1)}, bf16[128,768]{1,0:T(8,128)(2,1)S(1)}, u32[]{:S(2)}, u32[]{:S(2)}) collective-permute-start(bf16[128,768]{1,0:T(8,128)(2,1)S(1)} %add_packets.17), channel_id=1, source_target_pairs={{2,0},{7,1},{4,2},{1,3},{6,4},{3,5},{0,6},{5,7},{10,8},{15,9},{12,... | collective-permute-start | bytes 589832 | tf_op jit(solution)/shard_map/ppermute | solution.py:50
  95.0 10.6 %collective-permute-start.24 = (bf16[144,768]{1,0:T(8,128)(2,1)S(1)}, bf16[144,768]{1,0:T(8,128)(2,1)S(1)}, u32[]{:S(2)}, u32[]{:S(2)}) collective-permute-start(bf16[144,768]{1,0:T(8,128)(2,1)S(1)} %add_packets.20), channel_id=1, source_target_pairs={{0,1},{1,0},{2,3},{3,2},{4,5},{5,4},{6,7},{7,6},{8,9},{9,8},{10,11... | collective-permute-start | bytes 663560 | tf_op jit(solution)/shard_map/ppermute | solution.py:40
  99.9 5.7 %collective-permute-start.21 = (bf16[128,768]{1,0:T(8,128)(2,1)S(1)}, bf16[128,768]{1,0:T(8,128)(2,1)S(1)}, u32[]{:S(2)}, u32[]{:S(2)}) collective-permute-start(bf16[128,768]{1,0:T(8,128)(2,1)S(1)} %add_packets.18), channel_id=1, source_target_pairs={{0,1},{1,0},{2,3},{3,2},{4,5},{5,4},{6,7},{7,6},{8,9},{9,8},{10,11... | collective-permute-start | bytes 589832 | tf_op jit(solution)/shard_map/ppermute | solution.py:40
  106.5 10.3 %collective-permute-start.35 = (bf16[272,768]{1,0:T(8,128)(2,1)S(1)}, bf16[272,768]{1,0:T(8,128)(2,1)S(1)}, u32[]{:S(2)}, u32[]{:S(2)}) collective-permute-start(bf16[272,768]{1,0:T(8,128)(2,1)S(1)} %get-tuple-element.33.refs_8_.base), channel_id=1, source_target_pairs={{0,16},{8,24},{16,0},{24,8},{1,17},{9,25},{17,1},{25,9},{2,18},{10... | collective-permute-start | bytes 1253384 | tf_op jit(solution)/shard_map/ppermute | solution.py:27
  108.1 9.8 %collective-permute-start.25 = (bf16[128,768]{1,0:T(8,128)(2,1)S(1)}, bf16[128,768]{1,0:T(8,128)(2,1)S(1)}, u32[]{:S(2)}, u32[]{:S(2)}) collective-permute-start(bf16[128,768]{1,0:T(8,128)(2,1)S(1)} %get-tuple-element.34), channel_id=1, source_target_pairs={{0,1},{1,0},{2,3},{3,2},{4,5},{5,4},{6,7},{7,6},{8,9},{9,8},{10,11... | collective-permute-start | bytes 589832 | tf_op jit(solution)/shard_map/ppermute | solution.py:40
  109.4 9.9 %collective-permute-start.27 = (bf16[144,768]{1,0:T(8,128)(2,1)S(1)}, bf16[144,768]{1,0:T(8,128)(2,1)S(1)}, u32[]{:S(2)}, u32[]{:S(2)}) collective-permute-start(bf16[144,768]{1,0:T(8,128)(2,1)S(1)} %get-tuple-element.35), channel_id=1, source_target_pairs={{0,1},{1,0},{2,3},{3,2},{4,5},{5,4},{6,7},{7,6},{8,9},{9,8},{10,11... | collective-permute-start | bytes 663560 | tf_op jit(solution)/shard_map/ppermute | solution.py:40
  110.1 21.7 %collective-permute-start.36 = (bf16[272,768]{1,0:T(8,128)(2,1)S(1)}, bf16[272,768]{1,0:T(8,128)(2,1)S(1)}, u32[]{:S(2)}, u32[]{:S(2)}) collective-permute-start(bf16[272,768]{1,0:T(8,128)(2,1)S(1)} %get-tuple-element.33.refs_8_.base), channel_id=1, source_target_pairs={{0,8},{8,0},{16,24},{24,16},{1,9},{9,1},{17,25},{25,17},{2,10},{10... | collective-permute-start | bytes 1253384 | tf_op jit(solution)/shard_map/ppermute | solution.py:27
  116.9 15.5 %collective-permute-start.38 = (bf16[272,768]{1,0:T(8,128)(2,1)S(1)}, bf16[272,768]{1,0:T(8,128)(2,1)S(1)}, u32[]{:S(2)}, u32[]{:S(2)}) collective-permute-start(bf16[272,768]{1,0:T(8,128)(2,1)S(1)} %collective-permute-done.35.refs_9_), channel_id=1, source_target_pairs={{0,1},{1,0},{2,3},{3,2},{4,5},{5,4},{6,7},{7,6},{8,9},{9,8},{10,11... | collective-permute-start | bytes 1253384 | tf_op jit(solution)/shard_map/ppermute | solution.py:40
  119.3 10.2 %collective-permute-start.28 = (bf16[144,768]{1,0:T(8,128)(2,1)S(1)}, bf16[144,768]{1,0:T(8,128)(2,1)S(1)}, u32[]{:S(2)}, u32[]{:S(2)}) collective-permute-start(bf16[144,768]{1,0:T(8,128)(2,1)S(1)} %collective-permute-done.27.refs_13_), channel_id=1, source_target_pairs={{0,2},{1,7},{2,4},{3,1},{4,6},{5,3},{6,0},{7,5},{8,10},{9,15},{10,... | collective-permute-start | bytes 663560 | tf_op jit(solution)/shard_map/ppermute | solution.py:45
  119.3 12.5 %collective-permute-start.26 = (bf16[128,768]{1,0:T(8,128)(2,1)S(1)}, bf16[128,768]{1,0:T(8,128)(2,1)S(1)}, u32[]{:S(2)}, u32[]{:S(2)}) collective-permute-start(bf16[128,768]{1,0:T(8,128)(2,1)S(1)} %collective-permute-done.25.refs_12_), channel_id=1, source_target_pairs={{0,2},{1,7},{2,4},{3,1},{4,6},{5,3},{6,0},{7,5},{8,10},{9,15},{10,... | collective-permute-start | bytes 589832 | tf_op jit(solution)/shard_map/ppermute | solution.py:45
  120.3 12.1 %collective-permute-start.40 = (bf16[144,768]{1,0:T(8,128)(2,1)S(1)}, bf16[144,768]{1,0:T(8,128)(2,1)S(1)}, u32[]{:S(2)}, u32[]{:S(2)}) collective-permute-start(bf16[144,768]{1,0:T(8,128)(2,1)S(1)} %collective-permute-done.27.refs_13_), channel_id=1, source_target_pairs={{0,8},{8,0},{16,24},{24,16},{1,9},{9,1},{17,25},{25,17},{2,10},{10... | collective-permute-start | bytes 663560 | tf_op jit(solution)/shard_map/ppermute | solution.py:27
  129.5 5.9 %collective-permute-start.30 = (bf16[144,768]{1,0:T(8,128)(2,1)S(1)}, bf16[144,768]{1,0:T(8,128)(2,1)S(1)}, u32[]{:S(2)}, u32[]{:S(2)}) collective-permute-start(bf16[144,768]{1,0:T(8,128)(2,1)S(1)} %collective-permute-done.28.refs_1_), channel_id=1, source_target_pairs={{0,16},{8,24},{16,0},{24,8},{1,17},{9,25},{17,1},{25,9},{2,18},{10... | collective-permute-start | bytes 663560 | tf_op jit(solution)/shard_map/ppermute | solution.py:27
  131.8 9.3 %collective-permute-start.37 = (bf16[272,768]{1,0:T(8,128)(2,1)S(1)}, bf16[272,768]{1,0:T(8,128)(2,1)S(1)}, u32[]{:S(2)}, u32[]{:S(2)}) collective-permute-start(bf16[272,768]{1,0:T(8,128)(2,1)S(1)} %collective-permute-done.35.refs_9_), channel_id=1, source_target_pairs={{0,8},{8,0},{16,24},{24,16},{1,9},{9,1},{17,25},{25,17},{2,10},{10... | collective-permute-start | bytes 1253384 | tf_op jit(solution)/shard_map/ppermute | solution.py:27
  132.3 8.8 %collective-permute-start.41 = (bf16[272,768]{1,0:T(8,128)(2,1)S(1)}, bf16[272,768]{1,0:T(8,128)(2,1)S(1)}, u32[]{:S(2)}, u32[]{:S(2)}) collective-permute-start(bf16[272,768]{1,0:T(8,128)(2,1)S(1)} %collective-permute-done.38.refs_14_), channel_id=1, source_target_pairs={{0,8},{8,0},{16,24},{24,16},{1,9},{9,1},{17,25},{25,17},{2,10},{10... | collective-permute-start | bytes 1253384 | tf_op jit(solution)/shard_map/ppermute | solution.py:27
  132.4 7.3 %collective-permute-start.29 = (bf16[128,768]{1,0:T(8,128)(2,1)S(1)}, bf16[128,768]{1,0:T(8,128)(2,1)S(1)}, u32[]{:S(2)}, u32[]{:S(2)}) collective-permute-start(bf16[128,768]{1,0:T(8,128)(2,1)S(1)} %collective-permute-done.26.refs_0_), channel_id=1, source_target_pairs={{0,16},{8,24},{16,0},{24,8},{1,17},{9,25},{17,1},{25,9},{2,18},{10... | collective-permute-start | bytes 589832 | tf_op jit(solution)/shard_map/ppermute | solution.py:27
  134.1 5.5 %collective-permute-start.32 = (bf16[144,768]{1,0:T(8,128)(2,1)S(1)}, bf16[144,768]{1,0:T(8,128)(2,1)S(1)}, u32[]{:S(2)}, u32[]{:S(2)}) collective-permute-start(bf16[144,768]{1,0:T(8,128)(2,1)S(1)} %collective-permute-done.28.refs_1_), channel_id=1, source_target_pairs={{0,8},{8,0},{16,24},{24,16},{1,9},{9,1},{17,25},{25,17},{2,10},{10... | collective-permute-start | bytes 663560 | tf_op jit(solution)/shard_map/ppermute | solution.py:27
  135.4 5.7 %collective-permute-start.34 = (bf16[144,768]{1,0:T(8,128)(2,1)S(1)}, bf16[144,768]{1,0:T(8,128)(2,1)S(1)}, u32[]{:S(2)}, u32[]{:S(2)}) collective-permute-start(bf16[144,768]{1,0:T(8,128)(2,1)S(1)} %collective-permute-done.30.refs_3_), channel_id=1, source_target_pairs={{0,8},{8,0},{16,24},{24,16},{1,9},{9,1},{17,25},{25,17},{2,10},{10... | collective-permute-start | bytes 663560 | tf_op jit(solution)/shard_map/ppermute | solution.py:27
  169.2 17.5 %collective-permute-start.42 = (bf16[544,768]{1,0:T(8,128)(2,1)S(1)}, bf16[544,768]{1,0:T(8,128)(2,1)S(1)}, u32[]{:S(2)}, u32[]{:S(2)}) collective-permute-start(bf16[544,768]{1,0:T(8,128)(2,1)S(1)} %get-tuple-element.37), channel_id=1, source_target_pairs={{0,8},{8,0},{16,24},{24,16},{1,9},{9,1},{17,25},{25,17},{2,10},{10... | collective-permute-start | bytes 2506760 | tf_op jit(solution)/shard_map/ppermute | solution.py:27
  171.7 15.0 %collective-permute-start.44 = (bf16[272,768]{1,0:T(8,128)(2,1)S(1)}, bf16[272,768]{1,0:T(8,128)(2,1)S(1)}, u32[]{:S(2)}, u32[]{:S(2)}) collective-permute-start(bf16[272,768]{1,0:T(8,128)(2,1)S(1)} %add_packets.21), channel_id=1, source_target_pairs={{0,1},{1,0},{2,3},{3,2},{4,5},{5,4},{6,7},{7,6},{8,9},{9,8},{10,11... | collective-permute-start | bytes 1253384 | tf_op jit(solution)/shard_map/ppermute | solution.py:40
  173.3 8.4 %collective-permute-start.50 = (bf16[144,768]{1,0:T(8,128)(2,1)S(1)}, bf16[144,768]{1,0:T(8,128)(2,1)S(1)}, u32[]{:S(2)}, u32[]{:S(2)}) collective-permute-start(bf16[144,768]{1,0:T(8,128)(2,1)S(1)} %get-tuple-element.43), channel_id=1, source_target_pairs={{0,16},{8,24},{16,0},{24,8},{1,17},{9,25},{17,1},{25,9},{2,18},{10... | collective-permute-start | bytes 663560 | tf_op jit(solution)/shard_map/ppermute | solution.py:27
  175.1 14.0 %collective-permute-start.47 = (bf16[128,768]{1,0:T(8,128)(2,1)S(1)}, bf16[128,768]{1,0:T(8,128)(2,1)S(1)}, u32[]{:S(2)}, u32[]{:S(2)}) collective-permute-start(bf16[128,768]{1,0:T(8,128)(2,1)S(1)} %get-tuple-element.42), channel_id=1, source_target_pairs={{0,16},{8,24},{16,0},{24,8},{1,17},{9,25},{17,1},{25,9},{2,18},{10... | collective-permute-start | bytes 589832 | tf_op jit(solution)/shard_map/ppermute | solution.py:27
  182.3 8.3 %collective-permute-start.51 = (bf16[144,768]{1,0:T(8,128)(2,1)S(1)}, bf16[144,768]{1,0:T(8,128)(2,1)S(1)}, u32[]{:S(2)}, u32[]{:S(2)}) collective-permute-start(bf16[144,768]{1,0:T(8,128)(2,1)S(1)} %add_packets.26), channel_id=1, source_target_pairs={{2,0},{7,1},{4,2},{1,3},{6,4},{3,5},{0,6},{5,7},{10,8},{15,9},{12,... | collective-permute-start | bytes 663560 | tf_op jit(solution)/shard_map/ppermute | solution.py:50
  187.3 14.5 %collective-permute-start.45 = (bf16[272,768]{1,0:T(8,128)(2,1)S(1)}, bf16[272,768]{1,0:T(8,128)(2,1)S(1)}, u32[]{:S(2)}, u32[]{:S(2)}) collective-permute-start(bf16[272,768]{1,0:T(8,128)(2,1)S(1)} %add_packets.22), channel_id=1, source_target_pairs={{0,16},{8,24},{16,0},{24,8},{1,17},{9,25},{17,1},{25,9},{2,18},{10... | collective-permute-start | bytes 1253384 | tf_op jit(solution)/shard_map/ppermute | solution.py:27
  189.7 5.7 %collective-permute-start.48 = (bf16[128,768]{1,0:T(8,128)(2,1)S(1)}, bf16[128,768]{1,0:T(8,128)(2,1)S(1)}, u32[]{:S(2)}, u32[]{:S(2)}) collective-permute-start(bf16[128,768]{1,0:T(8,128)(2,1)S(1)} %add_packets.24), channel_id=1, source_target_pairs={{2,0},{7,1},{4,2},{1,3},{6,4},{3,5},{0,6},{5,7},{10,8},{15,9},{12,... | collective-permute-start | bytes 589832 | tf_op jit(solution)/shard_map/ppermute | solution.py:50
  191.2 10.6 %collective-permute-start.52 = (bf16[144,768]{1,0:T(8,128)(2,1)S(1)}, bf16[144,768]{1,0:T(8,128)(2,1)S(1)}, u32[]{:S(2)}, u32[]{:S(2)}) collective-permute-start(bf16[144,768]{1,0:T(8,128)(2,1)S(1)} %add_packets.27), channel_id=1, source_target_pairs={{0,1},{1,0},{2,3},{3,2},{4,5},{5,4},{6,7},{7,6},{8,9},{9,8},{10,11... | collective-permute-start | bytes 663560 | tf_op jit(solution)/shard_map/ppermute | solution.py:40
  196.1 5.7 %collective-permute-start.49 = (bf16[128,768]{1,0:T(8,128)(2,1)S(1)}, bf16[128,768]{1,0:T(8,128)(2,1)S(1)}, u32[]{:S(2)}, u32[]{:S(2)}) collective-permute-start(bf16[128,768]{1,0:T(8,128)(2,1)S(1)} %add_packets.25), channel_id=1, source_target_pairs={{0,1},{1,0},{2,3},{3,2},{4,5},{5,4},{6,7},{7,6},{8,9},{9,8},{10,11... | collective-permute-start | bytes 589832 | tf_op jit(solution)/shard_map/ppermute | solution.py:40
  202.6 8.4 %collective-permute-start.54 = (bf16[144,768]{1,0:T(8,128)(2,1)S(1)}, bf16[144,768]{1,0:T(8,128)(2,1)S(1)}, u32[]{:S(2)}, u32[]{:S(2)}) collective-permute-start(bf16[144,768]{1,0:T(8,128)(2,1)S(1)} %get-tuple-element.45.refs_1_), channel_id=1, source_target_pairs={{0,16},{8,24},{16,0},{24,8},{1,17},{9,25},{17,1},{25,9},{2,18},{10... | collective-permute-start | bytes 663560 | tf_op jit(solution)/shard_map/ppermute | solution.py:27
  204.8 8.4 %collective-permute-start.53 = (bf16[128,768]{1,0:T(8,128)(2,1)S(1)}, bf16[128,768]{1,0:T(8,128)(2,1)S(1)}, u32[]{:S(2)}, u32[]{:S(2)}) collective-permute-start(bf16[128,768]{1,0:T(8,128)(2,1)S(1)} %get-tuple-element.44.refs_0_), channel_id=1, source_target_pairs={{0,16},{8,24},{16,0},{24,8},{1,17},{9,25},{17,1},{25,9},{2,18},{10... | collective-permute-start | bytes 589832 | tf_op jit(solution)/shard_map/ppermute | solution.py:27
  204.9 8.3 %collective-permute-start.56 = (bf16[144,768]{1,0:T(8,128)(2,1)S(1)}, bf16[144,768]{1,0:T(8,128)(2,1)S(1)}, u32[]{:S(2)}, u32[]{:S(2)}) collective-permute-start(bf16[144,768]{1,0:T(8,128)(2,1)S(1)} %get-tuple-element.45.refs_1_), channel_id=1, source_target_pairs={{0,8},{8,0},{16,24},{24,16},{1,9},{9,1},{17,25},{25,17},{2,10},{10... | collective-permute-start | bytes 663560 | tf_op jit(solution)/shard_map/ppermute | solution.py:27
  (12 other events, 58.5 us)

commit v3 on v2

v3 whole, which is shorter than its diff:
```python
import functools

import jax
import jax.numpy as jnp
from jax import lax
from jax.experimental import pallas as pl
from jax.experimental.pallas import tpu as pltpu
from jax.sharding import PartitionSpec as P

BLOCK = 64
TILE = 128
SLOTS = 4
ITERS = 2
TAIL = 16
STEP_TILES = 8
CHUNKS = 2
prior_mass = 1.0
dual_step = 0.5
F32 = jnp.float32
BF16 = jnp.bfloat16
VMEM_LIMIT = 40 * 1024 * 1024
SMALL_LIMIT = 16 * 1024 * 1024


def swap(x, bit):
    groups = lax.axis_size("group")
    return lax.ppermute(x, "group", [(i, i ^ bit) for i in range(groups)])


def core_swap(x):
    return swap(x, 1)


def plane_swap(x):
    return swap(x, 2)


def pair_swap(x):
    count = lax.axis_size("blk")
    return lax.ppermute(x, "blk", [(i, i ^ 1) for i in range(count)])


def cross_swap(x):
    count = lax.axis_size("blk")
    return lax.ppermute(x, "blk", [(i, (i - 1 + i % 2 * 2) % count) for i in range(count)])


def outward(x):
    count = lax.axis_size("blk")
    return lax.ppermute(x, "blk", [(i, (i + 2 - i % 2 * 4) % count) for i in range(count)])


def inward(x):
    count = lax.axis_size("blk")
    return lax.ppermute(x, "blk", [((i + 2 - i % 2 * 4) % count, i) for i in range(count)])


def ranges(quarter):
    size = quarter // CHUNKS
    return [(k * size, (k + 1) * size) for k in range(CHUNKS)]


def part_rows(part, quarter):
    return part[1] - part[0] + (TAIL if part[1] == quarter else 0)


def eye():
    shape = (TILE, TILE)
    return lax.broadcasted_iota(jnp.int32, shape, 0) == lax.broadcasted_iota(jnp.int32, shape, 1)


def to_column(row):
    return jnp.sum(jnp.where(eye(), row, 0.0), axis=1, keepdims=True)


def to_row(column):
    return jnp.sum(jnp.where(eye(), column, 0.0), axis=0, keepdims=True)


def split_masses(row):
    high = row.astype(BF16)
    rest = row - high.astype(F32)
    mid = rest.astype(BF16)
    low = (rest - mid.astype(F32)).astype(BF16)
    return jnp.concatenate([high, mid, low], axis=1)


def tail_of(row):
    wide = jnp.broadcast_to(row.astype(F32), (TAIL, row.shape[1]))
    first = lax.broadcasted_iota(jnp.int32, wide.shape, 0) == 0
    return jnp.where(first, wide, 0.0)


def mass_of(tail, quarter):
    row = tail[0:1, :].astype(F32)
    return row[:, :quarter] + row[:, quarter : 2 * quarter] + row[:, 2 * quarter : 3 * quarter]


def packet_tail(weights, centroids):
    quarter, width = centroids.shape
    rows = []
    for k in range(quarter // TILE):
        base = centroids[k * TILE : (k + 1) * TILE].astype(F32)
        rows.append(to_row(jnp.sum(base * base, axis=1, keepdims=True)))
    offsets = weights - jnp.concatenate(rows, axis=1) * (16.0 / width)
    terms = split_masses(offsets).astype(F32)
    line = lax.broadcasted_iota(jnp.int32, (TAIL, quarter), 0)
    spread = jnp.zeros((TAIL, quarter), F32)
    for k in range(3):
        spread = jnp.where(line == k, terms[:, k * quarter : (k + 1) * quarter], spread)
    first = jnp.where(line == 0, weights, 0.0)
    rest = jnp.zeros((TAIL, width - 2 * quarter), F32)
    return jnp.concatenate([first, spread, rest], axis=1).astype(BF16)


def mass_row(macc, start, quarter):
    ones = jnp.ones((8, TILE), F32)
    rows = [
        lax.dot_general(
            ones,
            macc[pl.ds(start + k * TILE, TILE), :],
            (((1,), (1,)), ((), ())),
            precision=lax.Precision.HIGHEST,
            preferred_element_type=F32,
        )[0:1]
        for k in range(quarter // TILE)
    ]
    return jnp.concatenate(rows, axis=1)


def hand_over(core, rows, sides, acc, macc, sends, keeps):
    quarter = rows // 4
    packet = quarter + TAIL
    half = rows // 2
    for side in range(sides):
        for y in range(2):
            mine = pl.multiple_of(side * rows + core * half + y * quarter, quarter)
            other = pl.multiple_of(side * rows + (1 - core) * half + y * quarter, quarter)
            body = pl.ds(y * packet, quarter)
            tail = pl.ds(y * packet + quarter, TAIL)
            sends[side][body, :] = acc[pl.ds(other, quarter), :].astype(BF16)
            sends[side][tail, :] = tail_of(split_masses(mass_row(macc, other, quarter))).astype(
                BF16
            )
            row = mass_row(macc, mine, quarter)
            keeps[side][body, :] = acc[pl.ds(mine, quarter), :]
            keeps[side][tail, :] = tail_of(jnp.concatenate([row, row * 0.0, row * 0.0], axis=1))


def clear(acc, macc):
    @pl.loop(0, acc.shape[0] // BLOCK)
    def _(b):
        at = pl.ds(pl.multiple_of(b * BLOCK, BLOCK), BLOCK)
        acc[at, :] = jnp.zeros((BLOCK, acc.shape[1]), F32)
        macc[at, :] = jnp.zeros((BLOCK, TILE), F32)


def points_specs(width):
    rows = STEP_TILES * TILE // 2
    return [
        pl.BlockSpec((rows, width), lambda i, ids, me: (2 * i, 0)),
        pl.BlockSpec((rows, width), lambda i, ids, me: (2 * i + 1, 0)),
    ]


def points_of(low, high, t):
    half = STEP_TILES // 2
    return (low if t < half else high)[pl.ds(t % half * TILE, TILE), :]


def tiles_kernel(rows, sizes, ids_ref, me_ref, points_low, points_high, *refs):
    quarter = rows // 4
    count = sum(len(parts) for side in sizes for parts in side)
    parts_refs = list(refs[:count])
    sends = refs[count : count + 3]
    keeps = refs[count + 3 : count + 6]
    near, tails, offs, acc, macc, in_sem = refs[count + 6 :]
    step = pl.program_id(0)
    core = me_ref[0]
    plane = me_ref[1]

    def arrivals():
        out = []
        left = list(parts_refs)
        for side in range(3):
            for j in range(4):
                c = core if j < 2 else 1 - core
                y = plane if j % 2 == 0 else 1 - plane
                at = side * 4 + c * 2 + y
                first = 0
                for size in sizes[side][j]:
                    ref = left.pop(0)
                    last = min(first + size, quarter)
                    out.append(
                        pltpu.make_async_copy(
                            ref.at[pl.ds(0, last - first)],
                            near.at[
                                pl.ds(pl.multiple_of(at * quarter + first, TILE // 2), last - first)
                            ],
                            in_sem.at[len(out)],
                        )
                    )
                    if first + size > quarter:
                        out.append(
                            pltpu.make_async_copy(
                                ref.at[pl.ds(last - first, TAIL)],
                                tails.at[pl.ds(pl.multiple_of(at * TAIL, TAIL), TAIL)],
                                in_sem.at[len(out)],
                            )
                        )
                    first = last
        return out

    width = near.shape[1]

    @pl.when(step == 0)
    def _():
        copies = arrivals()
        for copy in copies:
            copy.start()
        clear(acc, macc)
        for copy in copies:
            copy.wait()
        ones = jnp.ones((TAIL, TILE), BF16)
        for n in range(12):
            for k in range(quarter // TILE):
                terms = tails[n * TAIL : (n + 1) * TAIL, quarter + k * TILE : quarter + (k + 1) * TILE]
                offs[pl.ds(n * quarter + k * TILE, TILE), :] = lax.dot_general(
                    terms, ones, (((0,), (0,)), ((), ())), preferred_element_type=F32
                )

    def blocks_of(t, slots):
        tile = step * STEP_TILES + t
        return [
            pl.ds(pl.multiple_of(ids_ref[tile * SLOTS + k] * BLOCK, BLOCK), BLOCK) for k in slots
        ]

    members = []
    for t in range(STEP_TILES):
        points = points_of(points_low, points_high, t)
        at = blocks_of(t, (0, 2, 1, 3))
        cand = jnp.concatenate([near[a, :] for a in at], axis=0)
        off = jnp.concatenate([offs[a, :] for a in at], axis=0)
        scores = lax.dot_general(
            cand, points, (((1,), (1,)), ((), ())), preferred_element_type=F32
        )
        scores = scores * (32.0 / width) + off
        top = jnp.max(scores, axis=0, keepdims=True)
        raw = jnp.exp(scores - top)
        total = jnp.sum(raw, axis=0, keepdims=True)
        member = (raw * (1.0 / total)).astype(BF16)
        members.append(member)
    for t in range(STEP_TILES):
        points = points_of(points_low, points_high, t)
        at = blocks_of(t, (0, 2, 1, 3))
        numerator = jnp.dot(members[t], points, preferred_element_type=F32)
        masses = members[t].astype(F32)
        for k in range(SLOTS):
            acc[at[k], :] += numerator[k * BLOCK : (k + 1) * BLOCK]
            macc[at[k], :] += masses[k * BLOCK : (k + 1) * BLOCK]

    @pl.when(step == pl.num_programs(0) - 1)
    def _():
        hand_over(core, rows, 3, acc, macc, sends, keeps)


def assign_tiles(points, ids, me, packets, rows):
    count, width = points.shape
    quarter = rows // 4
    packet = quarter + TAIL
    tiles = count // TILE
    any_spec = pl.BlockSpec(memory_space=pl.ANY)
    vmem_spec = pl.BlockSpec(memory_space=pltpu.VMEM)
    step_rows = STEP_TILES * TILE
    sizes = [[[part.shape[0] for part in parts] for parts in side] for side in packets]
    arrays = [part for side in packets for parts in side for part in parts]
    outs = pl.pallas_call(
        functools.partial(tiles_kernel, rows, sizes),
        grid_spec=pltpu.PrefetchScalarGridSpec(
            num_scalar_prefetch=2,
            grid=(tiles // STEP_TILES,),
            in_specs=points_specs(width) + [any_spec] * len(arrays),
            out_specs=[vmem_spec] * 6,
            scratch_shapes=[
                pltpu.VMEM((3 * rows, width), BF16),
                pltpu.VMEM((12 * TAIL, width), BF16),
                pltpu.VMEM((3 * rows, TILE), F32),
                pltpu.VMEM((3 * rows, width), F32),
                pltpu.VMEM((3 * rows, TILE), F32),
                pltpu.SemaphoreType.DMA((len(arrays) + 12,)),
            ],
        ),
        out_shape=[jax.ShapeDtypeStruct((2 * packet, width), BF16)] * 3
        + [jax.ShapeDtypeStruct((2 * packet, width), F32)] * 3,
        compiler_params=pltpu.CompilerParams(vmem_limit_bytes=VMEM_LIMIT),
        cost_estimate=pl.CostEstimate(
            flops=4 * count * SLOTS * BLOCK * width,
            bytes_accessed=2 * count * width,
            transcendentals=count * SLOTS * BLOCK,
        ),
        name="tiles",
    )(ids, me, points, points, *arrays)
    return outs[:3], outs[3:]


def small_call(kernel, me, arrays, outs, name, after=()):
    vmem_spec = pl.BlockSpec(memory_space=pltpu.VMEM)
    return pl.pallas_call(
        kernel,
        in_specs=[pl.BlockSpec(memory_space=pltpu.SMEM)]
        + [vmem_spec] * len(arrays)
        + [pl.BlockSpec(memory_space=pl.ANY)] * len(after),
        out_specs=[vmem_spec] * len(outs),
        out_shape=outs,
        compiler_params=pltpu.CompilerParams(vmem_limit_bytes=SMALL_LIMIT),
        cost_estimate=pl.CostEstimate(
            flops=sum(a.size for a in arrays),
            bytes_accessed=sum(a.size * a.dtype.itemsize for a in arrays),
            transcendentals=0,
        ),
        name=name,
    )(me, *arrays, *after)


def sum_kernel(quarter, pairs, singles, base, outputs, me_ref, *refs):
    terms = refs[: pairs + singles]
    outs = refs[len(refs) - len(outputs) :]

    def rows_of(start, first, size):
        at = [pl.ds(pl.multiple_of(start + first, TAIL), size)] * pairs
        at += [pl.ds(first - base, size)] * singles
        return [term[a, :] for term, a in zip(terms, at)]

    for (over, first, last), out in zip(outputs, outs):
        start = (1 - me_ref[1] if over else me_ref[1]) * (quarter + TAIL)
        size = last - first
        body = rows_of(start, first, size)
        out[pl.ds(0, size), :] = sum(r.astype(F32) for r in body).astype(BF16)
        if last == quarter:
            mass = sum(mass_of(r, quarter) for r in rows_of(start, quarter, TAIL))
            out[pl.ds(size, TAIL), :] = tail_of(split_masses(mass)).astype(BF16)


def add_packets(me, pairs, singles, outputs, base=0, after=()):
    packet, width = pairs[0].shape[0] // 2, pairs[0].shape[1]
    quarter = packet - TAIL
    return small_call(
        functools.partial(sum_kernel, quarter, len(pairs), len(singles), base, outputs),
        me,
        [*pairs, *singles],
        [jax.ShapeDtypeStruct((part_rows(p[1:], quarter), width), BF16) for p in outputs],
        "add_packets",
        after,
    )


def renew_kernel(quarter, target, ranges_in, ranges_out, me_ref, base, keep, beside, *refs):
    terms = list(zip(ranges_in, refs))
    outs = list(zip(ranges_out, refs[len(terms) :]))
    start = me_ref[1] * (quarter + TAIL)
    mass = sum(
        mass_of(ref[pl.ds(last - first, TAIL), :], quarter)
        for (first, last), ref in terms
        if last == quarter
    )
    for term in (keep, beside):
        tail = term[pl.ds(pl.multiple_of(start + quarter, TAIL), TAIL), :]
        mass = mass + mass_of(tail, quarter)
    weights = base[pl.ds(quarter, TAIL), :].astype(F32)[0:1, :quarter]
    renewed = weights + dual_step * (1.0 - mass / target)
    renewed = renewed.astype(BF16).astype(F32)
    blocks = []
    for row in range(0, quarter, TILE):
        here = pl.ds(pl.multiple_of(start + row, TAIL), TILE)
        total = keep[here, :] + beside[here, :].astype(F32)
        for (first, last), ref in terms:
            if first <= row < last:
                total = total + ref[pl.ds(row - first, TILE), :].astype(F32)
        column = to_column(mass[:, row : row + TILE]) + prior_mass
        total = total + prior_mass * base[pl.ds(row, TILE), :].astype(F32)
        blocks.append((total / column).astype(BF16))
    tail = packet_tail(renewed, jnp.concatenate(blocks, axis=0))
    for (first, last), out in outs:
        for row in range(first, last, TILE):
            out[pl.ds(row - first, TILE), :] = blocks[row // TILE]
        if last == quarter:
            out[pl.ds(last - first, TAIL), :] = tail


def renew(me, base, pair, terms, ranges_in, target, ranges_out):
    packet, width = base.shape
    quarter = packet - TAIL
    return small_call(
        functools.partial(renew_kernel, quarter, target, ranges_in, ranges_out),
        me,
        [base, *pair, *terms],
        [jax.ShapeDtypeStruct((part_rows(p, quarter), width), BF16) for p in ranges_out],
        "renew",
    )


def start_kernel(quarter, which, me_ref, centroids, weights, *refs):
    outs = refs[: len(which)]
    block, sem = refs[len(which) :]
    core, plane = me_ref[0], me_ref[1]
    places = []
    for c, y, first, last in which:
        if (c, y) not in places:
            places.append((c, y))
    copies = []
    for n, (c, y) in enumerate(places):
        place = (core if c else 1 - core) * 2 + (plane if y else 1 - plane)
        at = pl.multiple_of(place * quarter, quarter)
        copies.append(
            pltpu.make_async_copy(centroids.at[pl.ds(at, quarter)], block.at[n], sem.at[n])
        )
        copies[-1].start()
    for n, (c, y) in enumerate(places):
        place = (core if c else 1 - core) * 2 + (plane if y else 1 - plane)
        lines = jnp.zeros((1, quarter), F32)
        for q in range(4):
            lines = jnp.where(place == q, weights[q : q + 1, :].astype(F32), lines)
        copies[n].wait()
        rows = block[n]
        tail = packet_tail(lines, rows)
        for (oc, oy, first, last), out in zip(which, outs):
            if (oc, oy) == (c, y):
                out[pl.ds(0, last - first), :] = rows[first:last]
                if last == quarter:
                    out[pl.ds(last - first, TAIL), :] = tail


def start_packets(me, centroids, weights, which):
    rows, width = centroids.shape
    quarter = rows // 4
    vmem_spec = pl.BlockSpec(memory_space=pltpu.VMEM)
    return pl.pallas_call(
        functools.partial(start_kernel, quarter, which),
        in_specs=[
            pl.BlockSpec(memory_space=pltpu.SMEM),
            pl.BlockSpec(memory_space=pltpu.HBM),
            vmem_spec,
        ],
        out_specs=[vmem_spec] * len(which),
        out_shape=[
            jax.ShapeDtypeStruct((part_rows(p[2:], quarter), width), BF16) for p in which
        ],
        scratch_shapes=[pltpu.VMEM((3, quarter, width), BF16), pltpu.SemaphoreType.DMA((3,))],
        compiler_params=pltpu.CompilerParams(vmem_limit_bytes=SMALL_LIMIT),
        name="start_packets",
    )(me, centroids, weights)


def finish_kernel(rows, parts, me_ref, *refs):
    quarter = rows // 4
    n = 4 * len(parts)
    packets = refs[:n]
    out, weights_out, tails, sem = refs[n:]
    core, plane = me_ref[0], me_ref[1]
    copies = []
    places = []
    for j in range(4):
        c = core if j < 2 else 1 - core
        y = plane if j % 2 == 0 else 1 - plane
        places.append(c * 2 + y)
        for k, (first, last) in enumerate(parts):
            ref = packets[j * len(parts) + k]
            at = pl.multiple_of(places[j] * quarter + first, TILE)
            copies.append(
                pltpu.make_async_copy(
                    ref.at[pl.ds(0, last - first)],
                    out.at[pl.ds(at, last - first)],
                    sem.at[len(copies)],
                )
            )
            if last == quarter:
                copies.append(
                    pltpu.make_async_copy(
                        ref.at[pl.ds(last - first, TAIL)], tails.at[j], sem.at[len(copies)]
                    )
                )
    for copy in copies:
        copy.start()
    for copy in copies:
        copy.wait()
    found = [tails[j][0:1, :quarter].astype(F32) for j in range(4)]
    lines = []
    for q in range(4):
        line = found[0]
        for j in range(1, 4):
            line = jnp.where(places[j] == q, found[j], line)
        lines.append(line)
    weights_out[...] = jnp.concatenate(lines, axis=0).astype(BF16)


def finish(me, own, rows):
    width = own[0][0].shape[1]
    quarter = rows // 4
    parts = ranges(quarter)
    arrays = [part for packet in own for part in packet]
    any_spec = pl.BlockSpec(memory_space=pl.ANY)
    return pl.pallas_call(
        functools.partial(finish_kernel, rows, parts),
        in_specs=[pl.BlockSpec(memory_space=pltpu.SMEM)] + [any_spec] * len(arrays),
        out_specs=[any_spec, pl.BlockSpec(memory_space=pltpu.VMEM)],
        out_shape=[
            jax.ShapeDtypeStruct((rows, width), BF16),
            jax.ShapeDtypeStruct((4, quarter), BF16),
        ],
        scratch_shapes=[
            pltpu.VMEM((4, TAIL, width), BF16),
            pltpu.SemaphoreType.DMA((len(arrays) + 4,)),
        ],
        compiler_params=pltpu.CompilerParams(vmem_limit_bytes=SMALL_LIMIT),
        name="finish",
    )(me, *arrays)


def per_device(points, block_lists, centroids, dual_weights):
    rows, width = centroids.shape
    quarter = rows // 4
    own_blocks = rows // BLOCK
    position = lax.axis_index("blk")
    groups = lax.axis_size("group")
    member = lax.axis_index("group")
    core, plane = member % 2, member // 2
    me = jnp.stack([core, plane]).astype(jnp.int32)
    target = points.shape[0] * groups / rows
    parts = ranges(quarter)
    owner = block_lists // own_blocks
    side = jnp.where(owner == position, 2, jnp.where(owner == position ^ 1, 1, 0))
    near_ids = side * own_blocks + block_lists % own_blocks
    near_ids = near_ids.reshape(-1).astype(jnp.int32)

    def each(move, arrays):
        return [move(a) for a in arrays]

    lines = dual_weights.reshape(4, quarter)
    everything = (0, quarter)
    low, high = parts
    [mine] = start_packets(me, centroids, lines, [(1, 1, *everything)])
    for sweep in range(ITERS):
        far, near = cross_swap(mine), pair_swap(mine)
        if sweep == 0:
            which = [(c, y, *everything) for c, y in ((1, 0), (0, 1), (0, 0))]
            own = [mine, *start_packets(me, centroids, lines, which)]
            beside = own[1]
        else:
            beside = plane_swap(mine)
            own = [mine, beside, core_swap(mine), core_swap(beside)]
        near_beside = pair_swap(beside)
        far_beside = plane_swap(far)
        packets = [
            [far, far_beside, core_swap(far), core_swap(far_beside)],
            [near, near_beside, core_swap(near), core_swap(near_beside)],
            own,
        ]
        packets = [[[packet] for packet in side] for side in packets]
        sends, keeps = assign_tiles(points, near_ids, me, packets, rows)
        far_pair, near_pair, own_pair = [(k, core_swap(a)) for a, k in zip(sends, keeps)]
        far_sums = add_packets(me, far_pair, [], [(True, *high), (True, *low)])
        far_over_high, far_over_low = each(plane_swap, far_sums)
        near_sums = add_packets(
            me, near_pair, [], [(True, *low), (True, *high), (False, *low)]
        )
        near_over_low, near_over_high, near_here_low = each(pair_swap, near_sums)
        [far_high] = add_packets(
            me, far_pair, [far_over_high], [(False, *high)], high[0], [near_over_low]
        )
        far_high = inward(far_high)
        [far_low] = add_packets(
            me, far_pair, [far_over_low], [(False, *low)], low[0], [near_over_high]
        )
        far_here_low = cross_swap(far_low)
        own_low = add_packets(me, own_pair, [near_over_low], [(True, *low)], low[0])
        own_high = add_packets(me, own_pair, [near_over_high], [(True, *high)], high[0])
        own_over_low, own_over_high = each(plane_swap, [*own_low, *own_high])
        [near_high] = add_packets(
            me,
            near_pair,
            [far_high],
            [(False, *high)],
            high[0],
            [near_here_low, *own_low, *own_high],
        )
        near_here_high = pair_swap(near_high)
        last = sweep == ITERS - 1
        mine_parts = renew(
            me,
            mine,
            own_pair,
            [own_over_low, own_over_high, near_here_low, near_here_high, far_here_low],
            [low, high, low, high, low],
            target,
            parts if last else [everything],
        )
        mine = mine_parts[0]
    beside = each(plane_swap, mine_parts)
    own = [mine_parts, beside, each(core_swap, mine_parts), each(core_swap, beside)]
    new_centroids, new_weights = finish(me, own, rows)
    return (new_centroids, new_weights.reshape(rows))


def solution(mesh):
    return jax.shard_map(
        per_device,
        mesh=mesh,
        in_specs=(P(("group", "blk"), None), P(("group", "blk"), None), P("blk", None), P("blk")),
        out_specs=(P("blk", None), P("blk")),
        check_vma=False,
    )
```

time: 217 us -> 199 us (0.917)
  waiting for transfers between devices: 95.1 us -> 88 us
  starting transfers between devices: 47.4 us -> 43.1 us
  Pallas kernels: 67.2 us -> 64.1 us
    ppermute x12, waiting for transfers between devices: 24.8 us -> 48.9 us  [pair_swap(): return lax.ppermute(x, 'blk', [(i, i ^ 1) for i in range(count)])]
    ppermute x39 -> x33, waiting for transfers between devices: 46.2 us -> 24.4 us  [swap(): return lax.ppermute(x, 'group', [(i, i ^ bit) for i in range(groups)])]
    ppermute x4, starting transfers between devices: 4.92 us -> 14.7 us  [cross_swap(): lax.ppermute(x, 'blk', [(i, (i - 1 + i % 2 * 2) % count) for i in range(c...]
    ppermute x4 -> x2, waiting for transfers between devices: 7.37 us -> 0.01 us  [inward(): lax.ppermute(x, 'blk', [((i + 2 - i % 2 * 4) % count, i) for i in range(c...]
    ppermute x12, starting transfers between devices: 13.5 us -> 7.23 us  [pair_swap(): return lax.ppermute(x, 'blk', [(i, i ^ 1) for i in range(count)])]
    pallas_call x2, Pallas kernels: 54.9 us -> 48.7 us  [assign_tiles(): pl.pallas_call(functools.partial(tiles_kernel, rows, sizes), grid_spec=pl...]
    ppermute x4 -> x2, starting transfers between devices: 9.47 us -> 3.58 us  [inward(): lax.ppermute(x, 'blk', [((i + 2 - i % 2 * 4) % count, i) for i in range(c...]
    dynamic_slice x2 -> x0, local copies, waits for them, and re-layouts: 3.28 us -> none  [the longest x1 2.36 us: start_packet(): block = lax.dynamic_slice_in_dim(centroids, first, quarter, 0)]
  transfers between devices with their start and end apart: 59 -> 51, of which waited for: 26 -> 27; matrix products, arithmetic and copies ran while one was open for 1% -> 0% of each run, Pallas kernels for 4% -> 5%
where the time goes in v3:
time: 199 us
  waiting for transfers between devices  88 us (44%)
  Pallas kernels  64.1 us (32%)
  starting transfers between devices  43.1 us (22%)
  local copies, waits for them, and re-layouts  2.89 us (1%)
    ppermute x12, waiting for transfers between devices, pair_swap(): return lax.ppermute(x, 'blk', [(i, i ^ 1) for i in range(count)])  48.9 us
    pallas_call x2, Pallas kernels, assign_tiles(): pl.pallas_call(functools.partial(tiles_kernel, rows, sizes), grid_spec=pl...  48.7 us
    ppermute x33, waiting for transfers between devices, swap(): return lax.ppermute(x, 'group', [(i, i ^ bit) for i in range(groups)])  24.4 us
    ppermute x33, starting transfers between devices, swap(): return lax.ppermute(x, 'group', [(i, i ^ bit) for i in range(groups)])  17.6 us
    ppermute x4, starting transfers between devices, cross_swap(): lax.ppermute(x, 'blk', [(i, (i - 1 + i % 2 * 2) % count) for i in range(c...  14.7 us
    ppermute x4, waiting for transfers between devices, cross_swap(): lax.ppermute(x, 'blk', [(i, (i - 1 + i % 2 * 2) % count) for i in range(c...  14.7 us
    pallas_call x16, Pallas kernels, small_call(): pl.pallas_call(kernel, in_specs=[pl.BlockSpec(memory_space=pltpu.SMEM)] +...  10.9 us
    ppermute x12, starting transfers between devices, pair_swap(): return lax.ppermute(x, 'blk', [(i, i ^ 1) for i in range(count)])  7.23 us
  transfers between devices with their start and end apart: 51, of which 27 were waited for; matrix products, arithmetic and copies ran while one was open for 0% of the time, Pallas kernels for 5%

profile of v3, /device:TPU:0, one launch (start us, length us, event | category | flops | bytes accessed | tf_op | source)
XLA Modules:
  0.0 199.0 jit_solution(13649965038351937466)
XLA Ops:
  1.4 1.4 copy-done
  2.8 1.0 start_packets.2.refs_8_.base
  3.8 6.0 %collective-permute-start = (bf16[272,768]{1,0:T(8,128)(2,1)S(1)}, bf16[272,768]{1,0:T(8,128)(2,1)S(1)}, u32[]{:S(2)}, u32[]{:S(2)}) collective-permute-start(bf16[272,768]{1,0:T(8,128)(2,1)S(1)} %start_packets.2.refs_8_.base), channel_id=1, source_target_pairs={{0,7},{1,2},{2,1},{3,4},{4,3},{5,6},{6,5},{7,0},{8,15},{9,10},{10,... | collective-permute-start | bytes 1253384 | tf_op jit(solution)/shard_map/ppermute | solution.py:45
  9.8 1.7 start_packets.3
  11.6 2.1 %collective-permute-start.5 = (bf16[272,768]{1,0:T(8,128)(2,1)S(1)}, bf16[272,768]{1,0:T(8,128)(2,1)S(1)}, u32[]{:S(2)}, u32[]{:S(2)}) collective-permute-start(bf16[272,768]{1,0:T(8,128)(2,1)S(1)} %get-tuple-element.31.refs_9_), channel_id=1, source_target_pairs={{0,1},{1,0},{2,3},{3,2},{4,5},{5,4},{6,7},{7,6},{8,9},{9,8},{10,11... | collective-permute-start | bytes 1253384 | tf_op jit(solution)/shard_map/ppermute | solution.py:40
  13.7 5.9 %collective-permute-done.refs_0_ = bf16[272,768]{1,0:T(8,128)(2,1)S(1)} collective-permute-done((bf16[272,768]{1,0:T(8,128)(2,1)S(1)}, bf16[272,768]{1,0:T(8,128)(2,1)S(1)}, u32[]{:S(2)}, u32[]{:S(2)}) %collective-permute-start) | collective-permute-done | bytes 417824 | tf_op jit(solution)/shard_map/ppermute | solution.py:45
  19.6 1.5 collective-permute-start.1
  21.1 7.4 %collective-permute-done.4.refs_4_ = bf16[272,768]{1,0:T(8,128)(2,1)S(1)} collective-permute-done((bf16[272,768]{1,0:T(8,128)(2,1)S(1)}, bf16[272,768]{1,0:T(8,128)(2,1)S(1)}, u32[]{:S(2)}, u32[]{:S(2)}) %collective-permute-start.4) | collective-permute-done | bytes 417824 | tf_op jit(solution)/shard_map/ppermute | solution.py:40
  28.5 8.9 %collective-permute-done.5.refs_5_ = bf16[272,768]{1,0:T(8,128)(2,1)S(1)} collective-permute-done((bf16[272,768]{1,0:T(8,128)(2,1)S(1)}, bf16[272,768]{1,0:T(8,128)(2,1)S(1)}, u32[]{:S(2)}, u32[]{:S(2)}) %collective-permute-start.5) | collective-permute-done | bytes 417824 | tf_op jit(solution)/shard_map/ppermute | solution.py:40
  38.1 1.1 collective-permute-done.7.refs_7_
  39.9 23.8 %tiles.2 = (bf16[544,768]{1,0:T(8,128)(2,1)S(1)}, bf16[544,768]{1,0:T(8,128)(2,1)S(1)}, bf16[544,768]{1,0:T(8,128)(2,1)S(1)}, f32[544,768]{1,0:T(8,128)S(1)}, f3...) custom-call(s32[256]{0:T(256)S(1)} %reshape.14.ids_ref, s32[2]{0:T(128)S(1)} %pad_add_fusion.me_ref, ...), custom_call_target="tpu_custom_call" | custom-call | flops 6442450944 | bytes 12582912 | tf_op jit(solution)/shard_map/tiles/pallas_call | solution.py:277
  64.4 1.7 collective-permute-done.15.refs_1_
  66.8 1.6 collective-permute-start.16
  69.1 2.0 %collective-permute-start.12 = (bf16[144,768]{1,0:T(8,128)(2,1)S(1)}, bf16[144,768]{1,0:T(8,128)(2,1)S(1)}, u32[]{:S(2)}, u32[]{:S(2)}) collective-permute-start(bf16[144,768]{1,0:T(8,128)(2,1)S(1)} %get-tuple-element.39), channel_id=1, source_target_pairs={{0,1},{1,0},{2,3},{3,2},{4,5},{5,4},{6,7},{7,6},{8,9},{9,8},{10,11... | collective-permute-start | bytes 663560 | tf_op jit(solution)/shard_map/ppermute | solution.py:40
  71.1 5.8 %collective-permute-done.10.refs_2_.refs_3_ = bf16[128,768]{1,0:T(8,128)(2,1)S(1)} collective-permute-done((bf16[128,768]{1,0:T(8,128)(2,1)S(1)}, bf16[128,768]{1,0:T(8,128)(2,1)S(1)}, u32[]{:S(2)}, u32[]{:S(2)}) %collective-permute-start.10) | collective-permute-done | bytes 196640 | tf_op jit(solution)/shard_map/ppermute | solution.py:40
  77.5 1.9 collective-permute-start.17
  82.8 2.3 %collective-permute-done.14.refs_3_.refs_2_ = bf16[128,768]{1,0:T(8,128)(2,1)S(1)} collective-permute-done((bf16[128,768]{1,0:T(8,128)(2,1)S(1)}, bf16[128,768]{1,0:T(8,128)(2,1)S(1)}, u32[]{:S(2)}, u32[]{:S(2)}) %collective-permute-start.14) | collective-permute-done | bytes 196640 | tf_op jit(solution)/shard_map/ppermute | solution.py:40
  86.2 0.9 collective-permute-start.11
  87.9 2.7 %collective-permute-start.20 = (bf16[128,768]{1,0:T(8,128)(2,1)S(1)}, bf16[128,768]{1,0:T(8,128)(2,1)S(1)}, u32[]{:S(2)}, u32[]{:S(2)}) collective-permute-start(bf16[128,768]{1,0:T(8,128)(2,1)S(1)} %add_packets.20), channel_id=1, source_target_pairs={{0,7},{1,2},{2,1},{3,4},{4,3},{5,6},{6,5},{7,0},{8,15},{9,10},{10,... | collective-permute-start | bytes 589832 | tf_op jit(solution)/shard_map/ppermute | solution.py:45
  90.5 3.3 %collective-permute-done.11.refs_0_ = bf16[128,768]{1,0:T(8,128)(2,1)S(1)} collective-permute-done((bf16[128,768]{1,0:T(8,128)(2,1)S(1)}, bf16[128,768]{1,0:T(8,128)(2,1)S(1)}, u32[]{:S(2)}, u32[]{:S(2)}) %collective-permute-start.11) | collective-permute-done | bytes 196640 | tf_op jit(solution)/shard_map/ppermute | solution.py:27
  93.9 2.4 %collective-permute-done.20.refs_4_ = bf16[128,768]{1,0:T(8,128)(2,1)S(1)} collective-permute-done((bf16[128,768]{1,0:T(8,128)(2,1)S(1)}, bf16[128,768]{1,0:T(8,128)(2,1)S(1)}, u32[]{:S(2)}, u32[]{:S(2)}) %collective-permute-start.20) | collective-permute-done | bytes 196640 | tf_op jit(solution)/shard_map/ppermute | solution.py:45
  96.3 1.0 renew.2.refs_8_.base
  97.3 1.0 collective-permute-start.26
  98.3 3.2 %collective-permute-start.21 = (bf16[272,768]{1,0:T(8,128)(2,1)S(1)}, bf16[272,768]{1,0:T(8,128)(2,1)S(1)}, u32[]{:S(2)}, u32[]{:S(2)}) collective-permute-start(bf16[272,768]{1,0:T(8,128)(2,1)S(1)} %renew.2.refs_8_.base), channel_id=1, source_target_pairs={{0,7},{1,2},{2,1},{3,4},{4,3},{5,6},{6,5},{7,0},{8,15},{9,10},{10,... | collective-permute-start | bytes 1253384 | tf_op jit(solution)/shard_map/ppermute | solution.py:45
  101.5 3.9 %collective-permute-done.26.refs_9_ = bf16[272,768]{1,0:T(8,128)(2,1)S(1)} collective-permute-done((bf16[272,768]{1,0:T(8,128)(2,1)S(1)}, bf16[272,768]{1,0:T(8,128)(2,1)S(1)}, u32[]{:S(2)}, u32[]{:S(2)}) %collective-permute-start.26) | collective-permute-done | bytes 417824 | tf_op jit(solution)/shard_map/ppermute | solution.py:27
  105.4 3.7 %collective-permute-done.21.refs_0_ = bf16[272,768]{1,0:T(8,128)(2,1)S(1)} collective-permute-done((bf16[272,768]{1,0:T(8,128)(2,1)S(1)}, bf16[272,768]{1,0:T(8,128)(2,1)S(1)}, u32[]{:S(2)}, u32[]{:S(2)}) %collective-permute-start.21) | collective-permute-done | bytes 417824 | tf_op jit(solution)/shard_map/ppermute | solution.py:45
  109.2 1.0 collective-permute-start.22
  110.7 7.3 %collective-permute-done.25.refs_4_ = bf16[272,768]{1,0:T(8,128)(2,1)S(1)} collective-permute-done((bf16[272,768]{1,0:T(8,128)(2,1)S(1)}, bf16[272,768]{1,0:T(8,128)(2,1)S(1)}, u32[]{:S(2)}, u32[]{:S(2)}) %collective-permute-start.25) | collective-permute-done | bytes 417824 | tf_op jit(solution)/shard_map/ppermute | solution.py:40
  118.1 8.9 %collective-permute-done.27.refs_5_ = bf16[272,768]{1,0:T(8,128)(2,1)S(1)} collective-permute-done((bf16[272,768]{1,0:T(8,128)(2,1)S(1)}, bf16[272,768]{1,0:T(8,128)(2,1)S(1)}, u32[]{:S(2)}, u32[]{:S(2)}) %collective-permute-start.27) | collective-permute-done | bytes 417824 | tf_op jit(solution)/shard_map/ppermute | solution.py:40
  127.5 1.2 collective-permute-done.29.refs_7_
  129.3 24.9 %tiles.3 = (bf16[544,768]{1,0:T(8,128)(2,1)S(1)}, bf16[544,768]{1,0:T(8,128)(2,1)S(1)}, bf16[544,768]{1,0:T(8,128)(2,1)S(1)}, f32[544,768]{1,0:T(8,128)S(1)}, f3...) custom-call(s32[256]{0:T(256)S(1)} %reshape.14.ids_ref, s32[2]{0:T(128)S(1)} %pad_add_fusion.me_ref, ...), custom_call_target="tpu_custom_call" | custom-call | flops 6442450944 | bytes 12582912 | tf_op jit(solution)/shard_map/tiles/pallas_call | solution.py:277
  154.9 1.7 collective-permute-done.39.refs_1_
  158.8 2.0 %collective-permute-start.36 = (bf16[144,768]{1,0:T(8,128)(2,1)S(1)}, bf16[144,768]{1,0:T(8,128)(2,1)S(1)}, u32[]{:S(2)}, u32[]{:S(2)}) collective-permute-start(bf16[144,768]{1,0:T(8,128)(2,1)S(1)} %get-tuple-element.50), channel_id=1, source_target_pairs={{0,1},{1,0},{2,3},{3,2},{4,5},{5,4},{6,7},{7,6},{8,9},{9,8},{10,11... | collective-permute-start | bytes 663560 | tf_op jit(solution)/shard_map/ppermute | solution.py:40
  160.8 5.7 %collective-permute-done.34.refs_2_.refs_3_ = bf16[128,768]{1,0:T(8,128)(2,1)S(1)} collective-permute-done((bf16[128,768]{1,0:T(8,128)(2,1)S(1)}, bf16[128,768]{1,0:T(8,128)(2,1)S(1)}, u32[]{:S(2)}, u32[]{:S(2)}) %collective-permute-start.34) | collective-permute-done | bytes 196640 | tf_op jit(solution)/shard_map/ppermute | solution.py:40
  167.2 1.6 collective-permute-start.41
  168.8 1.0 collective-permute-start.43
  171.4 1.5 collective-permute-start.37
  173.0 1.5 collective-permute-done.38.refs_3_.refs_2_
  175.7 1.3 collective-permute-start.35
  177.6 2.8 %collective-permute-start.44 = (bf16[128,768]{1,0:T(8,128)(2,1)S(1)}, bf16[128,768]{1,0:T(8,128)(2,1)S(1)}, u32[]{:S(2)}, u32[]{:S(2)}) collective-permute-start(bf16[128,768]{1,0:T(8,128)(2,1)S(1)} %add_packets.27), channel_id=1, source_target_pairs={{0,7},{1,2},{2,1},{3,4},{4,3},{5,6},{6,5},{7,0},{8,15},{9,10},{10,... | collective-permute-start | bytes 589832 | tf_op jit(solution)/shard_map/ppermute | solution.py:45
  180.4 3.0 %collective-permute-done.35.refs_0_ = bf16[128,768]{1,0:T(8,128)(2,1)S(1)} collective-permute-done((bf16[128,768]{1,0:T(8,128)(2,1)S(1)}, bf16[128,768]{1,0:T(8,128)(2,1)S(1)}, u32[]{:S(2)}, u32[]{:S(2)}) %collective-permute-start.35) | collective-permute-done | bytes 196640 | tf_op jit(solution)/shard_map/ppermute | solution.py:27
  183.4 2.6 %collective-permute-done.44.refs_4_ = bf16[128,768]{1,0:T(8,128)(2,1)S(1)} collective-permute-done((bf16[128,768]{1,0:T(8,128)(2,1)S(1)}, bf16[128,768]{1,0:T(8,128)(2,1)S(1)}, u32[]{:S(2)}, u32[]{:S(2)}) %collective-permute-start.44) | collective-permute-done | bytes 196640 | tf_op jit(solution)/shard_map/ppermute | solution.py:45
  186.0 1.0 renew.3
  187.9 1.3 collective-permute-start.45
  189.1 4.0 %collective-permute-done.46.refs_3_ = bf16[144,768]{1,0:T(8,128)(2,1)S(1)} collective-permute-done((bf16[144,768]{1,0:T(8,128)(2,1)S(1)}, bf16[144,768]{1,0:T(8,128)(2,1)S(1)}, u32[]{:S(2)}, u32[]{:S(2)}) %collective-permute-start.46) | collective-permute-done | bytes 221216 | tf_op jit(solution)/shard_map/ppermute | solution.py:27
  193.6 1.6 collective-permute-done.45.refs_2_
  195.2 1.4 collective-permute-done.49.refs_6_
  196.6 1.8 finish.1
  (85 shorter events, 20.6 us)
Async XLA Ops:
  3.8 15.8 %collective-permute-start = (bf16[272,768]{1,0:T(8,128)(2,1)S(1)}, bf16[272,768]{1,0:T(8,128)(2,1)S(1)}, u32[]{:S(2)}, u32[]{:S(2)}) collective-permute-start(bf16[272,768]{1,0:T(8,128)(2,1)S(1)} %start_packets.2.refs_8_.base), channel_id=1, source_target_pairs={{0,7},{1,2},{2,1},{3,4},{4,3},{5,6},{6,5},{7,0},{8,15},{9,10},{10,... | collective-permute-start | bytes 1253384 | tf_op jit(solution)/shard_map/ppermute | solution.py:45
  9.8 18.7 %collective-permute-start.4 = (bf16[272,768]{1,0:T(8,128)(2,1)S(1)}, bf16[272,768]{1,0:T(8,128)(2,1)S(1)}, u32[]{:S(2)}, u32[]{:S(2)}) collective-permute-start(bf16[272,768]{1,0:T(8,128)(2,1)S(1)} %start_packets.2.refs_8_.base), channel_id=1, source_target_pairs={{0,1},{1,0},{2,3},{3,2},{4,5},{5,4},{6,7},{7,6},{8,9},{9,8},{10,11... | collective-permute-start | bytes 1253384 | tf_op jit(solution)/shard_map/ppermute | solution.py:40
  11.6 25.8 %collective-permute-start.5 = (bf16[272,768]{1,0:T(8,128)(2,1)S(1)}, bf16[272,768]{1,0:T(8,128)(2,1)S(1)}, u32[]{:S(2)}, u32[]{:S(2)}) collective-permute-start(bf16[272,768]{1,0:T(8,128)(2,1)S(1)} %get-tuple-element.31.refs_9_), channel_id=1, source_target_pairs={{0,1},{1,0},{2,3},{3,2},{4,5},{5,4},{6,7},{7,6},{8,9},{9,8},{10,11... | collective-permute-start | bytes 1253384 | tf_op jit(solution)/shard_map/ppermute | solution.py:40
  19.6 17.8 %collective-permute-start.1 = (bf16[272,768]{1,0:T(8,128)(2,1)S(1)}, bf16[272,768]{1,0:T(8,128)(2,1)S(1)}, u32[]{:S(2)}, u32[]{:S(2)}) collective-permute-start(bf16[272,768]{1,0:T(8,128)(2,1)S(1)} %collective-permute-done.refs_0_), channel_id=1, source_target_pairs={{0,16},{8,24},{16,0},{24,8},{1,17},{9,25},{17,1},{25,9},{2,18},{10... | collective-permute-start | bytes 1253384 | tf_op jit(solution)/shard_map/ppermute | solution.py:27
  21.1 17.0 %collective-permute-start.2 = (bf16[272,768]{1,0:T(8,128)(2,1)S(1)}, bf16[272,768]{1,0:T(8,128)(2,1)}, u32[]{:S(2)}, u32[]{:S(2)}) collective-permute-start(bf16[272,768]{1,0:T(8,128)(2,1)S(1)} %collective-permute-done.refs_0_), channel_id=1, source_target_pairs={{0,8},{8,0},{16,24},{24,16},{1,9},{9,1},{17,25},{25,17},{2,10},{10... | collective-permute-start | bytes 1253384 | tf_op jit(solution)/shard_map/ppermute | solution.py:27
  28.5 9.6 %collective-permute-start.6 = (bf16[272,768]{1,0:T(8,128)(2,1)S(1)}, bf16[272,768]{1,0:T(8,128)(2,1)}, u32[]{:S(2)}, u32[]{:S(2)}) collective-permute-start(bf16[272,768]{1,0:T(8,128)(2,1)S(1)} %collective-permute-done.4.refs_4_), channel_id=1, source_target_pairs={{0,8},{8,0},{16,24},{24,16},{1,9},{9,1},{17,25},{25,17},{2,10},{10... | collective-permute-start | bytes 1253384 | tf_op jit(solution)/shard_map/ppermute | solution.py:27
  37.4 2.5 %collective-permute-start.3 = (bf16[272,768]{1,0:T(8,128)(2,1)S(1)}, bf16[272,768]{1,0:T(8,128)(2,1)}, u32[]{:S(2)}, u32[]{:S(2)}) collective-permute-start(bf16[272,768]{1,0:T(8,128)(2,1)S(1)} %collective-permute-done.1.refs_1_), channel_id=1, source_target_pairs={{0,8},{8,0},{16,24},{24,16},{1,9},{9,1},{17,25},{25,17},{2,10},{10... | collective-permute-start | bytes 1253384 | tf_op jit(solution)/shard_map/ppermute | solution.py:27
  63.7 2.4 %collective-permute-start.15 = (bf16[544,768]{1,0:T(8,128)(2,1)S(1)}, bf16[544,768]{1,0:T(8,128)(2,1)S(1)}, u32[]{:S(2)}, u32[]{:S(2)}) collective-permute-start(bf16[544,768]{1,0:T(8,128)(2,1)S(1)} %get-tuple-element.42), channel_id=1, source_target_pairs={{0,8},{8,0},{16,24},{24,16},{1,9},{9,1},{17,25},{25,17},{2,10},{10... | collective-permute-start | bytes 2506760 | tf_op jit(solution)/shard_map/ppermute | solution.py:27
  63.9 4.4 %collective-permute-start.9 = (bf16[544,768]{1,0:T(8,128)(2,1)S(1)}, bf16[544,768]{1,0:T(8,128)(2,1)S(1)}, u32[]{:S(2)}, u32[]{:S(2)}) collective-permute-start(bf16[544,768]{1,0:T(8,128)(2,1)S(1)} %get-tuple-element.37), channel_id=1, source_target_pairs={{0,8},{8,0},{16,24},{24,16},{1,9},{9,1},{17,25},{25,17},{2,10},{10... | collective-permute-start | bytes 2506760 | tf_op jit(solution)/shard_map/ppermute | solution.py:27
  64.3 15.7 %collective-permute-start.8 = (bf16[544,768]{1,0:T(8,128)(2,1)S(1)}, bf16[544,768]{1,0:T(8,128)(2,1)S(1)}, u32[]{:S(2)}, u32[]{:S(2)}) collective-permute-start(bf16[544,768]{1,0:T(8,128)(2,1)S(1)} %get-tuple-element.35), channel_id=1, source_target_pairs={{0,8},{8,0},{16,24},{24,16},{1,9},{9,1},{17,25},{25,17},{2,10},{10... | collective-permute-start | bytes 2506760 | tf_op jit(solution)/shard_map/ppermute | solution.py:27
  66.8 10.1 %collective-permute-start.16 = (bf16[144,768]{1,0:T(8,128)(2,1)S(1)}, bf16[144,768]{1,0:T(8,128)(2,1)S(1)}, u32[]{:S(2)}, u32[]{:S(2)}) collective-permute-start(bf16[144,768]{1,0:T(8,128)(2,1)S(1)} %get-tuple-element.43), channel_id=1, source_target_pairs={{0,16},{8,24},{16,0},{24,8},{1,17},{9,25},{17,1},{25,9},{2,18},{10... | collective-permute-start | bytes 663560 | tf_op jit(solution)/shard_map/ppermute | solution.py:27
  69.1 7.9 %collective-permute-start.10 = (bf16[128,768]{1,0:T(8,128)(2,1)S(1)}, bf16[128,768]{1,0:T(8,128)(2,1)S(1)}, u32[]{:S(2)}, u32[]{:S(2)}) collective-permute-start(bf16[128,768]{1,0:T(8,128)(2,1)S(1)} %get-tuple-element.38), channel_id=1, source_target_pairs={{0,1},{1,0},{2,3},{3,2},{4,5},{5,4},{6,7},{7,6},{8,9},{9,8},{10,11... | collective-permute-start | bytes 589832 | tf_op jit(solution)/shard_map/ppermute | solution.py:40
  69.1 12.2 %collective-permute-start.12 = (bf16[144,768]{1,0:T(8,128)(2,1)S(1)}, bf16[144,768]{1,0:T(8,128)(2,1)S(1)}, u32[]{:S(2)}, u32[]{:S(2)}) collective-permute-start(bf16[144,768]{1,0:T(8,128)(2,1)S(1)} %get-tuple-element.39), channel_id=1, source_target_pairs={{0,1},{1,0},{2,3},{3,2},{4,5},{5,4},{6,7},{7,6},{8,9},{9,8},{10,11... | collective-permute-start | bytes 663560 | tf_op jit(solution)/shard_map/ppermute | solution.py:40
  77.5 7.6 %collective-permute-start.17 = (bf16[144,768]{1,0:T(8,128)(2,1)S(1)}, bf16[144,768]{1,0:T(8,128)(2,1)S(1)}, u32[]{:S(2)}, u32[]{:S(2)}) collective-permute-start(bf16[144,768]{1,0:T(8,128)(2,1)S(1)} %add_packets.18), channel_id=1, source_target_pairs={{2,0},{7,1},{4,2},{1,3},{6,4},{3,5},{0,6},{5,7},{10,8},{15,9},{12,... | collective-permute-start | bytes 663560 | tf_op jit(solution)/shard_map/ppermute | solution.py:55
  79.5 5.7 %collective-permute-start.14 = (bf16[128,768]{1,0:T(8,128)(2,1)S(1)}, bf16[128,768]{1,0:T(8,128)(2,1)S(1)}, u32[]{:S(2)}, u32[]{:S(2)}) collective-permute-start(bf16[128,768]{1,0:T(8,128)(2,1)S(1)} %get-tuple-element.40), channel_id=1, source_target_pairs={{0,1},{1,0},{2,3},{3,2},{4,5},{5,4},{6,7},{7,6},{8,9},{9,8},{10,11... | collective-permute-start | bytes 589832 | tf_op jit(solution)/shard_map/ppermute | solution.py:40
  79.5 7.8 %collective-permute-start.19 = (bf16[128,768]{1,0:T(8,128)(2,1)S(1)}, bf16[128,768]{1,0:T(8,128)(2,1)S(1)}, u32[]{:S(2)}, u32[]{:S(2)}) collective-permute-start(bf16[128,768]{1,0:T(8,128)(2,1)S(1)} %get-tuple-element.44), channel_id=1, source_target_pairs={{0,16},{8,24},{16,0},{24,8},{1,17},{9,25},{17,1},{25,9},{2,18},{10... | collective-permute-start | bytes 589832 | tf_op jit(solution)/shard_map/ppermute | solution.py:27
  81.9 14.4 %collective-permute-start.13 = (bf16[144,768]{1,0:T(8,128)(2,1)S(1)}, bf16[144,768]{1,0:T(8,128)(2,1)S(1)}, u32[]{:S(2)}, u32[]{:S(2)}) collective-permute-start(bf16[144,768]{1,0:T(8,128)(2,1)S(1)} %add_packets.16.refs_5_), channel_id=1, source_target_pairs={{0,16},{8,24},{16,0},{24,8},{1,17},{9,25},{17,1},{25,9},{2,18},{10... | collective-permute-start | bytes 663560 | tf_op jit(solution)/shard_map/ppermute | solution.py:27
  85.8 10.5 %collective-permute-start.18 = (bf16[144,768]{1,0:T(8,128)(2,1)S(1)}, bf16[144,768]{1,0:T(8,128)(2,1)S(1)}, u32[]{:S(2)}, u32[]{:S(2)}) collective-permute-start(bf16[144,768]{1,0:T(8,128)(2,1)S(1)} %add_packets.19), channel_id=1, source_target_pairs={{0,1},{1,0},{2,3},{3,2},{4,5},{5,4},{6,7},{7,6},{8,9},{9,8},{10,11... | collective-permute-start | bytes 663560 | tf_op jit(solution)/shard_map/ppermute | solution.py:40
  86.2 7.7 %collective-permute-start.11 = (bf16[128,768]{1,0:T(8,128)(2,1)S(1)}, bf16[128,768]{1,0:T(8,128)(2,1)S(1)}, u32[]{:S(2)}, u32[]{:S(2)}) collective-permute-start(bf16[128,768]{1,0:T(8,128)(2,1)S(1)} %add_packets.15.refs_4_), channel_id=1, source_target_pairs={{0,16},{8,24},{16,0},{24,8},{1,17},{9,25},{17,1},{25,9},{2,18},{10... | collective-permute-start | bytes 589832 | tf_op jit(solution)/shard_map/ppermute | solution.py:27
  87.9 8.4 %collective-permute-start.20 = (bf16[128,768]{1,0:T(8,128)(2,1)S(1)}, bf16[128,768]{1,0:T(8,128)(2,1)S(1)}, u32[]{:S(2)}, u32[]{:S(2)}) collective-permute-start(bf16[128,768]{1,0:T(8,128)(2,1)S(1)} %add_packets.20), channel_id=1, source_target_pairs={{0,7},{1,2},{2,1},{3,4},{4,3},{5,6},{6,5},{7,0},{8,15},{9,10},{10,... | collective-permute-start | bytes 589832 | tf_op jit(solution)/shard_map/ppermute | solution.py:45
  97.3 8.1 %collective-permute-start.26 = (bf16[272,768]{1,0:T(8,128)(2,1)S(1)}, bf16[272,768]{1,0:T(8,128)(2,1)S(1)}, u32[]{:S(2)}, u32[]{:S(2)}) collective-permute-start(bf16[272,768]{1,0:T(8,128)(2,1)S(1)} %renew.2.refs_8_.base), channel_id=1, source_target_pairs={{0,16},{8,24},{16,0},{24,8},{1,17},{9,25},{17,1},{25,9},{2,18},{10... | collective-permute-start | bytes 1253384 | tf_op jit(solution)/shard_map/ppermute | solution.py:27
  98.3 10.8 %collective-permute-start.21 = (bf16[272,768]{1,0:T(8,128)(2,1)S(1)}, bf16[272,768]{1,0:T(8,128)(2,1)S(1)}, u32[]{:S(2)}, u32[]{:S(2)}) collective-permute-start(bf16[272,768]{1,0:T(8,128)(2,1)S(1)} %renew.2.refs_8_.base), channel_id=1, source_target_pairs={{0,7},{1,2},{2,1},{3,4},{4,3},{5,6},{6,5},{7,0},{8,15},{9,10},{10,... | collective-permute-start | bytes 1253384 | tf_op jit(solution)/shard_map/ppermute | solution.py:45
  101.5 8.7 %collective-permute-start.30 = (bf16[272,768]{1,0:T(8,128)(2,1)S(1)}, bf16[272,768]{1,0:T(8,128)(2,1)S(1)}, u32[]{:S(2)}, u32[]{:S(2)}) collective-permute-start(bf16[272,768]{1,0:T(8,128)(2,1)S(1)} %renew.2.refs_8_.base), channel_id=1, source_target_pairs={{0,8},{8,0},{16,24},{24,16},{1,9},{9,1},{17,25},{25,17},{2,10},{10... | collective-permute-start | bytes 1253384 | tf_op jit(solution)/shard_map/ppermute | solution.py:27
  101.5 16.5 %collective-permute-start.25 = (bf16[272,768]{1,0:T(8,128)(2,1)S(1)}, bf16[272,768]{1,0:T(8,128)(2,1)S(1)}, u32[]{:S(2)}, u32[]{:S(2)}) collective-permute-start(bf16[272,768]{1,0:T(8,128)(2,1)S(1)} %renew.2.refs_8_.base), channel_id=1, source_target_pairs={{0,1},{1,0},{2,3},{3,2},{4,5},{5,4},{6,7},{7,6},{8,9},{9,8},{10,11... | collective-permute-start | bytes 1253384 | tf_op jit(solution)/shard_map/ppermute | solution.py:40
  105.4 21.5 %collective-permute-start.27 = (bf16[272,768]{1,0:T(8,128)(2,1)S(1)}, bf16[272,768]{1,0:T(8,128)(2,1)S(1)}, u32[]{:S(2)}, u32[]{:S(2)}) collective-permute-start(bf16[272,768]{1,0:T(8,128)(2,1)S(1)} %collective-permute-done.26.refs_9_), channel_id=1, source_target_pairs={{0,1},{1,0},{2,3},{3,2},{4,5},{5,4},{6,7},{7,6},{8,9},{9,8},{10,11... | collective-permute-start | bytes 1253384 | tf_op jit(solution)/shard_map/ppermute | solution.py:40
  109.2 17.9 %collective-permute-start.22 = (bf16[272,768]{1,0:T(8,128)(2,1)S(1)}, bf16[272,768]{1,0:T(8,128)(2,1)S(1)}, u32[]{:S(2)}, u32[]{:S(2)}) collective-permute-start(bf16[272,768]{1,0:T(8,128)(2,1)S(1)} %collective-permute-done.21.refs_0_), channel_id=1, source_target_pairs={{0,16},{8,24},{16,0},{24,8},{1,17},{9,25},{17,1},{25,9},{2,18},{10... | collective-permute-start | bytes 1253384 | tf_op jit(solution)/shard_map/ppermute | solution.py:27
  110.2 17.3 %collective-permute-start.31 = (bf16[272,768]{1,0:T(8,128)(2,1)S(1)}, bf16[272,768]{1,0:T(8,128)(2,1)S(1)}, u32[]{:S(2)}, u32[]{:S(2)}) collective-permute-start(bf16[272,768]{1,0:T(8,128)(2,1)S(1)} %collective-permute-done.26.refs_9_), channel_id=1, source_target_pairs={{0,8},{8,0},{16,24},{24,16},{1,9},{9,1},{17,25},{25,17},{2,10},{10... | collective-permute-start | bytes 1253384 | tf_op jit(solution)/shard_map/ppermute | solution.py:27
  110.2 17.3 %collective-permute-start.23 = (bf16[272,768]{1,0:T(8,128)(2,1)S(1)}, bf16[272,768]{1,0:T(8,128)(2,1)S(1)}, u32[]{:S(2)}, u32[]{:S(2)}) collective-permute-start(bf16[272,768]{1,0:T(8,128)(2,1)S(1)} %collective-permute-done.21.refs_0_), channel_id=1, source_target_pairs={{0,8},{8,0},{16,24},{24,16},{1,9},{9,1},{17,25},{25,17},{2,10},{10... | collective-permute-start | bytes 1253384 | tf_op jit(solution)/shard_map/ppermute | solution.py:27
  118.0 9.4 %collective-permute-start.28 = (bf16[272,768]{1,0:T(8,128)(2,1)S(1)}, bf16[272,768]{1,0:T(8,128)(2,1)S(1)}, u32[]{:S(2)}, u32[]{:S(2)}) collective-permute-start(bf16[272,768]{1,0:T(8,128)(2,1)S(1)} %collective-permute-done.25.refs_4_), channel_id=1, source_target_pairs={{0,8},{8,0},{16,24},{24,16},{1,9},{9,1},{17,25},{25,17},{2,10},{10... | collective-permute-start | bytes 1253384 | tf_op jit(solution)/shard_map/ppermute | solution.py:27
  127.0 2.3 %collective-permute-start.24 = (bf16[272,768]{1,0:T(8,128)(2,1)S(1)}, bf16[272,768]{1,0:T(8,128)(2,1)S(1)}, u32[]{:S(2)}, u32[]{:S(2)}) collective-permute-start(bf16[272,768]{1,0:T(8,128)(2,1)S(1)} %collective-permute-done.22.refs_1_), channel_id=1, source_target_pairs={{0,8},{8,0},{16,24},{24,16},{1,9},{9,1},{17,25},{25,17},{2,10},{10... | collective-permute-start | bytes 1253384 | tf_op jit(solution)/shard_map/ppermute | solution.py:27
  154.2 2.4 %collective-permute-start.39 = (bf16[544,768]{1,0:T(8,128)(2,1)S(1)}, bf16[544,768]{1,0:T(8,128)(2,1)S(1)}, u32[]{:S(2)}, u32[]{:S(2)}) collective-permute-start(bf16[544,768]{1,0:T(8,128)(2,1)S(1)} %get-tuple-element.53), channel_id=1, source_target_pairs={{0,8},{8,0},{16,24},{24,16},{1,9},{9,1},{17,25},{25,17},{2,10},{10... | collective-permute-start | bytes 2506760 | tf_op jit(solution)/shard_map/ppermute | solution.py:27
  154.4 3.6 %collective-permute-start.33 = (bf16[544,768]{1,0:T(8,128)(2,1)S(1)}, bf16[544,768]{1,0:T(8,128)(2,1)S(1)}, u32[]{:S(2)}, u32[]{:S(2)}) collective-permute-start(bf16[544,768]{1,0:T(8,128)(2,1)S(1)} %get-tuple-element.48), channel_id=1, source_target_pairs={{0,8},{8,0},{16,24},{24,16},{1,9},{9,1},{17,25},{25,17},{2,10},{10... | collective-permute-start | bytes 2506760 | tf_op jit(solution)/shard_map/ppermute | solution.py:27
  154.8 15.1 %collective-permute-start.32 = (bf16[544,768]{1,0:T(8,128)(2,1)S(1)}, bf16[544,768]{1,0:T(8,128)(2,1)S(1)}, u32[]{:S(2)}, u32[]{:S(2)}) collective-permute-start(bf16[544,768]{1,0:T(8,128)(2,1)S(1)} %get-tuple-element.46), channel_id=1, source_target_pairs={{0,8},{8,0},{16,24},{24,16},{1,9},{9,1},{17,25},{25,17},{2,10},{10... | collective-permute-start | bytes 2506760 | tf_op jit(solution)/shard_map/ppermute | solution.py:27
  157.3 9.3 %collective-permute-start.40 = (bf16[144,768]{1,0:T(8,128)(2,1)S(1)}, bf16[144,768]{1,0:T(8,128)(2,1)S(1)}, u32[]{:S(2)}, u32[]{:S(2)}) collective-permute-start(bf16[144,768]{1,0:T(8,128)(2,1)S(1)} %get-tuple-element.54), channel_id=1, source_target_pairs={{0,16},{8,24},{16,0},{24,8},{1,17},{9,25},{17,1},{25,9},{2,18},{10... | collective-permute-start | bytes 663560 | tf_op jit(solution)/shard_map/ppermute | solution.py:27
  158.7 7.8 %collective-permute-start.34 = (bf16[128,768]{1,0:T(8,128)(2,1)S(1)}, bf16[128,768]{1,0:T(8,128)(2,1)S(1)}, u32[]{:S(2)}, u32[]{:S(2)}) collective-permute-start(bf16[128,768]{1,0:T(8,128)(2,1)S(1)} %get-tuple-element.49), channel_id=1, source_target_pairs={{0,1},{1,0},{2,3},{3,2},{4,5},{5,4},{6,7},{7,6},{8,9},{9,8},{10,11... | collective-permute-start | bytes 589832 | tf_op jit(solution)/shard_map/ppermute | solution.py:40
  158.8 12.0 %collective-permute-start.36 = (bf16[144,768]{1,0:T(8,128)(2,1)S(1)}, bf16[144,768]{1,0:T(8,128)(2,1)S(1)}, u32[]{:S(2)}, u32[]{:S(2)}) collective-permute-start(bf16[144,768]{1,0:T(8,128)(2,1)S(1)} %get-tuple-element.50), channel_id=1, source_target_pairs={{0,1},{1,0},{2,3},{3,2},{4,5},{5,4},{6,7},{7,6},{8,9},{9,8},{10,11... | collective-permute-start | bytes 663560 | tf_op jit(solution)/shard_map/ppermute | solution.py:40
  167.2 7.3 %collective-permute-start.41 = (bf16[144,768]{1,0:T(8,128)(2,1)S(1)}, bf16[144,768]{1,0:T(8,128)(2,1)S(1)}, u32[]{:S(2)}, u32[]{:S(2)}) collective-permute-start(bf16[144,768]{1,0:T(8,128)(2,1)S(1)} %add_packets.25), channel_id=1, source_target_pairs={{2,0},{7,1},{4,2},{1,3},{6,4},{3,5},{0,6},{5,7},{10,8},{15,9},{12,... | collective-permute-start | bytes 663560 | tf_op jit(solution)/shard_map/ppermute | solution.py:55
  168.8 5.7 %collective-permute-start.38 = (bf16[128,768]{1,0:T(8,128)(2,1)S(1)}, bf16[128,768]{1,0:T(8,128)(2,1)S(1)}, u32[]{:S(2)}, u32[]{:S(2)}) collective-permute-start(bf16[128,768]{1,0:T(8,128)(2,1)S(1)} %get-tuple-element.51), channel_id=1, source_target_pairs={{0,1},{1,0},{2,3},{3,2},{4,5},{5,4},{6,7},{7,6},{8,9},{9,8},{10,11... | collective-permute-start | bytes 589832 | tf_op jit(solution)/shard_map/ppermute | solution.py:40
  168.8 8.2 %collective-permute-start.43 = (bf16[128,768]{1,0:T(8,128)(2,1)S(1)}, bf16[128,768]{1,0:T(8,128)(2,1)S(1)}, u32[]{:S(2)}, u32[]{:S(2)}) collective-permute-start(bf16[128,768]{1,0:T(8,128)(2,1)S(1)} %get-tuple-element.55), channel_id=1, source_target_pairs={{0,16},{8,24},{16,0},{24,8},{1,17},{9,25},{17,1},{25,9},{2,18},{10... | collective-permute-start | bytes 589832 | tf_op jit(solution)/shard_map/ppermute | solution.py:27
  171.4 14.6 %collective-permute-start.37 = (bf16[144,768]{1,0:T(8,128)(2,1)S(1)}, bf16[144,768]{1,0:T(8,128)(2,1)S(1)}, u32[]{:S(2)}, u32[]{:S(2)}) collective-permute-start(bf16[144,768]{1,0:T(8,128)(2,1)S(1)} %add_packets.23.refs_5_), channel_id=1, source_target_pairs={{0,16},{8,24},{16,0},{24,8},{1,17},{9,25},{17,1},{25,9},{2,18},{10... | collective-permute-start | bytes 663560 | tf_op jit(solution)/shard_map/ppermute | solution.py:27
  175.1 10.9 %collective-permute-start.42 = (bf16[144,768]{1,0:T(8,128)(2,1)S(1)}, bf16[144,768]{1,0:T(8,128)(2,1)S(1)}, u32[]{:S(2)}, u32[]{:S(2)}) collective-permute-start(bf16[144,768]{1,0:T(8,128)(2,1)S(1)} %add_packets.26), channel_id=1, source_target_pairs={{0,1},{1,0},{2,3},{3,2},{4,5},{5,4},{6,7},{7,6},{8,9},{9,8},{10,11... | collective-permute-start | bytes 663560 | tf_op jit(solution)/shard_map/ppermute | solution.py:40
  175.7 7.7 %collective-permute-start.35 = (bf16[128,768]{1,0:T(8,128)(2,1)S(1)}, bf16[128,768]{1,0:T(8,128)(2,1)S(1)}, u32[]{:S(2)}, u32[]{:S(2)}) collective-permute-start(bf16[128,768]{1,0:T(8,128)(2,1)S(1)} %add_packets.22.refs_4_), channel_id=1, source_target_pairs={{0,16},{8,24},{16,0},{24,8},{1,17},{9,25},{17,1},{25,9},{2,18},{10... | collective-permute-start | bytes 589832 | tf_op jit(solution)/shard_map/ppermute | solution.py:27
  177.6 8.4 %collective-permute-start.44 = (bf16[128,768]{1,0:T(8,128)(2,1)S(1)}, bf16[128,768]{1,0:T(8,128)(2,1)S(1)}, u32[]{:S(2)}, u32[]{:S(2)}) collective-permute-start(bf16[128,768]{1,0:T(8,128)(2,1)S(1)} %add_packets.27), channel_id=1, source_target_pairs={{0,7},{1,2},{2,1},{3,4},{4,3},{5,6},{6,5},{7,0},{8,15},{9,10},{10,... | collective-permute-start | bytes 589832 | tf_op jit(solution)/shard_map/ppermute | solution.py:45
  187.0 6.1 %collective-permute-start.46 = (bf16[144,768]{1,0:T(8,128)(2,1)S(1)}, bf16[144,768]{1,0:T(8,128)(2,1)S(1)}, u32[]{:S(2)}, u32[]{:S(2)}) collective-permute-start(bf16[144,768]{1,0:T(8,128)(2,1)S(1)} %get-tuple-element.57.refs_1_), channel_id=1, source_target_pairs={{0,16},{8,24},{16,0},{24,8},{1,17},{9,25},{17,1},{25,9},{2,18},{10... | collective-permute-start | bytes 663560 | tf_op jit(solution)/shard_map/ppermute | solution.py:27
  187.9 7.3 %collective-permute-start.45 = (bf16[128,768]{1,0:T(8,128)(2,1)S(1)}, bf16[128,768]{1,0:T(8,128)(2,1)S(1)}, u32[]{:S(2)}, u32[]{:S(2)}) collective-permute-start(bf16[128,768]{1,0:T(8,128)(2,1)S(1)} %get-tuple-element.56.refs_0_), channel_id=1, source_target_pairs={{0,16},{8,24},{16,0},{24,8},{1,17},{9,25},{17,1},{25,9},{2,18},{10... | collective-permute-start | bytes 589832 | tf_op jit(solution)/shard_map/ppermute | solution.py:27
  189.1 6.1 %collective-permute-start.48 = (bf16[144,768]{1,0:T(8,128)(2,1)S(1)}, bf16[144,768]{1,0:T(8,128)(2,1)S(1)}, u32[]{:S(2)}, u32[]{:S(2)}) collective-permute-start(bf16[144,768]{1,0:T(8,128)(2,1)S(1)} %get-tuple-element.57.refs_1_), channel_id=1, source_target_pairs={{0,8},{8,0},{16,24},{24,16},{1,9},{9,1},{17,25},{25,17},{2,10},{10... | collective-permute-start | bytes 663560 | tf_op jit(solution)/shard_map/ppermute | solution.py:27
  193.1 3.6 %collective-permute-start.50 = (bf16[144,768]{1,0:T(8,128)(2,1)S(1)}, bf16[144,768]{1,0:T(8,128)(2,1)S(1)}, u32[]{:S(2)}, u32[]{:S(2)}) collective-permute-start(bf16[144,768]{1,0:T(8,128)(2,1)S(1)} %collective-permute-done.46.refs_3_), channel_id=1, source_target_pairs={{0,8},{8,0},{16,24},{24,16},{1,9},{9,1},{17,25},{25,17},{2,10},{10... | collective-permute-start | bytes 663560 | tf_op jit(solution)/shard_map/ppermute | solution.py:27
  193.1 2.1 %collective-permute-start.47 = (bf16[128,768]{1,0:T(8,128)(2,1)S(1)}, bf16[128,768]{1,0:T(8,128)(2,1)S(1)}, u32[]{:S(2)}, u32[]{:S(2)}) collective-permute-start(bf16[128,768]{1,0:T(8,128)(2,1)S(1)} %get-tuple-element.56.refs_0_), channel_id=1, source_target_pairs={{0,8},{8,0},{16,24},{24,16},{1,9},{9,1},{17,25},{25,17},{2,10},{10... | collective-permute-start | bytes 589832 | tf_op jit(solution)/shard_map/ppermute | solution.py:27
  (5 other events, 41.6 us)

commit v4 on v3

--- a/solution.py
+++ b/solution.py
@@ -155,26 +155,13 @@
         macc[at, :] = jnp.zeros((BLOCK, TILE), F32)
 
 
-def points_specs(width):
-    rows = STEP_TILES * TILE // 2
-    return [
-        pl.BlockSpec((rows, width), lambda i, ids, me: (2 * i, 0)),
-        pl.BlockSpec((rows, width), lambda i, ids, me: (2 * i + 1, 0)),
-    ]
-
-
-def points_of(low, high, t):
-    half = STEP_TILES // 2
-    return (low if t < half else high)[pl.ds(t % half * TILE, TILE), :]
-
-
-def tiles_kernel(rows, sizes, ids_ref, me_ref, points_low, points_high, *refs):
+def tiles_kernel(rows, sizes, ids_ref, me_ref, points_ref, *refs):
     quarter = rows // 4
     count = sum(len(parts) for side in sizes for parts in side)
     parts_refs = list(refs[:count])
     sends = refs[count : count + 3]
     keeps = refs[count + 3 : count + 6]
-    near, tails, offs, acc, macc, in_sem = refs[count + 6 :]
+    near, tails, offs, acc, macc, held, in_sem, held_sem = refs[count + 6 :]
     step = pl.program_id(0)
     core = me_ref[0]
     plane = me_ref[1]
@@ -212,12 +199,22 @@
         return out
 
     width = near.shape[1]
+    step_rows = STEP_TILES * TILE
+
+    def points_copy(n):
+        at = pl.ds(pl.multiple_of(n * step_rows, step_rows), step_rows)
+        return pltpu.make_async_copy(points_ref.at[at], held.at[at], held_sem.at[n])
+
+    def rows_at(t):
+        return pl.ds(pl.multiple_of(step * step_rows + t * TILE, TILE), TILE)
 
     @pl.when(step == 0)
     def _():
         copies = arrivals()
         for copy in copies:
             copy.start()
+        for n in range(held.shape[0] // step_rows):
+            points_copy(n).start()
         clear(acc, macc)
         for copy in copies:
             copy.wait()
@@ -235,9 +232,10 @@
             pl.ds(pl.multiple_of(ids_ref[tile * SLOTS + k] * BLOCK, BLOCK), BLOCK) for k in slots
         ]
 
+    points_copy(step).wait()
     members = []
     for t in range(STEP_TILES):
-        points = points_of(points_low, points_high, t)
+        points = held[rows_at(t), :]
         at = blocks_of(t, (0, 2, 1, 3))
         cand = jnp.concatenate([near[a, :] for a in at], axis=0)
         off = jnp.concatenate([offs[a, :] for a in at], axis=0)
@@ -251,7 +249,7 @@
         member = (raw * (1.0 / total)).astype(BF16)
         members.append(member)
     for t in range(STEP_TILES):
-        points = points_of(points_low, points_high, t)
+        points = held[rows_at(t), :]
         at = blocks_of(t, (0, 2, 1, 3))
         numerator = jnp.dot(members[t], points, preferred_element_type=F32)
         masses = members[t].astype(F32)
@@ -279,7 +277,7 @@
         grid_spec=pltpu.PrefetchScalarGridSpec(
             num_scalar_prefetch=2,
             grid=(tiles // STEP_TILES,),
-            in_specs=points_specs(width) + [any_spec] * len(arrays),
+            in_specs=[pl.BlockSpec(memory_space=pltpu.HBM)] + [any_spec] * len(arrays),
             out_specs=[vmem_spec] * 6,
             scratch_shapes=[
                 pltpu.VMEM((3 * rows, width), BF16),
@@ -287,7 +285,9 @@
                 pltpu.VMEM((3 * rows, TILE), F32),
                 pltpu.VMEM((3 * rows, width), F32),
                 pltpu.VMEM((3 * rows, TILE), F32),
+                pltpu.VMEM((count, width), BF16),
                 pltpu.SemaphoreType.DMA((len(arrays) + 12,)),
+                pltpu.SemaphoreType.DMA((tiles // STEP_TILES,)),
             ],
         ),
         out_shape=[jax.ShapeDtypeStruct((2 * packet, width), BF16)] * 3
@@ -299,7 +299,7 @@
             transcendentals=count * SLOTS * BLOCK,
         ),
         name="tiles",
-    )(ids, me, points, points, *arrays)
+    )(ids, me, points, *arrays)
     return outs[:3], outs[3:]
 
 

time: 199 us -> 197 us (0.990)
  Pallas kernels: 64.1 us -> 61.7 us
    pallas_call x2, Pallas kernels: 48.7 us -> 46.3 us  [assign_tiles(): pl.pallas_call(functools.partial(tiles_kernel, rows, sizes), grid_spec=pl...]
where the time goes in v4:
time: 197 us
  waiting for transfers between devices  88 us (45%)
  Pallas kernels  61.7 us (31%)
  starting transfers between devices  43.1 us (22%)
  local copies, waits for them, and re-layouts  2.89 us (1%)
    ppermute x12, waiting for transfers between devices, pair_swap(): return lax.ppermute(x, 'blk', [(i, i ^ 1) for i in range(count)])  48.9 us
    pallas_call x2, Pallas kernels, assign_tiles(): pl.pallas_call(functools.partial(tiles_kernel, rows, sizes), grid_spec=pl...  46.3 us
    ppermute x33, waiting for transfers between devices, swap(): return lax.ppermute(x, 'group', [(i, i ^ bit) for i in range(groups)])  24.4 us
    ppermute x33, starting transfers between devices, swap(): return lax.ppermute(x, 'group', [(i, i ^ bit) for i in range(groups)])  17.6 us
    ppermute x4, starting transfers between devices, cross_swap(): lax.ppermute(x, 'blk', [(i, (i - 1 + i % 2 * 2) % count) for i in range(c...  14.7 us
    ppermute x4, waiting for transfers between devices, cross_swap(): lax.ppermute(x, 'blk', [(i, (i - 1 + i % 2 * 2) % count) for i in range(c...  14.7 us
    pallas_call x16, Pallas kernels, small_call(): pl.pallas_call(kernel, in_specs=[pl.BlockSpec(memory_space=pltpu.SMEM)] +...  10.9 us
    ppermute x12, starting transfers between devices, pair_swap(): return lax.ppermute(x, 'blk', [(i, i ^ 1) for i in range(count)])  7.23 us
  transfers between devices with their start and end apart: 51, of which 27 were waited for; matrix products, arithmetic and copies ran while one was open for 0% of the time, Pallas kernels for 5%

profile of v4, /device:TPU:0, one launch (start us, length us, event | category | flops | bytes accessed | tf_op | source)
XLA Modules:
  0.0 196.7 jit_solution(8101693207109377263)
XLA Ops:
  1.4 1.4 copy-done
  2.8 1.0 start_packets.2.refs_8_.base
  3.8 6.0 %collective-permute-start = (bf16[272,768]{1,0:T(8,128)(2,1)S(1)}, bf16[272,768]{1,0:T(8,128)(2,1)S(1)}, u32[]{:S(2)}, u32[]{:S(2)}) collective-permute-start(bf16[272,768]{1,0:T(8,128)(2,1)S(1)} %start_packets.2.refs_8_.base), channel_id=1, source_target_pairs={{0,7},{1,2},{2,1},{3,4},{4,3},{5,6},{6,5},{7,0},{8,15},{9,10},{10,... | collective-permute-start | bytes 1253384 | tf_op jit(solution)/shard_map/ppermute | solution.py:45
  9.8 1.7 start_packets.3
  11.6 2.1 %collective-permute-start.5 = (bf16[272,768]{1,0:T(8,128)(2,1)S(1)}, bf16[272,768]{1,0:T(8,128)(2,1)S(1)}, u32[]{:S(2)}, u32[]{:S(2)}) collective-permute-start(bf16[272,768]{1,0:T(8,128)(2,1)S(1)} %get-tuple-element.31.refs_9_), channel_id=1, source_target_pairs={{0,1},{1,0},{2,3},{3,2},{4,5},{5,4},{6,7},{7,6},{8,9},{9,8},{10,11... | collective-permute-start | bytes 1253384 | tf_op jit(solution)/shard_map/ppermute | solution.py:40
  13.7 5.9 %collective-permute-done.refs_0_ = bf16[272,768]{1,0:T(8,128)(2,1)S(1)} collective-permute-done((bf16[272,768]{1,0:T(8,128)(2,1)S(1)}, bf16[272,768]{1,0:T(8,128)(2,1)S(1)}, u32[]{:S(2)}, u32[]{:S(2)}) %collective-permute-start) | collective-permute-done | bytes 417824 | tf_op jit(solution)/shard_map/ppermute | solution.py:45
  19.6 1.5 collective-permute-start.1
  21.1 7.4 %collective-permute-done.4.refs_4_ = bf16[272,768]{1,0:T(8,128)(2,1)S(1)} collective-permute-done((bf16[272,768]{1,0:T(8,128)(2,1)S(1)}, bf16[272,768]{1,0:T(8,128)(2,1)S(1)}, u32[]{:S(2)}, u32[]{:S(2)}) %collective-permute-start.4) | collective-permute-done | bytes 417824 | tf_op jit(solution)/shard_map/ppermute | solution.py:40
  28.5 8.9 %collective-permute-done.5.refs_5_ = bf16[272,768]{1,0:T(8,128)(2,1)S(1)} collective-permute-done((bf16[272,768]{1,0:T(8,128)(2,1)S(1)}, bf16[272,768]{1,0:T(8,128)(2,1)S(1)}, u32[]{:S(2)}, u32[]{:S(2)}) %collective-permute-start.5) | collective-permute-done | bytes 417824 | tf_op jit(solution)/shard_map/ppermute | solution.py:40
  38.1 1.1 collective-permute-done.7.refs_7_
  39.9 22.6 %tiles.2 = (bf16[544,768]{1,0:T(8,128)(2,1)S(1)}, bf16[544,768]{1,0:T(8,128)(2,1)S(1)}, bf16[544,768]{1,0:T(8,128)(2,1)S(1)}, f32[544,768]{1,0:T(8,128)S(1)}, f3...) custom-call(s32[256]{0:T(256)S(1)} %reshape.14.ids_ref, s32[2]{0:T(128)S(1)} %pad_add_fusion.me_ref, ...), custom_call_target="tpu_custom_call" | custom-call | flops 6442450944 | bytes 12582912 | tf_op jit(solution)/shard_map/tiles/pallas_call | solution.py:275
  63.2 1.7 collective-permute-done.15.refs_1_
  65.6 1.6 collective-permute-start.16
  67.9 2.0 %collective-permute-start.12 = (bf16[144,768]{1,0:T(8,128)(2,1)S(1)}, bf16[144,768]{1,0:T(8,128)(2,1)S(1)}, u32[]{:S(2)}, u32[]{:S(2)}) collective-permute-start(bf16[144,768]{1,0:T(8,128)(2,1)S(1)} %get-tuple-element.39), channel_id=1, source_target_pairs={{0,1},{1,0},{2,3},{3,2},{4,5},{5,4},{6,7},{7,6},{8,9},{9,8},{10,11... | collective-permute-start | bytes 663560 | tf_op jit(solution)/shard_map/ppermute | solution.py:40
  70.0 5.8 %collective-permute-done.10.refs_2_.refs_3_ = bf16[128,768]{1,0:T(8,128)(2,1)S(1)} collective-permute-done((bf16[128,768]{1,0:T(8,128)(2,1)S(1)}, bf16[128,768]{1,0:T(8,128)(2,1)S(1)}, u32[]{:S(2)}, u32[]{:S(2)}) %collective-permute-start.10) | collective-permute-done | bytes 196640 | tf_op jit(solution)/shard_map/ppermute | solution.py:40
  76.3 2.0 collective-permute-start.17
  81.7 2.3 %collective-permute-done.14.refs_3_.refs_2_ = bf16[128,768]{1,0:T(8,128)(2,1)S(1)} collective-permute-done((bf16[128,768]{1,0:T(8,128)(2,1)S(1)}, bf16[128,768]{1,0:T(8,128)(2,1)S(1)}, u32[]{:S(2)}, u32[]{:S(2)}) %collective-permute-start.14) | collective-permute-done | bytes 196640 | tf_op jit(solution)/shard_map/ppermute | solution.py:40
  85.0 0.9 collective-permute-start.11
  86.7 2.7 %collective-permute-start.20 = (bf16[128,768]{1,0:T(8,128)(2,1)S(1)}, bf16[128,768]{1,0:T(8,128)(2,1)S(1)}, u32[]{:S(2)}, u32[]{:S(2)}) collective-permute-start(bf16[128,768]{1,0:T(8,128)(2,1)S(1)} %add_packets.20), channel_id=1, source_target_pairs={{0,7},{1,2},{2,1},{3,4},{4,3},{5,6},{6,5},{7,0},{8,15},{9,10},{10,... | collective-permute-start | bytes 589832 | tf_op jit(solution)/shard_map/ppermute | solution.py:45
  89.3 3.3 %collective-permute-done.11.refs_0_ = bf16[128,768]{1,0:T(8,128)(2,1)S(1)} collective-permute-done((bf16[128,768]{1,0:T(8,128)(2,1)S(1)}, bf16[128,768]{1,0:T(8,128)(2,1)S(1)}, u32[]{:S(2)}, u32[]{:S(2)}) %collective-permute-start.11) | collective-permute-done | bytes 196640 | tf_op jit(solution)/shard_map/ppermute | solution.py:27
  92.7 2.4 %collective-permute-done.20.refs_4_ = bf16[128,768]{1,0:T(8,128)(2,1)S(1)} collective-permute-done((bf16[128,768]{1,0:T(8,128)(2,1)S(1)}, bf16[128,768]{1,0:T(8,128)(2,1)S(1)}, u32[]{:S(2)}, u32[]{:S(2)}) %collective-permute-start.20) | collective-permute-done | bytes 196640 | tf_op jit(solution)/shard_map/ppermute | solution.py:45
  95.1 1.0 renew.2.refs_8_.base
  96.1 1.0 collective-permute-start.26
  97.1 3.2 %collective-permute-start.21 = (bf16[272,768]{1,0:T(8,128)(2,1)S(1)}, bf16[272,768]{1,0:T(8,128)(2,1)S(1)}, u32[]{:S(2)}, u32[]{:S(2)}) collective-permute-start(bf16[272,768]{1,0:T(8,128)(2,1)S(1)} %renew.2.refs_8_.base), channel_id=1, source_target_pairs={{0,7},{1,2},{2,1},{3,4},{4,3},{5,6},{6,5},{7,0},{8,15},{9,10},{10,... | collective-permute-start | bytes 1253384 | tf_op jit(solution)/shard_map/ppermute | solution.py:45
  100.4 3.9 %collective-permute-done.26.refs_9_ = bf16[272,768]{1,0:T(8,128)(2,1)S(1)} collective-permute-done((bf16[272,768]{1,0:T(8,128)(2,1)S(1)}, bf16[272,768]{1,0:T(8,128)(2,1)S(1)}, u32[]{:S(2)}, u32[]{:S(2)}) %collective-permute-start.26) | collective-permute-done | bytes 417824 | tf_op jit(solution)/shard_map/ppermute | solution.py:27
  104.2 3.7 %collective-permute-done.21.refs_0_ = bf16[272,768]{1,0:T(8,128)(2,1)S(1)} collective-permute-done((bf16[272,768]{1,0:T(8,128)(2,1)S(1)}, bf16[272,768]{1,0:T(8,128)(2,1)S(1)}, u32[]{:S(2)}, u32[]{:S(2)}) %collective-permute-start.21) | collective-permute-done | bytes 417824 | tf_op jit(solution)/shard_map/ppermute | solution.py:45
  108.0 1.0 collective-permute-start.22
  109.5 7.3 %collective-permute-done.25.refs_4_ = bf16[272,768]{1,0:T(8,128)(2,1)S(1)} collective-permute-done((bf16[272,768]{1,0:T(8,128)(2,1)S(1)}, bf16[272,768]{1,0:T(8,128)(2,1)S(1)}, u32[]{:S(2)}, u32[]{:S(2)}) %collective-permute-start.25) | collective-permute-done | bytes 417824 | tf_op jit(solution)/shard_map/ppermute | solution.py:40
  116.9 8.9 %collective-permute-done.27.refs_5_ = bf16[272,768]{1,0:T(8,128)(2,1)S(1)} collective-permute-done((bf16[272,768]{1,0:T(8,128)(2,1)S(1)}, bf16[272,768]{1,0:T(8,128)(2,1)S(1)}, u32[]{:S(2)}, u32[]{:S(2)}) %collective-permute-start.27) | collective-permute-done | bytes 417824 | tf_op jit(solution)/shard_map/ppermute | solution.py:40
  126.3 1.2 collective-permute-done.29.refs_7_
  128.1 23.6 %tiles.3 = (bf16[544,768]{1,0:T(8,128)(2,1)S(1)}, bf16[544,768]{1,0:T(8,128)(2,1)S(1)}, bf16[544,768]{1,0:T(8,128)(2,1)S(1)}, f32[544,768]{1,0:T(8,128)S(1)}, f3...) custom-call(s32[256]{0:T(256)S(1)} %reshape.14.ids_ref, s32[2]{0:T(128)S(1)} %pad_add_fusion.me_ref, ...), custom_call_target="tpu_custom_call" | custom-call | flops 6442450944 | bytes 12582912 | tf_op jit(solution)/shard_map/tiles/pallas_call | solution.py:275
  152.5 1.7 collective-permute-done.39.refs_1_
  156.4 2.0 %collective-permute-start.36 = (bf16[144,768]{1,0:T(8,128)(2,1)S(1)}, bf16[144,768]{1,0:T(8,128)(2,1)S(1)}, u32[]{:S(2)}, u32[]{:S(2)}) collective-permute-start(bf16[144,768]{1,0:T(8,128)(2,1)S(1)} %get-tuple-element.50), channel_id=1, source_target_pairs={{0,1},{1,0},{2,3},{3,2},{4,5},{5,4},{6,7},{7,6},{8,9},{9,8},{10,11... | collective-permute-start | bytes 663560 | tf_op jit(solution)/shard_map/ppermute | solution.py:40
  158.4 5.7 %collective-permute-done.34.refs_2_.refs_3_ = bf16[128,768]{1,0:T(8,128)(2,1)S(1)} collective-permute-done((bf16[128,768]{1,0:T(8,128)(2,1)S(1)}, bf16[128,768]{1,0:T(8,128)(2,1)S(1)}, u32[]{:S(2)}, u32[]{:S(2)}) %collective-permute-start.34) | collective-permute-done | bytes 196640 | tf_op jit(solution)/shard_map/ppermute | solution.py:40
  164.8 1.6 collective-permute-start.41
  166.4 1.0 collective-permute-start.43
  169.1 1.5 collective-permute-start.37
  170.6 1.5 collective-permute-done.38.refs_3_.refs_2_
  173.3 1.3 collective-permute-start.35
  175.2 2.8 %collective-permute-start.44 = (bf16[128,768]{1,0:T(8,128)(2,1)S(1)}, bf16[128,768]{1,0:T(8,128)(2,1)S(1)}, u32[]{:S(2)}, u32[]{:S(2)}) collective-permute-start(bf16[128,768]{1,0:T(8,128)(2,1)S(1)} %add_packets.27), channel_id=1, source_target_pairs={{0,7},{1,2},{2,1},{3,4},{4,3},{5,6},{6,5},{7,0},{8,15},{9,10},{10,... | collective-permute-start | bytes 589832 | tf_op jit(solution)/shard_map/ppermute | solution.py:45
  178.0 3.0 %collective-permute-done.35.refs_0_ = bf16[128,768]{1,0:T(8,128)(2,1)S(1)} collective-permute-done((bf16[128,768]{1,0:T(8,128)(2,1)S(1)}, bf16[128,768]{1,0:T(8,128)(2,1)S(1)}, u32[]{:S(2)}, u32[]{:S(2)}) %collective-permute-start.35) | collective-permute-done | bytes 196640 | tf_op jit(solution)/shard_map/ppermute | solution.py:27
  181.1 2.6 %collective-permute-done.44.refs_4_ = bf16[128,768]{1,0:T(8,128)(2,1)S(1)} collective-permute-done((bf16[128,768]{1,0:T(8,128)(2,1)S(1)}, bf16[128,768]{1,0:T(8,128)(2,1)S(1)}, u32[]{:S(2)}, u32[]{:S(2)}) %collective-permute-start.44) | collective-permute-done | bytes 196640 | tf_op jit(solution)/shard_map/ppermute | solution.py:45
  183.6 1.0 renew.3
  185.5 1.2 collective-permute-start.45
  186.7 4.0 %collective-permute-done.46.refs_3_ = bf16[144,768]{1,0:T(8,128)(2,1)S(1)} collective-permute-done((bf16[144,768]{1,0:T(8,128)(2,1)S(1)}, bf16[144,768]{1,0:T(8,128)(2,1)S(1)}, u32[]{:S(2)}, u32[]{:S(2)}) %collective-permute-start.46) | collective-permute-done | bytes 221216 | tf_op jit(solution)/shard_map/ppermute | solution.py:27
  191.2 1.6 collective-permute-done.45.refs_2_
  192.8 1.4 collective-permute-done.49.refs_6_
  194.3 1.8 finish.1
  (85 shorter events, 20.6 us)
Async XLA Ops:
  3.8 15.8 %collective-permute-start = (bf16[272,768]{1,0:T(8,128)(2,1)S(1)}, bf16[272,768]{1,0:T(8,128)(2,1)S(1)}, u32[]{:S(2)}, u32[]{:S(2)}) collective-permute-start(bf16[272,768]{1,0:T(8,128)(2,1)S(1)} %start_packets.2.refs_8_.base), channel_id=1, source_target_pairs={{0,7},{1,2},{2,1},{3,4},{4,3},{5,6},{6,5},{7,0},{8,15},{9,10},{10,... | collective-permute-start | bytes 1253384 | tf_op jit(solution)/shard_map/ppermute | solution.py:45
  9.8 18.7 %collective-permute-start.4 = (bf16[272,768]{1,0:T(8,128)(2,1)S(1)}, bf16[272,768]{1,0:T(8,128)(2,1)S(1)}, u32[]{:S(2)}, u32[]{:S(2)}) collective-permute-start(bf16[272,768]{1,0:T(8,128)(2,1)S(1)} %start_packets.2.refs_8_.base), channel_id=1, source_target_pairs={{0,1},{1,0},{2,3},{3,2},{4,5},{5,4},{6,7},{7,6},{8,9},{9,8},{10,11... | collective-permute-start | bytes 1253384 | tf_op jit(solution)/shard_map/ppermute | solution.py:40
  11.6 25.8 %collective-permute-start.5 = (bf16[272,768]{1,0:T(8,128)(2,1)S(1)}, bf16[272,768]{1,0:T(8,128)(2,1)S(1)}, u32[]{:S(2)}, u32[]{:S(2)}) collective-permute-start(bf16[272,768]{1,0:T(8,128)(2,1)S(1)} %get-tuple-element.31.refs_9_), channel_id=1, source_target_pairs={{0,1},{1,0},{2,3},{3,2},{4,5},{5,4},{6,7},{7,6},{8,9},{9,8},{10,11... | collective-permute-start | bytes 1253384 | tf_op jit(solution)/shard_map/ppermute | solution.py:40
  19.6 17.8 %collective-permute-start.1 = (bf16[272,768]{1,0:T(8,128)(2,1)S(1)}, bf16[272,768]{1,0:T(8,128)(2,1)S(1)}, u32[]{:S(2)}, u32[]{:S(2)}) collective-permute-start(bf16[272,768]{1,0:T(8,128)(2,1)S(1)} %collective-permute-done.refs_0_), channel_id=1, source_target_pairs={{0,16},{8,24},{16,0},{24,8},{1,17},{9,25},{17,1},{25,9},{2,18},{10... | collective-permute-start | bytes 1253384 | tf_op jit(solution)/shard_map/ppermute | solution.py:27
  21.1 17.0 %collective-permute-start.2 = (bf16[272,768]{1,0:T(8,128)(2,1)S(1)}, bf16[272,768]{1,0:T(8,128)(2,1)}, u32[]{:S(2)}, u32[]{:S(2)}) collective-permute-start(bf16[272,768]{1,0:T(8,128)(2,1)S(1)} %collective-permute-done.refs_0_), channel_id=1, source_target_pairs={{0,8},{8,0},{16,24},{24,16},{1,9},{9,1},{17,25},{25,17},{2,10},{10... | collective-permute-start | bytes 1253384 | tf_op jit(solution)/shard_map/ppermute | solution.py:27
  28.5 9.6 %collective-permute-start.6 = (bf16[272,768]{1,0:T(8,128)(2,1)S(1)}, bf16[272,768]{1,0:T(8,128)(2,1)}, u32[]{:S(2)}, u32[]{:S(2)}) collective-permute-start(bf16[272,768]{1,0:T(8,128)(2,1)S(1)} %collective-permute-done.4.refs_4_), channel_id=1, source_target_pairs={{0,8},{8,0},{16,24},{24,16},{1,9},{9,1},{17,25},{25,17},{2,10},{10... | collective-permute-start | bytes 1253384 | tf_op jit(solution)/shard_map/ppermute | solution.py:27
  37.4 2.5 %collective-permute-start.3 = (bf16[272,768]{1,0:T(8,128)(2,1)S(1)}, bf16[272,768]{1,0:T(8,128)(2,1)}, u32[]{:S(2)}, u32[]{:S(2)}) collective-permute-start(bf16[272,768]{1,0:T(8,128)(2,1)S(1)} %collective-permute-done.1.refs_1_), channel_id=1, source_target_pairs={{0,8},{8,0},{16,24},{24,16},{1,9},{9,1},{17,25},{25,17},{2,10},{10... | collective-permute-start | bytes 1253384 | tf_op jit(solution)/shard_map/ppermute | solution.py:27
  62.5 2.4 %collective-permute-start.15 = (bf16[544,768]{1,0:T(8,128)(2,1)S(1)}, bf16[544,768]{1,0:T(8,128)(2,1)S(1)}, u32[]{:S(2)}, u32[]{:S(2)}) collective-permute-start(bf16[544,768]{1,0:T(8,128)(2,1)S(1)} %get-tuple-element.42), channel_id=1, source_target_pairs={{0,8},{8,0},{16,24},{24,16},{1,9},{9,1},{17,25},{25,17},{2,10},{10... | collective-permute-start | bytes 2506760 | tf_op jit(solution)/shard_map/ppermute | solution.py:27
  62.7 4.4 %collective-permute-start.9 = (bf16[544,768]{1,0:T(8,128)(2,1)S(1)}, bf16[544,768]{1,0:T(8,128)(2,1)S(1)}, u32[]{:S(2)}, u32[]{:S(2)}) collective-permute-start(bf16[544,768]{1,0:T(8,128)(2,1)S(1)} %get-tuple-element.37), channel_id=1, source_target_pairs={{0,8},{8,0},{16,24},{24,16},{1,9},{9,1},{17,25},{25,17},{2,10},{10... | collective-permute-start | bytes 2506760 | tf_op jit(solution)/shard_map/ppermute | solution.py:27
  63.1 15.7 %collective-permute-start.8 = (bf16[544,768]{1,0:T(8,128)(2,1)S(1)}, bf16[544,768]{1,0:T(8,128)(2,1)S(1)}, u32[]{:S(2)}, u32[]{:S(2)}) collective-permute-start(bf16[544,768]{1,0:T(8,128)(2,1)S(1)} %get-tuple-element.35), channel_id=1, source_target_pairs={{0,8},{8,0},{16,24},{24,16},{1,9},{9,1},{17,25},{25,17},{2,10},{10... | collective-permute-start | bytes 2506760 | tf_op jit(solution)/shard_map/ppermute | solution.py:27
  65.6 10.1 %collective-permute-start.16 = (bf16[144,768]{1,0:T(8,128)(2,1)S(1)}, bf16[144,768]{1,0:T(8,128)(2,1)S(1)}, u32[]{:S(2)}, u32[]{:S(2)}) collective-permute-start(bf16[144,768]{1,0:T(8,128)(2,1)S(1)} %get-tuple-element.43), channel_id=1, source_target_pairs={{0,16},{8,24},{16,0},{24,8},{1,17},{9,25},{17,1},{25,9},{2,18},{10... | collective-permute-start | bytes 663560 | tf_op jit(solution)/shard_map/ppermute | solution.py:27
  67.9 7.8 %collective-permute-start.10 = (bf16[128,768]{1,0:T(8,128)(2,1)S(1)}, bf16[128,768]{1,0:T(8,128)(2,1)S(1)}, u32[]{:S(2)}, u32[]{:S(2)}) collective-permute-start(bf16[128,768]{1,0:T(8,128)(2,1)S(1)} %get-tuple-element.38), channel_id=1, source_target_pairs={{0,1},{1,0},{2,3},{3,2},{4,5},{5,4},{6,7},{7,6},{8,9},{9,8},{10,11... | collective-permute-start | bytes 589832 | tf_op jit(solution)/shard_map/ppermute | solution.py:40
  67.9 12.2 %collective-permute-start.12 = (bf16[144,768]{1,0:T(8,128)(2,1)S(1)}, bf16[144,768]{1,0:T(8,128)(2,1)S(1)}, u32[]{:S(2)}, u32[]{:S(2)}) collective-permute-start(bf16[144,768]{1,0:T(8,128)(2,1)S(1)} %get-tuple-element.39), channel_id=1, source_target_pairs={{0,1},{1,0},{2,3},{3,2},{4,5},{5,4},{6,7},{7,6},{8,9},{9,8},{10,11... | collective-permute-start | bytes 663560 | tf_op jit(solution)/shard_map/ppermute | solution.py:40
  76.3 7.6 %collective-permute-start.17 = (bf16[144,768]{1,0:T(8,128)(2,1)S(1)}, bf16[144,768]{1,0:T(8,128)(2,1)S(1)}, u32[]{:S(2)}, u32[]{:S(2)}) collective-permute-start(bf16[144,768]{1,0:T(8,128)(2,1)S(1)} %add_packets.18), channel_id=1, source_target_pairs={{2,0},{7,1},{4,2},{1,3},{6,4},{3,5},{0,6},{5,7},{10,8},{15,9},{12,... | collective-permute-start | bytes 663560 | tf_op jit(solution)/shard_map/ppermute | solution.py:55
  78.3 5.7 %collective-permute-start.14 = (bf16[128,768]{1,0:T(8,128)(2,1)S(1)}, bf16[128,768]{1,0:T(8,128)(2,1)S(1)}, u32[]{:S(2)}, u32[]{:S(2)}) collective-permute-start(bf16[128,768]{1,0:T(8,128)(2,1)S(1)} %get-tuple-element.40), channel_id=1, source_target_pairs={{0,1},{1,0},{2,3},{3,2},{4,5},{5,4},{6,7},{7,6},{8,9},{9,8},{10,11... | collective-permute-start | bytes 589832 | tf_op jit(solution)/shard_map/ppermute | solution.py:40
  78.3 7.8 %collective-permute-start.19 = (bf16[128,768]{1,0:T(8,128)(2,1)S(1)}, bf16[128,768]{1,0:T(8,128)(2,1)S(1)}, u32[]{:S(2)}, u32[]{:S(2)}) collective-permute-start(bf16[128,768]{1,0:T(8,128)(2,1)S(1)} %get-tuple-element.44), channel_id=1, source_target_pairs={{0,16},{8,24},{16,0},{24,8},{1,17},{9,25},{17,1},{25,9},{2,18},{10... | collective-permute-start | bytes 589832 | tf_op jit(solution)/shard_map/ppermute | solution.py:27
  80.8 14.4 %collective-permute-start.13 = (bf16[144,768]{1,0:T(8,128)(2,1)S(1)}, bf16[144,768]{1,0:T(8,128)(2,1)S(1)}, u32[]{:S(2)}, u32[]{:S(2)}) collective-permute-start(bf16[144,768]{1,0:T(8,128)(2,1)S(1)} %add_packets.16.refs_5_), channel_id=1, source_target_pairs={{0,16},{8,24},{16,0},{24,8},{1,17},{9,25},{17,1},{25,9},{2,18},{10... | collective-permute-start | bytes 663560 | tf_op jit(solution)/shard_map/ppermute | solution.py:27
  84.6 10.5 %collective-permute-start.18 = (bf16[144,768]{1,0:T(8,128)(2,1)S(1)}, bf16[144,768]{1,0:T(8,128)(2,1)S(1)}, u32[]{:S(2)}, u32[]{:S(2)}) collective-permute-start(bf16[144,768]{1,0:T(8,128)(2,1)S(1)} %add_packets.19), channel_id=1, source_target_pairs={{0,1},{1,0},{2,3},{3,2},{4,5},{5,4},{6,7},{7,6},{8,9},{9,8},{10,11... | collective-permute-start | bytes 663560 | tf_op jit(solution)/shard_map/ppermute | solution.py:40
  85.0 7.7 %collective-permute-start.11 = (bf16[128,768]{1,0:T(8,128)(2,1)S(1)}, bf16[128,768]{1,0:T(8,128)(2,1)S(1)}, u32[]{:S(2)}, u32[]{:S(2)}) collective-permute-start(bf16[128,768]{1,0:T(8,128)(2,1)S(1)} %add_packets.15.refs_4_), channel_id=1, source_target_pairs={{0,16},{8,24},{16,0},{24,8},{1,17},{9,25},{17,1},{25,9},{2,18},{10... | collective-permute-start | bytes 589832 | tf_op jit(solution)/shard_map/ppermute | solution.py:27
  86.7 8.4 %collective-permute-start.20 = (bf16[128,768]{1,0:T(8,128)(2,1)S(1)}, bf16[128,768]{1,0:T(8,128)(2,1)S(1)}, u32[]{:S(2)}, u32[]{:S(2)}) collective-permute-start(bf16[128,768]{1,0:T(8,128)(2,1)S(1)} %add_packets.20), channel_id=1, source_target_pairs={{0,7},{1,2},{2,1},{3,4},{4,3},{5,6},{6,5},{7,0},{8,15},{9,10},{10,... | collective-permute-start | bytes 589832 | tf_op jit(solution)/shard_map/ppermute | solution.py:45
  96.1 8.1 %collective-permute-start.26 = (bf16[272,768]{1,0:T(8,128)(2,1)S(1)}, bf16[272,768]{1,0:T(8,128)(2,1)S(1)}, u32[]{:S(2)}, u32[]{:S(2)}) collective-permute-start(bf16[272,768]{1,0:T(8,128)(2,1)S(1)} %renew.2.refs_8_.base), channel_id=1, source_target_pairs={{0,16},{8,24},{16,0},{24,8},{1,17},{9,25},{17,1},{25,9},{2,18},{10... | collective-permute-start | bytes 1253384 | tf_op jit(solution)/shard_map/ppermute | solution.py:27
  97.1 10.8 %collective-permute-start.21 = (bf16[272,768]{1,0:T(8,128)(2,1)S(1)}, bf16[272,768]{1,0:T(8,128)(2,1)S(1)}, u32[]{:S(2)}, u32[]{:S(2)}) collective-permute-start(bf16[272,768]{1,0:T(8,128)(2,1)S(1)} %renew.2.refs_8_.base), channel_id=1, source_target_pairs={{0,7},{1,2},{2,1},{3,4},{4,3},{5,6},{6,5},{7,0},{8,15},{9,10},{10,... | collective-permute-start | bytes 1253384 | tf_op jit(solution)/shard_map/ppermute | solution.py:45
  100.4 8.7 %collective-permute-start.30 = (bf16[272,768]{1,0:T(8,128)(2,1)S(1)}, bf16[272,768]{1,0:T(8,128)(2,1)S(1)}, u32[]{:S(2)}, u32[]{:S(2)}) collective-permute-start(bf16[272,768]{1,0:T(8,128)(2,1)S(1)} %renew.2.refs_8_.base), channel_id=1, source_target_pairs={{0,8},{8,0},{16,24},{24,16},{1,9},{9,1},{17,25},{25,17},{2,10},{10... | collective-permute-start | bytes 1253384 | tf_op jit(solution)/shard_map/ppermute | solution.py:27
  100.4 16.5 %collective-permute-start.25 = (bf16[272,768]{1,0:T(8,128)(2,1)S(1)}, bf16[272,768]{1,0:T(8,128)(2,1)S(1)}, u32[]{:S(2)}, u32[]{:S(2)}) collective-permute-start(bf16[272,768]{1,0:T(8,128)(2,1)S(1)} %renew.2.refs_8_.base), channel_id=1, source_target_pairs={{0,1},{1,0},{2,3},{3,2},{4,5},{5,4},{6,7},{7,6},{8,9},{9,8},{10,11... | collective-permute-start | bytes 1253384 | tf_op jit(solution)/shard_map/ppermute | solution.py:40
  104.2 21.5 %collective-permute-start.27 = (bf16[272,768]{1,0:T(8,128)(2,1)S(1)}, bf16[272,768]{1,0:T(8,128)(2,1)S(1)}, u32[]{:S(2)}, u32[]{:S(2)}) collective-permute-start(bf16[272,768]{1,0:T(8,128)(2,1)S(1)} %collective-permute-done.26.refs_9_), channel_id=1, source_target_pairs={{0,1},{1,0},{2,3},{3,2},{4,5},{5,4},{6,7},{7,6},{8,9},{9,8},{10,11... | collective-permute-start | bytes 1253384 | tf_op jit(solution)/shard_map/ppermute | solution.py:40
  108.0 17.9 %collective-permute-start.22 = (bf16[272,768]{1,0:T(8,128)(2,1)S(1)}, bf16[272,768]{1,0:T(8,128)(2,1)S(1)}, u32[]{:S(2)}, u32[]{:S(2)}) collective-permute-start(bf16[272,768]{1,0:T(8,128)(2,1)S(1)} %collective-permute-done.21.refs_0_), channel_id=1, source_target_pairs={{0,16},{8,24},{16,0},{24,8},{1,17},{9,25},{17,1},{25,9},{2,18},{10... | collective-permute-start | bytes 1253384 | tf_op jit(solution)/shard_map/ppermute | solution.py:27
  109.0 17.3 %collective-permute-start.31 = (bf16[272,768]{1,0:T(8,128)(2,1)S(1)}, bf16[272,768]{1,0:T(8,128)(2,1)S(1)}, u32[]{:S(2)}, u32[]{:S(2)}) collective-permute-start(bf16[272,768]{1,0:T(8,128)(2,1)S(1)} %collective-permute-done.26.refs_9_), channel_id=1, source_target_pairs={{0,8},{8,0},{16,24},{24,16},{1,9},{9,1},{17,25},{25,17},{2,10},{10... | collective-permute-start | bytes 1253384 | tf_op jit(solution)/shard_map/ppermute | solution.py:27
  109.0 17.3 %collective-permute-start.23 = (bf16[272,768]{1,0:T(8,128)(2,1)S(1)}, bf16[272,768]{1,0:T(8,128)(2,1)S(1)}, u32[]{:S(2)}, u32[]{:S(2)}) collective-permute-start(bf16[272,768]{1,0:T(8,128)(2,1)S(1)} %collective-permute-done.21.refs_0_), channel_id=1, source_target_pairs={{0,8},{8,0},{16,24},{24,16},{1,9},{9,1},{17,25},{25,17},{2,10},{10... | collective-permute-start | bytes 1253384 | tf_op jit(solution)/shard_map/ppermute | solution.py:27
  116.9 9.4 %collective-permute-start.28 = (bf16[272,768]{1,0:T(8,128)(2,1)S(1)}, bf16[272,768]{1,0:T(8,128)(2,1)S(1)}, u32[]{:S(2)}, u32[]{:S(2)}) collective-permute-start(bf16[272,768]{1,0:T(8,128)(2,1)S(1)} %collective-permute-done.25.refs_4_), channel_id=1, source_target_pairs={{0,8},{8,0},{16,24},{24,16},{1,9},{9,1},{17,25},{25,17},{2,10},{10... | collective-permute-start | bytes 1253384 | tf_op jit(solution)/shard_map/ppermute | solution.py:27
  125.9 2.3 %collective-permute-start.24 = (bf16[272,768]{1,0:T(8,128)(2,1)S(1)}, bf16[272,768]{1,0:T(8,128)(2,1)S(1)}, u32[]{:S(2)}, u32[]{:S(2)}) collective-permute-start(bf16[272,768]{1,0:T(8,128)(2,1)S(1)} %collective-permute-done.22.refs_1_), channel_id=1, source_target_pairs={{0,8},{8,0},{16,24},{24,16},{1,9},{9,1},{17,25},{25,17},{2,10},{10... | collective-permute-start | bytes 1253384 | tf_op jit(solution)/shard_map/ppermute | solution.py:27
  151.8 2.4 %collective-permute-start.39 = (bf16[544,768]{1,0:T(8,128)(2,1)S(1)}, bf16[544,768]{1,0:T(8,128)(2,1)S(1)}, u32[]{:S(2)}, u32[]{:S(2)}) collective-permute-start(bf16[544,768]{1,0:T(8,128)(2,1)S(1)} %get-tuple-element.53), channel_id=1, source_target_pairs={{0,8},{8,0},{16,24},{24,16},{1,9},{9,1},{17,25},{25,17},{2,10},{10... | collective-permute-start | bytes 2506760 | tf_op jit(solution)/shard_map/ppermute | solution.py:27
  152.0 3.6 %collective-permute-start.33 = (bf16[544,768]{1,0:T(8,128)(2,1)S(1)}, bf16[544,768]{1,0:T(8,128)(2,1)S(1)}, u32[]{:S(2)}, u32[]{:S(2)}) collective-permute-start(bf16[544,768]{1,0:T(8,128)(2,1)S(1)} %get-tuple-element.48), channel_id=1, source_target_pairs={{0,8},{8,0},{16,24},{24,16},{1,9},{9,1},{17,25},{25,17},{2,10},{10... | collective-permute-start | bytes 2506760 | tf_op jit(solution)/shard_map/ppermute | solution.py:27
  152.4 15.1 %collective-permute-start.32 = (bf16[544,768]{1,0:T(8,128)(2,1)S(1)}, bf16[544,768]{1,0:T(8,128)(2,1)S(1)}, u32[]{:S(2)}, u32[]{:S(2)}) collective-permute-start(bf16[544,768]{1,0:T(8,128)(2,1)S(1)} %get-tuple-element.46), channel_id=1, source_target_pairs={{0,8},{8,0},{16,24},{24,16},{1,9},{9,1},{17,25},{25,17},{2,10},{10... | collective-permute-start | bytes 2506760 | tf_op jit(solution)/shard_map/ppermute | solution.py:27
  154.9 9.3 %collective-permute-start.40 = (bf16[144,768]{1,0:T(8,128)(2,1)S(1)}, bf16[144,768]{1,0:T(8,128)(2,1)S(1)}, u32[]{:S(2)}, u32[]{:S(2)}) collective-permute-start(bf16[144,768]{1,0:T(8,128)(2,1)S(1)} %get-tuple-element.54), channel_id=1, source_target_pairs={{0,16},{8,24},{16,0},{24,8},{1,17},{9,25},{17,1},{25,9},{2,18},{10... | collective-permute-start | bytes 663560 | tf_op jit(solution)/shard_map/ppermute | solution.py:27
  156.3 7.8 %collective-permute-start.34 = (bf16[128,768]{1,0:T(8,128)(2,1)S(1)}, bf16[128,768]{1,0:T(8,128)(2,1)S(1)}, u32[]{:S(2)}, u32[]{:S(2)}) collective-permute-start(bf16[128,768]{1,0:T(8,128)(2,1)S(1)} %get-tuple-element.49), channel_id=1, source_target_pairs={{0,1},{1,0},{2,3},{3,2},{4,5},{5,4},{6,7},{7,6},{8,9},{9,8},{10,11... | collective-permute-start | bytes 589832 | tf_op jit(solution)/shard_map/ppermute | solution.py:40
  156.4 12.0 %collective-permute-start.36 = (bf16[144,768]{1,0:T(8,128)(2,1)S(1)}, bf16[144,768]{1,0:T(8,128)(2,1)S(1)}, u32[]{:S(2)}, u32[]{:S(2)}) collective-permute-start(bf16[144,768]{1,0:T(8,128)(2,1)S(1)} %get-tuple-element.50), channel_id=1, source_target_pairs={{0,1},{1,0},{2,3},{3,2},{4,5},{5,4},{6,7},{7,6},{8,9},{9,8},{10,11... | collective-permute-start | bytes 663560 | tf_op jit(solution)/shard_map/ppermute | solution.py:40
  164.8 7.3 %collective-permute-start.41 = (bf16[144,768]{1,0:T(8,128)(2,1)S(1)}, bf16[144,768]{1,0:T(8,128)(2,1)S(1)}, u32[]{:S(2)}, u32[]{:S(2)}) collective-permute-start(bf16[144,768]{1,0:T(8,128)(2,1)S(1)} %add_packets.25), channel_id=1, source_target_pairs={{2,0},{7,1},{4,2},{1,3},{6,4},{3,5},{0,6},{5,7},{10,8},{15,9},{12,... | collective-permute-start | bytes 663560 | tf_op jit(solution)/shard_map/ppermute | solution.py:55
  166.4 5.7 %collective-permute-start.38 = (bf16[128,768]{1,0:T(8,128)(2,1)S(1)}, bf16[128,768]{1,0:T(8,128)(2,1)S(1)}, u32[]{:S(2)}, u32[]{:S(2)}) collective-permute-start(bf16[128,768]{1,0:T(8,128)(2,1)S(1)} %get-tuple-element.51), channel_id=1, source_target_pairs={{0,1},{1,0},{2,3},{3,2},{4,5},{5,4},{6,7},{7,6},{8,9},{9,8},{10,11... | collective-permute-start | bytes 589832 | tf_op jit(solution)/shard_map/ppermute | solution.py:40
  166.4 8.2 %collective-permute-start.43 = (bf16[128,768]{1,0:T(8,128)(2,1)S(1)}, bf16[128,768]{1,0:T(8,128)(2,1)S(1)}, u32[]{:S(2)}, u32[]{:S(2)}) collective-permute-start(bf16[128,768]{1,0:T(8,128)(2,1)S(1)} %get-tuple-element.55), channel_id=1, source_target_pairs={{0,16},{8,24},{16,0},{24,8},{1,17},{9,25},{17,1},{25,9},{2,18},{10... | collective-permute-start | bytes 589832 | tf_op jit(solution)/shard_map/ppermute | solution.py:27
  169.1 14.6 %collective-permute-start.37 = (bf16[144,768]{1,0:T(8,128)(2,1)S(1)}, bf16[144,768]{1,0:T(8,128)(2,1)S(1)}, u32[]{:S(2)}, u32[]{:S(2)}) collective-permute-start(bf16[144,768]{1,0:T(8,128)(2,1)S(1)} %add_packets.23.refs_5_), channel_id=1, source_target_pairs={{0,16},{8,24},{16,0},{24,8},{1,17},{9,25},{17,1},{25,9},{2,18},{10... | collective-permute-start | bytes 663560 | tf_op jit(solution)/shard_map/ppermute | solution.py:27
  172.7 10.9 %collective-permute-start.42 = (bf16[144,768]{1,0:T(8,128)(2,1)S(1)}, bf16[144,768]{1,0:T(8,128)(2,1)S(1)}, u32[]{:S(2)}, u32[]{:S(2)}) collective-permute-start(bf16[144,768]{1,0:T(8,128)(2,1)S(1)} %add_packets.26), channel_id=1, source_target_pairs={{0,1},{1,0},{2,3},{3,2},{4,5},{5,4},{6,7},{7,6},{8,9},{9,8},{10,11... | collective-permute-start | bytes 663560 | tf_op jit(solution)/shard_map/ppermute | solution.py:40
  173.3 7.7 %collective-permute-start.35 = (bf16[128,768]{1,0:T(8,128)(2,1)S(1)}, bf16[128,768]{1,0:T(8,128)(2,1)S(1)}, u32[]{:S(2)}, u32[]{:S(2)}) collective-permute-start(bf16[128,768]{1,0:T(8,128)(2,1)S(1)} %add_packets.22.refs_4_), channel_id=1, source_target_pairs={{0,16},{8,24},{16,0},{24,8},{1,17},{9,25},{17,1},{25,9},{2,18},{10... | collective-permute-start | bytes 589832 | tf_op jit(solution)/shard_map/ppermute | solution.py:27
  175.2 8.4 %collective-permute-start.44 = (bf16[128,768]{1,0:T(8,128)(2,1)S(1)}, bf16[128,768]{1,0:T(8,128)(2,1)S(1)}, u32[]{:S(2)}, u32[]{:S(2)}) collective-permute-start(bf16[128,768]{1,0:T(8,128)(2,1)S(1)} %add_packets.27), channel_id=1, source_target_pairs={{0,7},{1,2},{2,1},{3,4},{4,3},{5,6},{6,5},{7,0},{8,15},{9,10},{10,... | collective-permute-start | bytes 589832 | tf_op jit(solution)/shard_map/ppermute | solution.py:45
  184.6 6.1 %collective-permute-start.46 = (bf16[144,768]{1,0:T(8,128)(2,1)S(1)}, bf16[144,768]{1,0:T(8,128)(2,1)S(1)}, u32[]{:S(2)}, u32[]{:S(2)}) collective-permute-start(bf16[144,768]{1,0:T(8,128)(2,1)S(1)} %get-tuple-element.57.refs_1_), channel_id=1, source_target_pairs={{0,16},{8,24},{16,0},{24,8},{1,17},{9,25},{17,1},{25,9},{2,18},{10... | collective-permute-start | bytes 663560 | tf_op jit(solution)/shard_map/ppermute | solution.py:27
  185.5 7.3 %collective-permute-start.45 = (bf16[128,768]{1,0:T(8,128)(2,1)S(1)}, bf16[128,768]{1,0:T(8,128)(2,1)S(1)}, u32[]{:S(2)}, u32[]{:S(2)}) collective-permute-start(bf16[128,768]{1,0:T(8,128)(2,1)S(1)} %get-tuple-element.56.refs_0_), channel_id=1, source_target_pairs={{0,16},{8,24},{16,0},{24,8},{1,17},{9,25},{17,1},{25,9},{2,18},{10... | collective-permute-start | bytes 589832 | tf_op jit(solution)/shard_map/ppermute | solution.py:27
  186.7 6.1 %collective-permute-start.48 = (bf16[144,768]{1,0:T(8,128)(2,1)S(1)}, bf16[144,768]{1,0:T(8,128)(2,1)S(1)}, u32[]{:S(2)}, u32[]{:S(2)}) collective-permute-start(bf16[144,768]{1,0:T(8,128)(2,1)S(1)} %get-tuple-element.57.refs_1_), channel_id=1, source_target_pairs={{0,8},{8,0},{16,24},{24,16},{1,9},{9,1},{17,25},{25,17},{2,10},{10... | collective-permute-start | bytes 663560 | tf_op jit(solution)/shard_map/ppermute | solution.py:27
  190.7 3.6 %collective-permute-start.50 = (bf16[144,768]{1,0:T(8,128)(2,1)S(1)}, bf16[144,768]{1,0:T(8,128)(2,1)S(1)}, u32[]{:S(2)}, u32[]{:S(2)}) collective-permute-start(bf16[144,768]{1,0:T(8,128)(2,1)S(1)} %collective-permute-done.46.refs_3_), channel_id=1, source_target_pairs={{0,8},{8,0},{16,24},{24,16},{1,9},{9,1},{17,25},{25,17},{2,10},{10... | collective-permute-start | bytes 663560 | tf_op jit(solution)/shard_map/ppermute | solution.py:27
  190.7 2.1 %collective-permute-start.47 = (bf16[128,768]{1,0:T(8,128)(2,1)S(1)}, bf16[128,768]{1,0:T(8,128)(2,1)S(1)}, u32[]{:S(2)}, u32[]{:S(2)}) collective-permute-start(bf16[128,768]{1,0:T(8,128)(2,1)S(1)} %get-tuple-element.56.refs_0_), channel_id=1, source_target_pairs={{0,8},{8,0},{16,24},{24,16},{1,9},{9,1},{17,25},{25,17},{2,10},{10... | collective-permute-start | bytes 589832 | tf_op jit(solution)/shard_map/ppermute | solution.py:27
  (5 other events, 41.6 us)

commit v5 on v4

--- a/solution.py
+++ b/solution.py
@@ -12,7 +12,7 @@
 SLOTS = 4
 ITERS = 2
 TAIL = 16
-STEP_TILES = 8
+STEP_TILES = 16
 CHUNKS = 2
 prior_mass = 1.0
 dual_step = 0.5

time: 197 us -> 196 us (level)
  no operation moved by 1% of the time
where the time goes in v5:
time: 196 us
  waiting for transfers between devices  88 us (45%)
  Pallas kernels  61 us (31%)
  starting transfers between devices  43.1 us (22%)
  local copies, waits for them, and re-layouts  2.89 us (1%)
    ppermute x12, waiting for transfers between devices, pair_swap(): return lax.ppermute(x, 'blk', [(i, i ^ 1) for i in range(count)])  48.9 us
    pallas_call x2, Pallas kernels, assign_tiles(): pl.pallas_call(functools.partial(tiles_kernel, rows, sizes), grid_spec=pl...  45.6 us
    ppermute x33, waiting for transfers between devices, swap(): return lax.ppermute(x, 'group', [(i, i ^ bit) for i in range(groups)])  24.4 us
    ppermute x33, starting transfers between devices, swap(): return lax.ppermute(x, 'group', [(i, i ^ bit) for i in range(groups)])  17.6 us
    ppermute x4, starting transfers between devices, cross_swap(): lax.ppermute(x, 'blk', [(i, (i - 1 + i % 2 * 2) % count) for i in range(c...  14.7 us
    ppermute x4, waiting for transfers between devices, cross_swap(): lax.ppermute(x, 'blk', [(i, (i - 1 + i % 2 * 2) % count) for i in range(c...  14.7 us
    pallas_call x16, Pallas kernels, small_call(): pl.pallas_call(kernel, in_specs=[pl.BlockSpec(memory_space=pltpu.SMEM)] +...  10.9 us
    ppermute x12, starting transfers between devices, pair_swap(): return lax.ppermute(x, 'blk', [(i, i ^ 1) for i in range(count)])  7.23 us
  transfers between devices with their start and end apart: 51, of which 27 were waited for; matrix products, arithmetic and copies ran while one was open for 0% of the time, Pallas kernels for 5%

profile of v5, /device:TPU:0, one launch (start us, length us, event | category | flops | bytes accessed | tf_op | source)
XLA Modules:
  0.0 195.9 jit_solution(8696393574495692646)
XLA Ops:
  1.4 1.4 copy-done
  2.8 1.0 start_packets.2.refs_8_.base
  3.8 6.0 %collective-permute-start = (bf16[272,768]{1,0:T(8,128)(2,1)S(1)}, bf16[272,768]{1,0:T(8,128)(2,1)S(1)}, u32[]{:S(2)}, u32[]{:S(2)}) collective-permute-start(bf16[272,768]{1,0:T(8,128)(2,1)S(1)} %start_packets.2.refs_8_.base), channel_id=1, source_target_pairs={{0,7},{1,2},{2,1},{3,4},{4,3},{5,6},{6,5},{7,0},{8,15},{9,10},{10,... | collective-permute-start | bytes 1253384 | tf_op jit(solution)/shard_map/ppermute | solution.py:45
  9.8 1.7 start_packets.3
  11.6 2.1 %collective-permute-start.5 = (bf16[272,768]{1,0:T(8,128)(2,1)S(1)}, bf16[272,768]{1,0:T(8,128)(2,1)S(1)}, u32[]{:S(2)}, u32[]{:S(2)}) collective-permute-start(bf16[272,768]{1,0:T(8,128)(2,1)S(1)} %get-tuple-element.31.refs_9_), channel_id=1, source_target_pairs={{0,1},{1,0},{2,3},{3,2},{4,5},{5,4},{6,7},{7,6},{8,9},{9,8},{10,11... | collective-permute-start | bytes 1253384 | tf_op jit(solution)/shard_map/ppermute | solution.py:40
  13.7 5.9 %collective-permute-done.refs_0_ = bf16[272,768]{1,0:T(8,128)(2,1)S(1)} collective-permute-done((bf16[272,768]{1,0:T(8,128)(2,1)S(1)}, bf16[272,768]{1,0:T(8,128)(2,1)S(1)}, u32[]{:S(2)}, u32[]{:S(2)}) %collective-permute-start) | collective-permute-done | bytes 417824 | tf_op jit(solution)/shard_map/ppermute | solution.py:45
  19.6 1.5 collective-permute-start.1
  21.1 7.4 %collective-permute-done.4.refs_4_ = bf16[272,768]{1,0:T(8,128)(2,1)S(1)} collective-permute-done((bf16[272,768]{1,0:T(8,128)(2,1)S(1)}, bf16[272,768]{1,0:T(8,128)(2,1)S(1)}, u32[]{:S(2)}, u32[]{:S(2)}) %collective-permute-start.4) | collective-permute-done | bytes 417824 | tf_op jit(solution)/shard_map/ppermute | solution.py:40
  28.5 8.9 %collective-permute-done.5.refs_5_ = bf16[272,768]{1,0:T(8,128)(2,1)S(1)} collective-permute-done((bf16[272,768]{1,0:T(8,128)(2,1)S(1)}, bf16[272,768]{1,0:T(8,128)(2,1)S(1)}, u32[]{:S(2)}, u32[]{:S(2)}) %collective-permute-start.5) | collective-permute-done | bytes 417824 | tf_op jit(solution)/shard_map/ppermute | solution.py:40
  38.1 1.1 collective-permute-done.7.refs_7_
  39.9 22.3 %tiles.2 = (bf16[544,768]{1,0:T(8,128)(2,1)S(1)}, bf16[544,768]{1,0:T(8,128)(2,1)S(1)}, bf16[544,768]{1,0:T(8,128)(2,1)S(1)}, f32[544,768]{1,0:T(8,128)S(1)}, f3...) custom-call(s32[256]{0:T(256)S(1)} %reshape.14.ids_ref, s32[2]{0:T(128)S(1)} %pad_add_fusion.me_ref, ...), custom_call_target="tpu_custom_call" | custom-call | flops 6442450944 | bytes 12582912 | tf_op jit(solution)/shard_map/tiles/pallas_call | solution.py:275
  62.9 1.7 collective-permute-done.15.refs_1_
  65.2 1.6 collective-permute-start.16
  67.6 2.0 %collective-permute-start.12 = (bf16[144,768]{1,0:T(8,128)(2,1)S(1)}, bf16[144,768]{1,0:T(8,128)(2,1)S(1)}, u32[]{:S(2)}, u32[]{:S(2)}) collective-permute-start(bf16[144,768]{1,0:T(8,128)(2,1)S(1)} %get-tuple-element.39), channel_id=1, source_target_pairs={{0,1},{1,0},{2,3},{3,2},{4,5},{5,4},{6,7},{7,6},{8,9},{9,8},{10,11... | collective-permute-start | bytes 663560 | tf_op jit(solution)/shard_map/ppermute | solution.py:40
  69.6 5.8 %collective-permute-done.10.refs_2_.refs_3_ = bf16[128,768]{1,0:T(8,128)(2,1)S(1)} collective-permute-done((bf16[128,768]{1,0:T(8,128)(2,1)S(1)}, bf16[128,768]{1,0:T(8,128)(2,1)S(1)}, u32[]{:S(2)}, u32[]{:S(2)}) %collective-permute-start.10) | collective-permute-done | bytes 196640 | tf_op jit(solution)/shard_map/ppermute | solution.py:40
  76.0 1.9 collective-permute-start.17
  81.3 2.3 %collective-permute-done.14.refs_3_.refs_2_ = bf16[128,768]{1,0:T(8,128)(2,1)S(1)} collective-permute-done((bf16[128,768]{1,0:T(8,128)(2,1)S(1)}, bf16[128,768]{1,0:T(8,128)(2,1)S(1)}, u32[]{:S(2)}, u32[]{:S(2)}) %collective-permute-start.14) | collective-permute-done | bytes 196640 | tf_op jit(solution)/shard_map/ppermute | solution.py:40
  84.6 0.9 collective-permute-start.11
  86.3 2.7 %collective-permute-start.20 = (bf16[128,768]{1,0:T(8,128)(2,1)S(1)}, bf16[128,768]{1,0:T(8,128)(2,1)S(1)}, u32[]{:S(2)}, u32[]{:S(2)}) collective-permute-start(bf16[128,768]{1,0:T(8,128)(2,1)S(1)} %add_packets.20), channel_id=1, source_target_pairs={{0,7},{1,2},{2,1},{3,4},{4,3},{5,6},{6,5},{7,0},{8,15},{9,10},{10,... | collective-permute-start | bytes 589832 | tf_op jit(solution)/shard_map/ppermute | solution.py:45
  89.0 3.3 %collective-permute-done.11.refs_0_ = bf16[128,768]{1,0:T(8,128)(2,1)S(1)} collective-permute-done((bf16[128,768]{1,0:T(8,128)(2,1)S(1)}, bf16[128,768]{1,0:T(8,128)(2,1)S(1)}, u32[]{:S(2)}, u32[]{:S(2)}) %collective-permute-start.11) | collective-permute-done | bytes 196640 | tf_op jit(solution)/shard_map/ppermute | solution.py:27
  92.3 2.4 %collective-permute-done.20.refs_4_ = bf16[128,768]{1,0:T(8,128)(2,1)S(1)} collective-permute-done((bf16[128,768]{1,0:T(8,128)(2,1)S(1)}, bf16[128,768]{1,0:T(8,128)(2,1)S(1)}, u32[]{:S(2)}, u32[]{:S(2)}) %collective-permute-start.20) | collective-permute-done | bytes 196640 | tf_op jit(solution)/shard_map/ppermute | solution.py:45
  94.8 1.0 renew.2.refs_8_.base
  95.8 1.0 collective-permute-start.26
  96.8 3.2 %collective-permute-start.21 = (bf16[272,768]{1,0:T(8,128)(2,1)S(1)}, bf16[272,768]{1,0:T(8,128)(2,1)S(1)}, u32[]{:S(2)}, u32[]{:S(2)}) collective-permute-start(bf16[272,768]{1,0:T(8,128)(2,1)S(1)} %renew.2.refs_8_.base), channel_id=1, source_target_pairs={{0,7},{1,2},{2,1},{3,4},{4,3},{5,6},{6,5},{7,0},{8,15},{9,10},{10,... | collective-permute-start | bytes 1253384 | tf_op jit(solution)/shard_map/ppermute | solution.py:45
  100.0 3.9 %collective-permute-done.26.refs_9_ = bf16[272,768]{1,0:T(8,128)(2,1)S(1)} collective-permute-done((bf16[272,768]{1,0:T(8,128)(2,1)S(1)}, bf16[272,768]{1,0:T(8,128)(2,1)S(1)}, u32[]{:S(2)}, u32[]{:S(2)}) %collective-permute-start.26) | collective-permute-done | bytes 417824 | tf_op jit(solution)/shard_map/ppermute | solution.py:27
  103.9 3.7 %collective-permute-done.21.refs_0_ = bf16[272,768]{1,0:T(8,128)(2,1)S(1)} collective-permute-done((bf16[272,768]{1,0:T(8,128)(2,1)S(1)}, bf16[272,768]{1,0:T(8,128)(2,1)S(1)}, u32[]{:S(2)}, u32[]{:S(2)}) %collective-permute-start.21) | collective-permute-done | bytes 417824 | tf_op jit(solution)/shard_map/ppermute | solution.py:45
  107.6 1.0 collective-permute-start.22
  109.2 7.3 %collective-permute-done.25.refs_4_ = bf16[272,768]{1,0:T(8,128)(2,1)S(1)} collective-permute-done((bf16[272,768]{1,0:T(8,128)(2,1)S(1)}, bf16[272,768]{1,0:T(8,128)(2,1)S(1)}, u32[]{:S(2)}, u32[]{:S(2)}) %collective-permute-start.25) | collective-permute-done | bytes 417824 | tf_op jit(solution)/shard_map/ppermute | solution.py:40
  116.5 8.9 %collective-permute-done.27.refs_5_ = bf16[272,768]{1,0:T(8,128)(2,1)S(1)} collective-permute-done((bf16[272,768]{1,0:T(8,128)(2,1)S(1)}, bf16[272,768]{1,0:T(8,128)(2,1)S(1)}, u32[]{:S(2)}, u32[]{:S(2)}) %collective-permute-start.27) | collective-permute-done | bytes 417824 | tf_op jit(solution)/shard_map/ppermute | solution.py:40
  126.0 1.2 collective-permute-done.29.refs_7_
  127.8 23.3 %tiles.3 = (bf16[544,768]{1,0:T(8,128)(2,1)S(1)}, bf16[544,768]{1,0:T(8,128)(2,1)S(1)}, bf16[544,768]{1,0:T(8,128)(2,1)S(1)}, f32[544,768]{1,0:T(8,128)S(1)}, f3...) custom-call(s32[256]{0:T(256)S(1)} %reshape.14.ids_ref, s32[2]{0:T(128)S(1)} %pad_add_fusion.me_ref, ...), custom_call_target="tpu_custom_call" | custom-call | flops 6442450944 | bytes 12582912 | tf_op jit(solution)/shard_map/tiles/pallas_call | solution.py:275
  151.8 1.7 collective-permute-done.39.refs_1_
  155.7 2.0 %collective-permute-start.36 = (bf16[144,768]{1,0:T(8,128)(2,1)S(1)}, bf16[144,768]{1,0:T(8,128)(2,1)S(1)}, u32[]{:S(2)}, u32[]{:S(2)}) collective-permute-start(bf16[144,768]{1,0:T(8,128)(2,1)S(1)} %get-tuple-element.50), channel_id=1, source_target_pairs={{0,1},{1,0},{2,3},{3,2},{4,5},{5,4},{6,7},{7,6},{8,9},{9,8},{10,11... | collective-permute-start | bytes 663560 | tf_op jit(solution)/shard_map/ppermute | solution.py:40
  157.7 5.7 %collective-permute-done.34.refs_2_.refs_3_ = bf16[128,768]{1,0:T(8,128)(2,1)S(1)} collective-permute-done((bf16[128,768]{1,0:T(8,128)(2,1)S(1)}, bf16[128,768]{1,0:T(8,128)(2,1)S(1)}, u32[]{:S(2)}, u32[]{:S(2)}) %collective-permute-start.34) | collective-permute-done | bytes 196640 | tf_op jit(solution)/shard_map/ppermute | solution.py:40
  164.1 1.6 collective-permute-start.41
  165.7 1.0 collective-permute-start.43
  168.3 1.5 collective-permute-start.37
  169.9 1.5 collective-permute-done.38.refs_3_.refs_2_
  172.6 1.3 collective-permute-start.35
  174.5 2.8 %collective-permute-start.44 = (bf16[128,768]{1,0:T(8,128)(2,1)S(1)}, bf16[128,768]{1,0:T(8,128)(2,1)S(1)}, u32[]{:S(2)}, u32[]{:S(2)}) collective-permute-start(bf16[128,768]{1,0:T(8,128)(2,1)S(1)} %add_packets.27), channel_id=1, source_target_pairs={{0,7},{1,2},{2,1},{3,4},{4,3},{5,6},{6,5},{7,0},{8,15},{9,10},{10,... | collective-permute-start | bytes 589832 | tf_op jit(solution)/shard_map/ppermute | solution.py:45
  177.3 3.0 %collective-permute-done.35.refs_0_ = bf16[128,768]{1,0:T(8,128)(2,1)S(1)} collective-permute-done((bf16[128,768]{1,0:T(8,128)(2,1)S(1)}, bf16[128,768]{1,0:T(8,128)(2,1)S(1)}, u32[]{:S(2)}, u32[]{:S(2)}) %collective-permute-start.35) | collective-permute-done | bytes 196640 | tf_op jit(solution)/shard_map/ppermute | solution.py:27
  180.3 2.6 %collective-permute-done.44.refs_4_ = bf16[128,768]{1,0:T(8,128)(2,1)S(1)} collective-permute-done((bf16[128,768]{1,0:T(8,128)(2,1)S(1)}, bf16[128,768]{1,0:T(8,128)(2,1)S(1)}, u32[]{:S(2)}, u32[]{:S(2)}) %collective-permute-start.44) | collective-permute-done | bytes 196640 | tf_op jit(solution)/shard_map/ppermute | solution.py:45
  182.9 1.0 renew.3
  184.8 1.3 collective-permute-start.45
  186.0 4.0 %collective-permute-done.46.refs_3_ = bf16[144,768]{1,0:T(8,128)(2,1)S(1)} collective-permute-done((bf16[144,768]{1,0:T(8,128)(2,1)S(1)}, bf16[144,768]{1,0:T(8,128)(2,1)S(1)}, u32[]{:S(2)}, u32[]{:S(2)}) %collective-permute-start.46) | collective-permute-done | bytes 221216 | tf_op jit(solution)/shard_map/ppermute | solution.py:27
  190.5 1.6 collective-permute-done.45.refs_2_
  192.1 1.4 collective-permute-done.49.refs_6_
  193.6 1.8 finish.1
  (85 shorter events, 20.6 us)
Async XLA Ops:
  3.8 15.8 %collective-permute-start = (bf16[272,768]{1,0:T(8,128)(2,1)S(1)}, bf16[272,768]{1,0:T(8,128)(2,1)S(1)}, u32[]{:S(2)}, u32[]{:S(2)}) collective-permute-start(bf16[272,768]{1,0:T(8,128)(2,1)S(1)} %start_packets.2.refs_8_.base), channel_id=1, source_target_pairs={{0,7},{1,2},{2,1},{3,4},{4,3},{5,6},{6,5},{7,0},{8,15},{9,10},{10,... | collective-permute-start | bytes 1253384 | tf_op jit(solution)/shard_map/ppermute | solution.py:45
  9.8 18.7 %collective-permute-start.4 = (bf16[272,768]{1,0:T(8,128)(2,1)S(1)}, bf16[272,768]{1,0:T(8,128)(2,1)S(1)}, u32[]{:S(2)}, u32[]{:S(2)}) collective-permute-start(bf16[272,768]{1,0:T(8,128)(2,1)S(1)} %start_packets.2.refs_8_.base), channel_id=1, source_target_pairs={{0,1},{1,0},{2,3},{3,2},{4,5},{5,4},{6,7},{7,6},{8,9},{9,8},{10,11... | collective-permute-start | bytes 1253384 | tf_op jit(solution)/shard_map/ppermute | solution.py:40
  11.6 25.8 %collective-permute-start.5 = (bf16[272,768]{1,0:T(8,128)(2,1)S(1)}, bf16[272,768]{1,0:T(8,128)(2,1)S(1)}, u32[]{:S(2)}, u32[]{:S(2)}) collective-permute-start(bf16[272,768]{1,0:T(8,128)(2,1)S(1)} %get-tuple-element.31.refs_9_), channel_id=1, source_target_pairs={{0,1},{1,0},{2,3},{3,2},{4,5},{5,4},{6,7},{7,6},{8,9},{9,8},{10,11... | collective-permute-start | bytes 1253384 | tf_op jit(solution)/shard_map/ppermute | solution.py:40
  19.6 17.8 %collective-permute-start.1 = (bf16[272,768]{1,0:T(8,128)(2,1)S(1)}, bf16[272,768]{1,0:T(8,128)(2,1)S(1)}, u32[]{:S(2)}, u32[]{:S(2)}) collective-permute-start(bf16[272,768]{1,0:T(8,128)(2,1)S(1)} %collective-permute-done.refs_0_), channel_id=1, source_target_pairs={{0,16},{8,24},{16,0},{24,8},{1,17},{9,25},{17,1},{25,9},{2,18},{10... | collective-permute-start | bytes 1253384 | tf_op jit(solution)/shard_map/ppermute | solution.py:27
  21.1 17.0 %collective-permute-start.2 = (bf16[272,768]{1,0:T(8,128)(2,1)S(1)}, bf16[272,768]{1,0:T(8,128)(2,1)}, u32[]{:S(2)}, u32[]{:S(2)}) collective-permute-start(bf16[272,768]{1,0:T(8,128)(2,1)S(1)} %collective-permute-done.refs_0_), channel_id=1, source_target_pairs={{0,8},{8,0},{16,24},{24,16},{1,9},{9,1},{17,25},{25,17},{2,10},{10... | collective-permute-start | bytes 1253384 | tf_op jit(solution)/shard_map/ppermute | solution.py:27
  28.5 9.6 %collective-permute-start.6 = (bf16[272,768]{1,0:T(8,128)(2,1)S(1)}, bf16[272,768]{1,0:T(8,128)(2,1)}, u32[]{:S(2)}, u32[]{:S(2)}) collective-permute-start(bf16[272,768]{1,0:T(8,128)(2,1)S(1)} %collective-permute-done.4.refs_4_), channel_id=1, source_target_pairs={{0,8},{8,0},{16,24},{24,16},{1,9},{9,1},{17,25},{25,17},{2,10},{10... | collective-permute-start | bytes 1253384 | tf_op jit(solution)/shard_map/ppermute | solution.py:27
  37.4 2.5 %collective-permute-start.3 = (bf16[272,768]{1,0:T(8,128)(2,1)S(1)}, bf16[272,768]{1,0:T(8,128)(2,1)}, u32[]{:S(2)}, u32[]{:S(2)}) collective-permute-start(bf16[272,768]{1,0:T(8,128)(2,1)S(1)} %collective-permute-done.1.refs_1_), channel_id=1, source_target_pairs={{0,8},{8,0},{16,24},{24,16},{1,9},{9,1},{17,25},{25,17},{2,10},{10... | collective-permute-start | bytes 1253384 | tf_op jit(solution)/shard_map/ppermute | solution.py:27
  62.2 2.4 %collective-permute-start.15 = (bf16[544,768]{1,0:T(8,128)(2,1)S(1)}, bf16[544,768]{1,0:T(8,128)(2,1)S(1)}, u32[]{:S(2)}, u32[]{:S(2)}) collective-permute-start(bf16[544,768]{1,0:T(8,128)(2,1)S(1)} %get-tuple-element.42), channel_id=1, source_target_pairs={{0,8},{8,0},{16,24},{24,16},{1,9},{9,1},{17,25},{25,17},{2,10},{10... | collective-permute-start | bytes 2506760 | tf_op jit(solution)/shard_map/ppermute | solution.py:27
  62.4 4.4 %collective-permute-start.9 = (bf16[544,768]{1,0:T(8,128)(2,1)S(1)}, bf16[544,768]{1,0:T(8,128)(2,1)S(1)}, u32[]{:S(2)}, u32[]{:S(2)}) collective-permute-start(bf16[544,768]{1,0:T(8,128)(2,1)S(1)} %get-tuple-element.37), channel_id=1, source_target_pairs={{0,8},{8,0},{16,24},{24,16},{1,9},{9,1},{17,25},{25,17},{2,10},{10... | collective-permute-start | bytes 2506760 | tf_op jit(solution)/shard_map/ppermute | solution.py:27
  62.7 15.7 %collective-permute-start.8 = (bf16[544,768]{1,0:T(8,128)(2,1)S(1)}, bf16[544,768]{1,0:T(8,128)(2,1)S(1)}, u32[]{:S(2)}, u32[]{:S(2)}) collective-permute-start(bf16[544,768]{1,0:T(8,128)(2,1)S(1)} %get-tuple-element.35), channel_id=1, source_target_pairs={{0,8},{8,0},{16,24},{24,16},{1,9},{9,1},{17,25},{25,17},{2,10},{10... | collective-permute-start | bytes 2506760 | tf_op jit(solution)/shard_map/ppermute | solution.py:27
  65.2 10.1 %collective-permute-start.16 = (bf16[144,768]{1,0:T(8,128)(2,1)S(1)}, bf16[144,768]{1,0:T(8,128)(2,1)S(1)}, u32[]{:S(2)}, u32[]{:S(2)}) collective-permute-start(bf16[144,768]{1,0:T(8,128)(2,1)S(1)} %get-tuple-element.43), channel_id=1, source_target_pairs={{0,16},{8,24},{16,0},{24,8},{1,17},{9,25},{17,1},{25,9},{2,18},{10... | collective-permute-start | bytes 663560 | tf_op jit(solution)/shard_map/ppermute | solution.py:27
  67.5 7.9 %collective-permute-start.10 = (bf16[128,768]{1,0:T(8,128)(2,1)S(1)}, bf16[128,768]{1,0:T(8,128)(2,1)S(1)}, u32[]{:S(2)}, u32[]{:S(2)}) collective-permute-start(bf16[128,768]{1,0:T(8,128)(2,1)S(1)} %get-tuple-element.38), channel_id=1, source_target_pairs={{0,1},{1,0},{2,3},{3,2},{4,5},{5,4},{6,7},{7,6},{8,9},{9,8},{10,11... | collective-permute-start | bytes 589832 | tf_op jit(solution)/shard_map/ppermute | solution.py:40
  67.6 12.2 %collective-permute-start.12 = (bf16[144,768]{1,0:T(8,128)(2,1)S(1)}, bf16[144,768]{1,0:T(8,128)(2,1)S(1)}, u32[]{:S(2)}, u32[]{:S(2)}) collective-permute-start(bf16[144,768]{1,0:T(8,128)(2,1)S(1)} %get-tuple-element.39), channel_id=1, source_target_pairs={{0,1},{1,0},{2,3},{3,2},{4,5},{5,4},{6,7},{7,6},{8,9},{9,8},{10,11... | collective-permute-start | bytes 663560 | tf_op jit(solution)/shard_map/ppermute | solution.py:40
  76.0 7.6 %collective-permute-start.17 = (bf16[144,768]{1,0:T(8,128)(2,1)S(1)}, bf16[144,768]{1,0:T(8,128)(2,1)S(1)}, u32[]{:S(2)}, u32[]{:S(2)}) collective-permute-start(bf16[144,768]{1,0:T(8,128)(2,1)S(1)} %add_packets.18), channel_id=1, source_target_pairs={{2,0},{7,1},{4,2},{1,3},{6,4},{3,5},{0,6},{5,7},{10,8},{15,9},{12,... | collective-permute-start | bytes 663560 | tf_op jit(solution)/shard_map/ppermute | solution.py:55
  77.9 5.7 %collective-permute-start.14 = (bf16[128,768]{1,0:T(8,128)(2,1)S(1)}, bf16[128,768]{1,0:T(8,128)(2,1)S(1)}, u32[]{:S(2)}, u32[]{:S(2)}) collective-permute-start(bf16[128,768]{1,0:T(8,128)(2,1)S(1)} %get-tuple-element.40), channel_id=1, source_target_pairs={{0,1},{1,0},{2,3},{3,2},{4,5},{5,4},{6,7},{7,6},{8,9},{9,8},{10,11... | collective-permute-start | bytes 589832 | tf_op jit(solution)/shard_map/ppermute | solution.py:40
  77.9 7.8 %collective-permute-start.19 = (bf16[128,768]{1,0:T(8,128)(2,1)S(1)}, bf16[128,768]{1,0:T(8,128)(2,1)S(1)}, u32[]{:S(2)}, u32[]{:S(2)}) collective-permute-start(bf16[128,768]{1,0:T(8,128)(2,1)S(1)} %get-tuple-element.44), channel_id=1, source_target_pairs={{0,16},{8,24},{16,0},{24,8},{1,17},{9,25},{17,1},{25,9},{2,18},{10... | collective-permute-start | bytes 589832 | tf_op jit(solution)/shard_map/ppermute | solution.py:27
  80.4 14.4 %collective-permute-start.13 = (bf16[144,768]{1,0:T(8,128)(2,1)S(1)}, bf16[144,768]{1,0:T(8,128)(2,1)S(1)}, u32[]{:S(2)}, u32[]{:S(2)}) collective-permute-start(bf16[144,768]{1,0:T(8,128)(2,1)S(1)} %add_packets.16.refs_5_), channel_id=1, source_target_pairs={{0,16},{8,24},{16,0},{24,8},{1,17},{9,25},{17,1},{25,9},{2,18},{10... | collective-permute-start | bytes 663560 | tf_op jit(solution)/shard_map/ppermute | solution.py:27
  84.2 10.5 %collective-permute-start.18 = (bf16[144,768]{1,0:T(8,128)(2,1)S(1)}, bf16[144,768]{1,0:T(8,128)(2,1)S(1)}, u32[]{:S(2)}, u32[]{:S(2)}) collective-permute-start(bf16[144,768]{1,0:T(8,128)(2,1)S(1)} %add_packets.19), channel_id=1, source_target_pairs={{0,1},{1,0},{2,3},{3,2},{4,5},{5,4},{6,7},{7,6},{8,9},{9,8},{10,11... | collective-permute-start | bytes 663560 | tf_op jit(solution)/shard_map/ppermute | solution.py:40
  84.6 7.7 %collective-permute-start.11 = (bf16[128,768]{1,0:T(8,128)(2,1)S(1)}, bf16[128,768]{1,0:T(8,128)(2,1)S(1)}, u32[]{:S(2)}, u32[]{:S(2)}) collective-permute-start(bf16[128,768]{1,0:T(8,128)(2,1)S(1)} %add_packets.15.refs_4_), channel_id=1, source_target_pairs={{0,16},{8,24},{16,0},{24,8},{1,17},{9,25},{17,1},{25,9},{2,18},{10... | collective-permute-start | bytes 589832 | tf_op jit(solution)/shard_map/ppermute | solution.py:27
  86.3 8.4 %collective-permute-start.20 = (bf16[128,768]{1,0:T(8,128)(2,1)S(1)}, bf16[128,768]{1,0:T(8,128)(2,1)S(1)}, u32[]{:S(2)}, u32[]{:S(2)}) collective-permute-start(bf16[128,768]{1,0:T(8,128)(2,1)S(1)} %add_packets.20), channel_id=1, source_target_pairs={{0,7},{1,2},{2,1},{3,4},{4,3},{5,6},{6,5},{7,0},{8,15},{9,10},{10,... | collective-permute-start | bytes 589832 | tf_op jit(solution)/shard_map/ppermute | solution.py:45
  95.8 8.1 %collective-permute-start.26 = (bf16[272,768]{1,0:T(8,128)(2,1)S(1)}, bf16[272,768]{1,0:T(8,128)(2,1)S(1)}, u32[]{:S(2)}, u32[]{:S(2)}) collective-permute-start(bf16[272,768]{1,0:T(8,128)(2,1)S(1)} %renew.2.refs_8_.base), channel_id=1, source_target_pairs={{0,16},{8,24},{16,0},{24,8},{1,17},{9,25},{17,1},{25,9},{2,18},{10... | collective-permute-start | bytes 1253384 | tf_op jit(solution)/shard_map/ppermute | solution.py:27
  96.8 10.8 %collective-permute-start.21 = (bf16[272,768]{1,0:T(8,128)(2,1)S(1)}, bf16[272,768]{1,0:T(8,128)(2,1)S(1)}, u32[]{:S(2)}, u32[]{:S(2)}) collective-permute-start(bf16[272,768]{1,0:T(8,128)(2,1)S(1)} %renew.2.refs_8_.base), channel_id=1, source_target_pairs={{0,7},{1,2},{2,1},{3,4},{4,3},{5,6},{6,5},{7,0},{8,15},{9,10},{10,... | collective-permute-start | bytes 1253384 | tf_op jit(solution)/shard_map/ppermute | solution.py:45
  100.0 8.7 %collective-permute-start.30 = (bf16[272,768]{1,0:T(8,128)(2,1)S(1)}, bf16[272,768]{1,0:T(8,128)(2,1)S(1)}, u32[]{:S(2)}, u32[]{:S(2)}) collective-permute-start(bf16[272,768]{1,0:T(8,128)(2,1)S(1)} %renew.2.refs_8_.base), channel_id=1, source_target_pairs={{0,8},{8,0},{16,24},{24,16},{1,9},{9,1},{17,25},{25,17},{2,10},{10... | collective-permute-start | bytes 1253384 | tf_op jit(solution)/shard_map/ppermute | solution.py:27
  100.0 16.5 %collective-permute-start.25 = (bf16[272,768]{1,0:T(8,128)(2,1)S(1)}, bf16[272,768]{1,0:T(8,128)(2,1)S(1)}, u32[]{:S(2)}, u32[]{:S(2)}) collective-permute-start(bf16[272,768]{1,0:T(8,128)(2,1)S(1)} %renew.2.refs_8_.base), channel_id=1, source_target_pairs={{0,1},{1,0},{2,3},{3,2},{4,5},{5,4},{6,7},{7,6},{8,9},{9,8},{10,11... | collective-permute-start | bytes 1253384 | tf_op jit(solution)/shard_map/ppermute | solution.py:40
  103.9 21.5 %collective-permute-start.27 = (bf16[272,768]{1,0:T(8,128)(2,1)S(1)}, bf16[272,768]{1,0:T(8,128)(2,1)S(1)}, u32[]{:S(2)}, u32[]{:S(2)}) collective-permute-start(bf16[272,768]{1,0:T(8,128)(2,1)S(1)} %collective-permute-done.26.refs_9_), channel_id=1, source_target_pairs={{0,1},{1,0},{2,3},{3,2},{4,5},{5,4},{6,7},{7,6},{8,9},{9,8},{10,11... | collective-permute-start | bytes 1253384 | tf_op jit(solution)/shard_map/ppermute | solution.py:40
  107.6 17.9 %collective-permute-start.22 = (bf16[272,768]{1,0:T(8,128)(2,1)S(1)}, bf16[272,768]{1,0:T(8,128)(2,1)S(1)}, u32[]{:S(2)}, u32[]{:S(2)}) collective-permute-start(bf16[272,768]{1,0:T(8,128)(2,1)S(1)} %collective-permute-done.21.refs_0_), channel_id=1, source_target_pairs={{0,16},{8,24},{16,0},{24,8},{1,17},{9,25},{17,1},{25,9},{2,18},{10... | collective-permute-start | bytes 1253384 | tf_op jit(solution)/shard_map/ppermute | solution.py:27
  108.7 17.3 %collective-permute-start.31 = (bf16[272,768]{1,0:T(8,128)(2,1)S(1)}, bf16[272,768]{1,0:T(8,128)(2,1)S(1)}, u32[]{:S(2)}, u32[]{:S(2)}) collective-permute-start(bf16[272,768]{1,0:T(8,128)(2,1)S(1)} %collective-permute-done.26.refs_9_), channel_id=1, source_target_pairs={{0,8},{8,0},{16,24},{24,16},{1,9},{9,1},{17,25},{25,17},{2,10},{10... | collective-permute-start | bytes 1253384 | tf_op jit(solution)/shard_map/ppermute | solution.py:27
  108.7 17.3 %collective-permute-start.23 = (bf16[272,768]{1,0:T(8,128)(2,1)S(1)}, bf16[272,768]{1,0:T(8,128)(2,1)S(1)}, u32[]{:S(2)}, u32[]{:S(2)}) collective-permute-start(bf16[272,768]{1,0:T(8,128)(2,1)S(1)} %collective-permute-done.21.refs_0_), channel_id=1, source_target_pairs={{0,8},{8,0},{16,24},{24,16},{1,9},{9,1},{17,25},{25,17},{2,10},{10... | collective-permute-start | bytes 1253384 | tf_op jit(solution)/shard_map/ppermute | solution.py:27
  116.5 9.4 %collective-permute-start.28 = (bf16[272,768]{1,0:T(8,128)(2,1)S(1)}, bf16[272,768]{1,0:T(8,128)(2,1)S(1)}, u32[]{:S(2)}, u32[]{:S(2)}) collective-permute-start(bf16[272,768]{1,0:T(8,128)(2,1)S(1)} %collective-permute-done.25.refs_4_), channel_id=1, source_target_pairs={{0,8},{8,0},{16,24},{24,16},{1,9},{9,1},{17,25},{25,17},{2,10},{10... | collective-permute-start | bytes 1253384 | tf_op jit(solution)/shard_map/ppermute | solution.py:27
  125.5 2.3 %collective-permute-start.24 = (bf16[272,768]{1,0:T(8,128)(2,1)S(1)}, bf16[272,768]{1,0:T(8,128)(2,1)S(1)}, u32[]{:S(2)}, u32[]{:S(2)}) collective-permute-start(bf16[272,768]{1,0:T(8,128)(2,1)S(1)} %collective-permute-done.22.refs_1_), channel_id=1, source_target_pairs={{0,8},{8,0},{16,24},{24,16},{1,9},{9,1},{17,25},{25,17},{2,10},{10... | collective-permute-start | bytes 1253384 | tf_op jit(solution)/shard_map/ppermute | solution.py:27
  151.1 2.4 %collective-permute-start.39 = (bf16[544,768]{1,0:T(8,128)(2,1)S(1)}, bf16[544,768]{1,0:T(8,128)(2,1)S(1)}, u32[]{:S(2)}, u32[]{:S(2)}) collective-permute-start(bf16[544,768]{1,0:T(8,128)(2,1)S(1)} %get-tuple-element.53), channel_id=1, source_target_pairs={{0,8},{8,0},{16,24},{24,16},{1,9},{9,1},{17,25},{25,17},{2,10},{10... | collective-permute-start | bytes 2506760 | tf_op jit(solution)/shard_map/ppermute | solution.py:27
  151.3 3.6 %collective-permute-start.33 = (bf16[544,768]{1,0:T(8,128)(2,1)S(1)}, bf16[544,768]{1,0:T(8,128)(2,1)S(1)}, u32[]{:S(2)}, u32[]{:S(2)}) collective-permute-start(bf16[544,768]{1,0:T(8,128)(2,1)S(1)} %get-tuple-element.48), channel_id=1, source_target_pairs={{0,8},{8,0},{16,24},{24,16},{1,9},{9,1},{17,25},{25,17},{2,10},{10... | collective-permute-start | bytes 2506760 | tf_op jit(solution)/shard_map/ppermute | solution.py:27
  151.7 15.1 %collective-permute-start.32 = (bf16[544,768]{1,0:T(8,128)(2,1)S(1)}, bf16[544,768]{1,0:T(8,128)(2,1)S(1)}, u32[]{:S(2)}, u32[]{:S(2)}) collective-permute-start(bf16[544,768]{1,0:T(8,128)(2,1)S(1)} %get-tuple-element.46), channel_id=1, source_target_pairs={{0,8},{8,0},{16,24},{24,16},{1,9},{9,1},{17,25},{25,17},{2,10},{10... | collective-permute-start | bytes 2506760 | tf_op jit(solution)/shard_map/ppermute | solution.py:27
  154.2 9.3 %collective-permute-start.40 = (bf16[144,768]{1,0:T(8,128)(2,1)S(1)}, bf16[144,768]{1,0:T(8,128)(2,1)S(1)}, u32[]{:S(2)}, u32[]{:S(2)}) collective-permute-start(bf16[144,768]{1,0:T(8,128)(2,1)S(1)} %get-tuple-element.54), channel_id=1, source_target_pairs={{0,16},{8,24},{16,0},{24,8},{1,17},{9,25},{17,1},{25,9},{2,18},{10... | collective-permute-start | bytes 663560 | tf_op jit(solution)/shard_map/ppermute | solution.py:27
  155.6 7.8 %collective-permute-start.34 = (bf16[128,768]{1,0:T(8,128)(2,1)S(1)}, bf16[128,768]{1,0:T(8,128)(2,1)S(1)}, u32[]{:S(2)}, u32[]{:S(2)}) collective-permute-start(bf16[128,768]{1,0:T(8,128)(2,1)S(1)} %get-tuple-element.49), channel_id=1, source_target_pairs={{0,1},{1,0},{2,3},{3,2},{4,5},{5,4},{6,7},{7,6},{8,9},{9,8},{10,11... | collective-permute-start | bytes 589832 | tf_op jit(solution)/shard_map/ppermute | solution.py:40
  155.7 12.0 %collective-permute-start.36 = (bf16[144,768]{1,0:T(8,128)(2,1)S(1)}, bf16[144,768]{1,0:T(8,128)(2,1)S(1)}, u32[]{:S(2)}, u32[]{:S(2)}) collective-permute-start(bf16[144,768]{1,0:T(8,128)(2,1)S(1)} %get-tuple-element.50), channel_id=1, source_target_pairs={{0,1},{1,0},{2,3},{3,2},{4,5},{5,4},{6,7},{7,6},{8,9},{9,8},{10,11... | collective-permute-start | bytes 663560 | tf_op jit(solution)/shard_map/ppermute | solution.py:40
  164.1 7.3 %collective-permute-start.41 = (bf16[144,768]{1,0:T(8,128)(2,1)S(1)}, bf16[144,768]{1,0:T(8,128)(2,1)S(1)}, u32[]{:S(2)}, u32[]{:S(2)}) collective-permute-start(bf16[144,768]{1,0:T(8,128)(2,1)S(1)} %add_packets.25), channel_id=1, source_target_pairs={{2,0},{7,1},{4,2},{1,3},{6,4},{3,5},{0,6},{5,7},{10,8},{15,9},{12,... | collective-permute-start | bytes 663560 | tf_op jit(solution)/shard_map/ppermute | solution.py:55
  165.7 5.7 %collective-permute-start.38 = (bf16[128,768]{1,0:T(8,128)(2,1)S(1)}, bf16[128,768]{1,0:T(8,128)(2,1)S(1)}, u32[]{:S(2)}, u32[]{:S(2)}) collective-permute-start(bf16[128,768]{1,0:T(8,128)(2,1)S(1)} %get-tuple-element.51), channel_id=1, source_target_pairs={{0,1},{1,0},{2,3},{3,2},{4,5},{5,4},{6,7},{7,6},{8,9},{9,8},{10,11... | collective-permute-start | bytes 589832 | tf_op jit(solution)/shard_map/ppermute | solution.py:40
  165.7 8.2 %collective-permute-start.43 = (bf16[128,768]{1,0:T(8,128)(2,1)S(1)}, bf16[128,768]{1,0:T(8,128)(2,1)S(1)}, u32[]{:S(2)}, u32[]{:S(2)}) collective-permute-start(bf16[128,768]{1,0:T(8,128)(2,1)S(1)} %get-tuple-element.55), channel_id=1, source_target_pairs={{0,16},{8,24},{16,0},{24,8},{1,17},{9,25},{17,1},{25,9},{2,18},{10... | collective-permute-start | bytes 589832 | tf_op jit(solution)/shard_map/ppermute | solution.py:27
  168.3 14.6 %collective-permute-start.37 = (bf16[144,768]{1,0:T(8,128)(2,1)S(1)}, bf16[144,768]{1,0:T(8,128)(2,1)S(1)}, u32[]{:S(2)}, u32[]{:S(2)}) collective-permute-start(bf16[144,768]{1,0:T(8,128)(2,1)S(1)} %add_packets.23.refs_5_), channel_id=1, source_target_pairs={{0,16},{8,24},{16,0},{24,8},{1,17},{9,25},{17,1},{25,9},{2,18},{10... | collective-permute-start | bytes 663560 | tf_op jit(solution)/shard_map/ppermute | solution.py:27
  172.0 10.9 %collective-permute-start.42 = (bf16[144,768]{1,0:T(8,128)(2,1)S(1)}, bf16[144,768]{1,0:T(8,128)(2,1)S(1)}, u32[]{:S(2)}, u32[]{:S(2)}) collective-permute-start(bf16[144,768]{1,0:T(8,128)(2,1)S(1)} %add_packets.26), channel_id=1, source_target_pairs={{0,1},{1,0},{2,3},{3,2},{4,5},{5,4},{6,7},{7,6},{8,9},{9,8},{10,11... | collective-permute-start | bytes 663560 | tf_op jit(solution)/shard_map/ppermute | solution.py:40
  172.6 7.7 %collective-permute-start.35 = (bf16[128,768]{1,0:T(8,128)(2,1)S(1)}, bf16[128,768]{1,0:T(8,128)(2,1)S(1)}, u32[]{:S(2)}, u32[]{:S(2)}) collective-permute-start(bf16[128,768]{1,0:T(8,128)(2,1)S(1)} %add_packets.22.refs_4_), channel_id=1, source_target_pairs={{0,16},{8,24},{16,0},{24,8},{1,17},{9,25},{17,1},{25,9},{2,18},{10... | collective-permute-start | bytes 589832 | tf_op jit(solution)/shard_map/ppermute | solution.py:27
  174.5 8.4 %collective-permute-start.44 = (bf16[128,768]{1,0:T(8,128)(2,1)S(1)}, bf16[128,768]{1,0:T(8,128)(2,1)S(1)}, u32[]{:S(2)}, u32[]{:S(2)}) collective-permute-start(bf16[128,768]{1,0:T(8,128)(2,1)S(1)} %add_packets.27), channel_id=1, source_target_pairs={{0,7},{1,2},{2,1},{3,4},{4,3},{5,6},{6,5},{7,0},{8,15},{9,10},{10,... | collective-permute-start | bytes 589832 | tf_op jit(solution)/shard_map/ppermute | solution.py:45
  183.9 6.1 %collective-permute-start.46 = (bf16[144,768]{1,0:T(8,128)(2,1)S(1)}, bf16[144,768]{1,0:T(8,128)(2,1)S(1)}, u32[]{:S(2)}, u32[]{:S(2)}) collective-permute-start(bf16[144,768]{1,0:T(8,128)(2,1)S(1)} %get-tuple-element.57.refs_1_), channel_id=1, source_target_pairs={{0,16},{8,24},{16,0},{24,8},{1,17},{9,25},{17,1},{25,9},{2,18},{10... | collective-permute-start | bytes 663560 | tf_op jit(solution)/shard_map/ppermute | solution.py:27
  184.8 7.3 %collective-permute-start.45 = (bf16[128,768]{1,0:T(8,128)(2,1)S(1)}, bf16[128,768]{1,0:T(8,128)(2,1)S(1)}, u32[]{:S(2)}, u32[]{:S(2)}) collective-permute-start(bf16[128,768]{1,0:T(8,128)(2,1)S(1)} %get-tuple-element.56.refs_0_), channel_id=1, source_target_pairs={{0,16},{8,24},{16,0},{24,8},{1,17},{9,25},{17,1},{25,9},{2,18},{10... | collective-permute-start | bytes 589832 | tf_op jit(solution)/shard_map/ppermute | solution.py:27
  186.0 6.1 %collective-permute-start.48 = (bf16[144,768]{1,0:T(8,128)(2,1)S(1)}, bf16[144,768]{1,0:T(8,128)(2,1)S(1)}, u32[]{:S(2)}, u32[]{:S(2)}) collective-permute-start(bf16[144,768]{1,0:T(8,128)(2,1)S(1)} %get-tuple-element.57.refs_1_), channel_id=1, source_target_pairs={{0,8},{8,0},{16,24},{24,16},{1,9},{9,1},{17,25},{25,17},{2,10},{10... | collective-permute-start | bytes 663560 | tf_op jit(solution)/shard_map/ppermute | solution.py:27
  190.0 3.6 %collective-permute-start.50 = (bf16[144,768]{1,0:T(8,128)(2,1)S(1)}, bf16[144,768]{1,0:T(8,128)(2,1)S(1)}, u32[]{:S(2)}, u32[]{:S(2)}) collective-permute-start(bf16[144,768]{1,0:T(8,128)(2,1)S(1)} %collective-permute-done.46.refs_3_), channel_id=1, source_target_pairs={{0,8},{8,0},{16,24},{24,16},{1,9},{9,1},{17,25},{25,17},{2,10},{10... | collective-permute-start | bytes 663560 | tf_op jit(solution)/shard_map/ppermute | solution.py:27
  190.0 2.1 %collective-permute-start.47 = (bf16[128,768]{1,0:T(8,128)(2,1)S(1)}, bf16[128,768]{1,0:T(8,128)(2,1)S(1)}, u32[]{:S(2)}, u32[]{:S(2)}) collective-permute-start(bf16[128,768]{1,0:T(8,128)(2,1)S(1)} %get-tuple-element.56.refs_0_), channel_id=1, source_target_pairs={{0,8},{8,0},{16,24},{24,16},{1,9},{9,1},{17,25},{25,17},{2,10},{10... | collective-permute-start | bytes 589832 | tf_op jit(solution)/shard_map/ppermute | solution.py:27
  (5 other events, 41.6 us)
